TPU v7x, 128 devices: a whole 4x4x4 slice. The times are simulated.
128 devices in a mesh: head: 4 (over x), seq: 32 (over y, z, core).
Axes of the slice: x: 4, y: 4, z: 4, core: 2. Of those that a mesh axis runs over, the one named last changes fastest.
Arguments:
- queries: bfloat16 [16384, 8192], P('seq', 'head'), may hold values from -200 to 200
- keys: bfloat16 [16384, 8192], P('seq', 'head'), may hold values from -6 to 6
- values: bfloat16 [16384, 8192], P('seq', 'head'), may hold values from -6 to 6
- cotangent: bfloat16 [16384, 8192], P('seq', 'head'), may hold values from -6 to 6
- prefix_keys: bfloat16 [16384, 8192], P('seq', 'head'), may hold values from -1.5 to 1.5
- prefix_values: bfloat16 [16384, 8192], P('seq', 'head'), may hold values from -1.5 to 1.5
- gain: float32 [8192], P('head'), may hold values from 0.5 to 1.5
- lengths: int32 [32], P('seq'), may hold values from 64 to 512, as said below
Outputs:
- normed: bfloat16 [16384, 8192], P('seq', 'head')
- query_grad: bfloat16 [16384, 8192], P('seq', 'head')
- key_grad: bfloat16 [16384, 8192], P('seq', 'head')
- value_grad: bfloat16 [16384, 8192], P('seq', 'head')
- prefix_key_grad: bfloat16 [16384, 8192], P('seq', 'head')
- prefix_value_grad: bfloat16 [16384, 8192], P('seq', 'head')
Inputs may be any that keep to these rules, and one draw needn't show every extreme that they name: `lengths`: one length per response; some response has exactly 512 live slots and some exactly 64.
All inputs are finite; a program needn't handle non-finite values.
Results may differ from a plain program's by a relative error of at most 0.0058.
Values sent between devices are 32-bit elements; how exact they have to be, the bound alone decides.
No kernel may reach another device: no remote copies, remote signals or barrier semaphores. Data moves between devices by JAX's collectives and lax.ppermute only.
A program may use at most 128 MiB of HBM per device.

v0:
```python
import functools

import jax
import jax.numpy as jnp
from jax import lax
from jax.sharding import PartitionSpec as P

H = 64
HEAD_DIM = 128
BLOCK = 256


epsilon = 1e-06


def summed_prefix(partial_state):
    return lax.psum(partial_state, "seq")


def body(queries, keys, values, cotangent, prefix_keys, prefix_values, gain, lengths):
    tok_rows, tok_cols = queries.shape
    heads_here = tok_cols // HEAD_DIM
    block_count = tok_rows // BLOCK
    length = lengths[0]
    is_live = lax.iota(jnp.int32, tok_rows) < length
    live_mask = is_live.astype(jnp.bfloat16)[:, None]
    block_shape = (block_count, BLOCK, heads_here, HEAD_DIM)
    q_live = (queries * live_mask).reshape(block_shape)
    k_live = (keys * live_mask).reshape(block_shape)
    v_live = (values * live_mask).reshape(block_shape)
    causal = (lax.iota(jnp.int32, BLOCK)[:, None] >= lax.iota(jnp.int32, BLOCK)[None, :]).astype(
        jnp.float32
    )
    pre_keys = prefix_keys.reshape(-1, heads_here, HEAD_DIM)
    pre_values = prefix_values.reshape(-1, heads_here, HEAD_DIM)
    partial_state = jnp.einsum(
        "thd,the->hde", pre_keys, pre_values, preferred_element_type=jnp.float32
    )

    def intra_block(index):
        q_block = q_live[index]
        k_block = k_live[index]
        v_block = v_live[index]
        scores = jnp.einsum("bhd,shd->hbs", q_block, k_block, preferred_element_type=jnp.float32)
        scores = (scores * causal).astype(jnp.bfloat16)
        in_block = jnp.einsum("hbs,she->bhe", scores, v_block, preferred_element_type=jnp.float32)
        block_kv = jnp.einsum("bhd,bhe->hde", k_block, v_block, preferred_element_type=jnp.float32)
        return (in_block, scores, block_kv)

    def from_state_of(index, state_bf):
        return jnp.einsum(
            "bhd,hde->bhe", q_live[index], state_bf, preferred_element_type=jnp.float32
        )

    results = []
    score_list = []
    state_list = []
    prefix_state = summed_prefix(partial_state)

    def forward_block(index, state_now):
        state_bf = state_now.astype(jnp.bfloat16)
        in_block, scores, block_kv = intra_block(index)
        return (from_state_of(index, state_bf) + in_block, scores, state_bf, state_now + block_kv)

    state_now = prefix_state
    for index in range(block_count):
        step_fn = functools.partial(forward_block, index)
        packed = step_fn(state_now)
        results.append(packed[0])
        score_list.append(packed[1])
        state_list.append(packed[2])
        state_now = packed[3]
    attended = jnp.concatenate(results, axis=0).reshape(tok_rows, tok_cols)
    scaled_cot = gain * (cotangent * live_mask).astype(jnp.float32)
    square_sum, inner_sum = lax.psum(
        (jnp.sum(attended * attended, axis=1), jnp.sum(scaled_cot * attended, axis=1)), "head"
    )
    root_mean = jnp.sqrt(square_sum / (H * HEAD_DIM) + epsilon)[:, None]
    inner_sum = inner_sum[:, None]
    normed = (gain * attended / root_mean).astype(jnp.bfloat16)
    out_grad = scaled_cot / root_mean - attended * inner_sum / (H * HEAD_DIM * root_mean**3)
    out_grad = out_grad.astype(jnp.bfloat16).reshape(block_shape)

    def backward_block(index, grad_state):
        q_block = q_live[index]
        k_block = k_live[index]
        v_block = v_live[index]
        d_block = out_grad[index]
        scores = score_list[index]
        state_bf = state_list[index]
        grad_bf = grad_state.astype(jnp.bfloat16)
        pscore = jnp.einsum("bhe,she->hbs", d_block, v_block, preferred_element_type=jnp.float32)
        pscore = (pscore * causal).astype(jnp.bfloat16)
        grad_q = jnp.einsum(
            "bhe,hde->bhd", d_block, state_bf, preferred_element_type=jnp.float32
        ) + jnp.einsum("hbs,shd->bhd", pscore, k_block, preferred_element_type=jnp.float32)
        grad_k = jnp.einsum(
            "bhe,hde->bhd", v_block, grad_bf, preferred_element_type=jnp.float32
        ) + jnp.einsum("hbs,bhd->shd", pscore, q_block, preferred_element_type=jnp.float32)
        grad_v = jnp.einsum(
            "bhd,hde->bhe", k_block, grad_bf, preferred_element_type=jnp.float32
        ) + jnp.einsum("hbs,bhe->she", scores, d_block, preferred_element_type=jnp.float32)
        grad_next = grad_state + jnp.einsum(
            "bhd,bhe->hde", q_block, d_block, preferred_element_type=jnp.float32
        )
        return (
            grad_q.astype(jnp.bfloat16),
            grad_k.astype(jnp.bfloat16),
            grad_v.astype(jnp.bfloat16),
            grad_next,
        )

    grad_state = jnp.zeros((heads_here, HEAD_DIM, HEAD_DIM), jnp.float32)
    query_parts = []
    key_parts = []
    value_parts = []
    for index in reversed(range(block_count)):
        step_fn = functools.partial(backward_block, index)
        packed = step_fn(grad_state)
        query_parts.insert(0, packed[0])
        key_parts.insert(0, packed[1])
        value_parts.insert(0, packed[2])
        grad_state = packed[3]
    total_grad = lax.psum(grad_state, "seq")
    wide_keys = pre_keys.astype(jnp.float32)
    wide_values = pre_values.astype(jnp.float32)
    prefix_key_grad = jnp.einsum(
        "the,hde->thd", wide_values, total_grad, precision=lax.Precision.HIGHEST
    )
    prefix_value_grad = jnp.einsum(
        "thd,hde->the", wide_keys, total_grad, precision=lax.Precision.HIGHEST
    )
    query_grad = jnp.concatenate(query_parts, axis=0).reshape(tok_rows, tok_cols)
    key_grad = jnp.concatenate(key_parts, axis=0).reshape(tok_rows, tok_cols)
    value_grad = jnp.concatenate(value_parts, axis=0).reshape(tok_rows, tok_cols)
    return (
        normed,
        query_grad,
        key_grad,
        value_grad,
        prefix_key_grad.astype(jnp.bfloat16).reshape(prefix_keys.shape),
        prefix_value_grad.astype(jnp.bfloat16).reshape(prefix_values.shape),
    )


def solution(mesh):
    return jax.shard_map(
        body,
        mesh=mesh,
        in_specs=(
            P("seq", "head"),
            P("seq", "head"),
            P("seq", "head"),
            P("seq", "head"),
            P("seq", "head"),
            P("seq", "head"),
            P("head"),
            P("seq"),
        ),
        out_specs=(
            P("seq", "head"),
            P("seq", "head"),
            P("seq", "head"),
            P("seq", "head"),
            P("seq", "head"),
            P("seq", "head"),
        ),
        check_vma=False,
    )
```

profile of v0, /device:TPU:1, one launch (start us, length us, event | category | flops | bytes accessed | tf_op | source)
XLA Modules:
  0.0 292.5 jit_solution(10290730926463739367)
XLA Ops:
  7.2 1.5 copy-done
  8.8 3.4 %fusion.8 = f32[16,128,128]{2,1,0:T(8,128)} fusion(bf16[512,2048]{1,0:T(8,128)(2,1)} %param.13, bf16[512,2048]{1,0:T(8,128)(2,1)S(1)} %copy-done), kind=kOutput, calls=%fused_computation.18 | convolution fusion | flops 268435456 | bytes 5242880 | tf_op jit(solution)/shard_map/thd,the->hde/dot_general | solution.py:36
  13.0 3.9 %copy.49 = bf16[512,2048]{0,1:T(8,128)(2,1)} copy(bf16[512,2048]{1,0:T(8,128)(2,1)} %param.8) | data formatting | bytes 4194304 | tf_op args[0]
  16.9 3.9 %copy.53 = bf16[512,2048]{0,1:T(8,128)(2,1)} copy(bf16[512,2048]{1,0:T(8,128)(2,1)} %param.9) | data formatting | bytes 4194304 | tf_op args[1]
  20.8 3.9 %copy.52 = bf16[512,2048]{0,1:T(8,128)(2,1)} copy(bf16[512,2048]{1,0:T(8,128)(2,1)} %param.10) | data formatting | bytes 4194304 | tf_op args[2]
  24.7 3.3 %broadcast_multiply_fusion = (bf16[512,2048]{0,1:T(8,128)(2,1)S(1)}, bf16[512,2048]{0,1:T(8,128)(2,1)S(1)}, bf16[512,2048]{0,1:T(8,128)(2,1)S(1)}) fusion(bf16[512,2048]{0,1:T(8,128)(2,1)} %copy.53, bf16[512]{0:T(512)(128)(2,1)S(1)} %fusion.38, bf16[512,2048]{0,1:T(8,128)(2,1)} %copy.52, bf16[512,2048]{0,1:T(8,128)(2,1)} %copy.49), kind=kLoop, calls=%fused_computation.49 | loop fusion | flops 3145728 | bytes 12583936 | tf_op jit(solution)/shard_map/mul | solution.py:29
  28.2 1.3 fusion.42
  29.4 0.8 multiply_convert_fusion.3
  30.8 2.2 fusion.45
  33.0 2.1 multiply_convert_fusion.2
  35.1 3.9 %copy.61 = bf16[512,2048]{0,1:T(8,128)(2,1)} copy(bf16[512,2048]{1,0:T(8,128)(2,1)} %param.11) | data formatting | bytes 4194304 | tf_op args[3]
  39.0 4.1 %fusion.46 = f32[16,128,256]{2,1,0:T(8,128)} fusion(bf16[256,16,128]{0,2,1:T(8,128)(2,1)} %bitcast.148, bf16[16,256,256]{2,1,0:T(8,128)(2,1)} %multiply_convert_fusion.2), kind=kOutput, calls=%fused_computation.72 | convolution fusion | flops 268435456 | bytes 5242880 | tf_op jit(solution)/shard_map/hbs,she->bhe/dot_general | solution.py:46
  43.0 77.5 %all-reduce.4.cloned.1.call-done = f32[16,128,128]{2,1,0:T(8,128)} async-done(((f32[16,128,128]{2,1,0:T(8,128)}), f32[16,128,128]{2,1,0:T(8,128)}) %all-reduce.4.cloned.1.call-update) | async-done | bytes 1048592 | tf_op jit(solution)/shard_map/psum | solution.py:17
  120.5 2.1 fusion.29
  126.5 1.1 copy-done.15
  127.7 0.7 fusion.2
  128.5 8.7 %all-reduce = (f32[512]{0:T(512)S(1)}, f32[512]{0:T(512)S(1)}) all-reduce(f32[512]{0:T(512)S(1)} %get-tuple-element.22, f32[512]{0:T(512)S(1)} %fusion.2), channel_id=1, replica_groups=mesh['head'=4,'seq'=32] {'head'}, use_global_device_ids=true, to_apply=%region_2.0 | all-reduce | flops 1024 | bytes 8192 | tf_op jit(solution)/shard_map/psum | solution.py:75
  137.3 4.5 %fusion.5 = (bf16[512,2048]{0,1:T(8,128)(2,1)S(1)}, bf16[512,2048]{0,1:T(8,128)(2,1)}) fusion(f32[512,16,128]{0,2,1:T(8,128)} %copy-done.1, f32[512]{0:T(512)S(1)} %get-tuple-element.32, f32[512]{0:T(512)S(1)} %get-tuple-element.19, f32[512]{0:T(512)S(1)} %get-tuple-element.33, f32[2048]{0:T(1024)S(1)} %copy-done.35, bf16[512,2048]{0,1:T(8,128)(2,1)} %copy.61, ...), kind=kLoop, calls=%fused_computation.9 | loop fusion | flops 11534336 | bytes 10501120 | tf_op jit(solution)/shard_map/convert_element_type | solution.py:82
  141.9 2.2 copy-done.18
  144.5 0.8 copy-done.11
  145.8 0.8 copy-done.22
  146.6 0.8 multiply_convert_fusion
  147.4 1.8 fusion.51
  149.1 2.1 fusion.48
  151.3 1.8 fusion.52
  153.1 0.8 multiply_convert_fusion.1
  154.3 1.8 fusion.50
  156.1 2.1 fusion.47
  158.2 1.4 fusion.28
  159.6 1.4 convolution_add_fusion
  161.1 3.4 %fusion.27 = bf16[256,16,128]{0,2,1:T(8,128)(2,1)} fusion(f32[16,128,256]{2,1,0:T(8,128)} %fusion.52, bf16[256,16,128]{0,2,1:T(8,128)(2,1)S(1)} %bitcast.124, f32[16,128,128]{2,1,0:T(8,128)} %copy-done.19), kind=kOutput, calls=%fused_computation.44 | convolution fusion | flops 135528448 | bytes 5242880 | tf_op jit(solution)/shard_map/bhd,hde->bhe/dot_general | solution.py:100
  164.5 3.6 %fusion.26 = bf16[256,16,128]{0,2,1:T(8,128)(2,1)} fusion(f32[16,128,256]{2,1,0:T(8,128)} %fusion.51, bf16[256,16,128]{0,2,1:T(8,128)(2,1)} %bitcast.149), kind=kOutput, calls=%fused_computation.43 | convolution fusion | flops 135266304 | bytes 4194304 | tf_op jit(solution)/shard_map/bhe,hde->bhd/dot_general | solution.py:97
  168.5 0.8 copy-done.32
  169.6 1.5 pad_maximum_fusion.3
  171.1 0.8 copy-done.24
  171.9 0.8 copy-done.27
  173.1 1.5 pad_maximum_fusion.1
  174.6 3.9 %copy.82 = bf16[512,2048]{1,0:T(8,128)(2,1)} copy(bf16[512,2048]{0,1:T(8,128)(2,1)} %bitcast.151) | data formatting | bytes 4194304
  178.6 4.0 %copy.80 = bf16[512,2048]{1,0:T(8,128)(2,1)} copy(bf16[512,2048]{0,1:T(8,128)(2,1)} %bitcast.152) | data formatting | bytes 4194304
  182.6 2.4 fusion.25
  185.0 1.5 pad_maximum_fusion.2
  186.6 3.9 %copy.81 = bf16[512,2048]{1,0:T(8,128)(2,1)} copy(bf16[512,2048]{0,1:T(8,128)(2,1)} %bitcast.153) | data formatting | bytes 4194304
  190.5 3.9 %copy.79 = bf16[512,2048]{1,0:T(8,128)(2,1)} copy(bf16[512,2048]{0,1:T(8,128)(2,1)} %get-tuple-element.21) | data formatting | bytes 4194304
  194.4 74.1 %all-reduce.6.cloned.1.call-done = f32[16,128,128]{2,1,0:T(8,128)} async-done(((f32[16,128,128]{2,1,0:T(8,128)}), f32[16,128,128]{2,1,0:T(8,128)}) %all-reduce.6.cloned.1.call-update) | async-done | bytes 1048592 | tf_op jit(solution)/shard_map/psum | solution.py:124
  268.5 4.4 %fusion.13 = bf16[16,128,512]{2,1,0:T(8,128)(2,1)} fusion(f32[16,128,128]{2,1,0:T(8,128)} %all-reduce.6.cloned.1.call-done, bf16[512,2048]{1,0:T(8,128)(2,1)S(1)} %copy-done), kind=kOutput, calls=%fused_computation.34 | convolution fusion | flops 1611661312 | bytes 5242880 | tf_op jit(solution)/shard_map/thd,hde->the/dot_general | solution.py:130
  273.0 4.0 %copy.84 = bf16[512,2048]{1,0:T(8,128)(2,1)} copy(bf16[512,2048]{0,1:T(8,128)(2,1)} %bitcast.155) | data formatting | bytes 4194304
  277.0 4.8 %fusion.16 = bf16[16,128,512]{2,1,0:T(8,128)(2,1)} fusion(f32[16,128,128]{2,1,0:T(8,128)S(1)} %copy-done.31, bf16[512,2048]{1,0:T(8,128)(2,1)} %param.13), kind=kOutput, calls=%fused_computation.35 | convolution fusion | flops 1611661312 | bytes 5242880 | tf_op jit(solution)/shard_map/the,hde->thd/dot_general | solution.py:127
  281.7 3.9 %copy.83 = bf16[512,2048]{1,0:T(8,128)(2,1)} copy(bf16[512,2048]{0,1:T(8,128)(2,1)} %bitcast.154) | data formatting | bytes 4194304
  (80 shorter events, 7.6 us)
Async XLA Ops:
  7.2 1.6 copy-start
  7.2 113.3 %all-reduce.4.cloned.1.call-start = ((), (), s32[]{:S(2)}) async-start(), calls=%async_computation | async-start | bytes 2097152 | tf_op jit(solution)/shard_map/psum | solution.py:17
  12.2 256.3 %all-reduce.6.cloned.1.call-start = ((), (), s32[]{:S(2)}) async-start(), calls=%async_computation.1 | async-start | bytes 2097152 | tf_op jit(solution)/shard_map/psum | solution.py:124
  28.1 4.8 %copy-start.20 = (bf16[256,2048]{0,1:T(8,128)(2,1)}, bf16[256,2048]{0,1:T(8,128)(2,1)S(1)}, u32[]{:S(2)}) copy-start(bf16[256,2048]{0,1:T(8,128)(2,1)S(1)} %get-tuple-element.31) | copy-start | bytes 3145732
  29.4 1.0 copy-start.12
  29.4 1.4 copy-start.2
  29.4 3.5 %copy-start.9 = (bf16[256,2048]{0,1:T(8,128)(2,1)}, bf16[256,2048]{0,1:T(8,128)(2,1)S(1)}, u32[]{:S(2)}) copy-start(bf16[256,2048]{0,1:T(8,128)(2,1)S(1)} %get-tuple-element.27) | copy-start | bytes 3145732
  30.4 2.5 copy-start.16
  120.5 2.1 copy-start.10
  120.5 2.5 copy-start.28
  123.1 0.8 copy-start.29
  123.1 1.4 copy-start.13
  123.1 1.7 copy-start.23
  123.1 2.4 copy-start.25
  126.0 1.7 copy-start.15
  126.0 1.7 copy-start.35
  126.5 2.0 copy-start.1
  141.8 2.3 copy-start.18
  141.9 3.9 %copy-start.7 = (bf16[256,2048]{0,1:T(8,128)(2,1)}, bf16[256,2048]{0,1:T(8,128)(2,1)S(1)}, u32[]{:S(2)}) copy-start(bf16[256,2048]{0,1:T(8,128)(2,1)S(1)} %get-tuple-element.25) | copy-start | bytes 3145732
  141.9 17.7 %copy-start.5 = (bf16[256,2048]{0,1:T(8,128)(2,1)}, bf16[256,2048]{0,1:T(8,128)(2,1)S(1)}, u32[]{:S(2)}) copy-start(bf16[256,2048]{0,1:T(8,128)(2,1)S(1)} %get-tuple-element.24) | copy-start | bytes 3145732
  144.1 1.2 copy-start.11
  145.3 1.2 copy-start.22
  146.6 13.1 %copy-start.19 = (f32[16,128,128]{2,1,0:T(8,128)}, f32[16,128,128]{2,1,0:T(8,128)S(1)}, u32[]{:S(2)}) copy-start(f32[16,128,128]{2,1,0:T(8,128)S(1)} %fusion.49) | copy-start | bytes 3145732
  147.3 1.8 copy-start.21
  149.1 2.1 copy-start.17
  151.3 1.8 copy-start.3
  153.1 1.2 copy-start.14
  164.5 3.6 %copy-start.8 = (bf16[256,2048]{0,1:T(8,128)(2,1)S(1)}, bf16[256,2048]{0,1:T(8,128)(2,1)}, u32[]{:S(2)}) copy-start(bf16[256,2048]{0,1:T(8,128)(2,1)} %copy-done.7) | copy-start | bytes 3145732
  164.5 3.6 %copy-start.26 = (f32[16,128,256]{2,1,0:T(8,128)S(1)}, f32[16,128,256]{2,1,0:T(8,128)}, u32[]{:S(2)}) copy-start(f32[16,128,256]{2,1,0:T(8,128)} %fusion.48) | copy-start | bytes 6291460
  164.5 3.6 %copy-start.30 = (bf16[16,128,128]{2,1,0:T(8,128)(2,1)S(1)}, bf16[16,128,128]{2,1,0:T(8,128)(2,1)}, u32[]{:S(2)}) copy-start(bf16[16,128,128]{2,1,0:T(8,128)(2,1)} %copy-done.29) | copy-start | bytes 1572868
  168.1 1.2 copy-start.32
  168.1 1.5 copy-start.34
  169.6 1.5 copy-start.6
  169.6 2.3 copy-start.24
  169.6 3.1 %copy-start.27 = (f32[16,128,256]{2,1,0:T(8,128)S(1)}, f32[16,128,256]{2,1,0:T(8,128)}, u32[]{:S(2)}) copy-start(f32[16,128,256]{2,1,0:T(8,128)} %fusion.47) | copy-start | bytes 6291460
  178.6 4.0 %copy-start.4 = (bf16[256,2048]{0,1:T(8,128)(2,1)S(1)}, bf16[256,2048]{0,1:T(8,128)(2,1)}, u32[]{:S(2)}) copy-start(bf16[256,2048]{0,1:T(8,128)(2,1)} %copy-done.2) | copy-start | bytes 3145732
  182.6 2.5 copy-start.33
  272.9 4.0 %copy-start.31 = (f32[16,128,128]{2,1,0:T(8,128)S(1)}, f32[16,128,128]{2,1,0:T(8,128)}, u32[]{:S(2)}) copy-start(f32[16,128,128]{2,1,0:T(8,128)} %all-reduce.6.cloned.1.call-done) | copy-start | bytes 3145732
Sparse Core Ops, SparseCore 0:
  12.3 108.1 all-reduce.3
  164.6 103.9 all-reduce.5
where the time goes:
time: 294 us; the launch traced here: 292 us
  waiting for transfers between devices  152 us (52%)
  local copies, waits for them, and re-layouts  53.5 us (18%)
  matrix products  50 us (17%)
  between operations  15 us (5%)
  other arithmetic  13.6 us (5%)
  blocking collectives  8.75 us (3%)
    psum x1, waiting for transfers between devices, summed_prefix(): return lax.psum(partial_state, 'seq')  77.5 us
    psum x1, waiting for transfers between devices, body(): total_grad = lax.psum(grad_state, 'seq')  74.1 us
    unnamed x82, local copies, waits for them, and re-layouts  52 us
    psum x1, blocking collectives, body(): lax.psum((jnp.sum(attended * attended, axis=1), jnp.sum(scaled_cot * atte...  8.75 us
    dot_general x2, matrix products, intra_block(): jnp.einsum('hbs,she->bhe', scores, v_block, preferred_element_type=jnp.fl...  6.21 us
    dot_general x2, matrix products, backward_block(): jnp.einsum('bhe,hde->bhd', v_block, grad_bf, preferred_element_type=jnp.f...  6.01 us
  transfers between devices with their start and end apart: 2, of which 2 were waited for; matrix products, arithmetic and copies ran while one was open for 19% of the time, Pallas kernels for 0%

commit v1 on v0

--- a/solution.py
+++ b/solution.py
@@ -13,8 +13,27 @@
 epsilon = 1e-06
 
 
-def summed_prefix(partial_state):
-    return lax.psum(partial_state, "seq")
+def sum_over_seq(part):
+    seq_size = lax.axis_size("seq")
+    chips = seq_size // 2
+    half = part.shape[0] // 2
+    core = lax.axis_index("seq") % 2
+    swap = [(i, i ^ 1) for i in range(seq_size)]
+    groups = [list(range(c, seq_size, 2)) for c in range(2)]
+    mine = lax.dynamic_slice_in_dim(part, core * half, half, 0)
+    theirs = lax.dynamic_slice_in_dim(part, (1 - core) * half, half, 0)
+    paired = mine + lax.ppermute(theirs, "seq", swap)
+    pieces = lax.all_to_all(
+        paired.reshape(chips, -1, HEAD_DIM), "seq", 0, 0, axis_index_groups=groups, tiled=True
+    )
+    piece = jnp.sum(pieces, axis=0)
+    gathered = lax.all_to_all(
+        jnp.broadcast_to(piece[None], pieces.shape), "seq", 0, 0, axis_index_groups=groups, tiled=True
+    ).reshape(mine.shape)
+    other = lax.ppermute(gathered, "seq", swap)
+    first = jnp.where(core == 0, gathered, other)
+    second = jnp.where(core == 0, other, gathered)
+    return jnp.concatenate([first, second], axis=0)
 
 
 def body(queries, keys, values, cotangent, prefix_keys, prefix_values, gain, lengths):
@@ -55,7 +74,7 @@
     results = []
     score_list = []
     state_list = []
-    prefix_state = summed_prefix(partial_state)
+    prefix_state = sum_over_seq(partial_state)
 
     def forward_block(index, state_now):
         state_bf = state_now.astype(jnp.bfloat16)
@@ -121,7 +140,7 @@
         key_parts.insert(0, packed[1])
         value_parts.insert(0, packed[2])
         grad_state = packed[3]
-    total_grad = lax.psum(grad_state, "seq")
+    total_grad = sum_over_seq(grad_state)
     wide_keys = pre_keys.astype(jnp.float32)
     wide_values = pre_values.astype(jnp.float32)
     prefix_key_grad = jnp.einsum(

time: 294 us -> 195 us (0.66)
  waiting for transfers between devices: 152 us -> 20.7 us
  starting transfers between devices: 0.08 us -> 30.9 us
  between operations: 15 us -> 1.7 us
  other arithmetic: 13.6 us -> 24.7 us
  local copies, waits for them, and re-layouts: 53.5 us -> 63.4 us
  matrix products: 50 us -> 42.7 us
    psum x2 -> x0, waiting for transfers between devices: 152 us -> none  [the longest x1 77.5 us: summed_prefix(): return lax.psum(partial_state, 'seq')]
    all_to_all x0 -> x4, starting transfers between devices: none -> 20.8 us  [the longest x2 12.2 us: sum_over_seq(): lax.all_to_all(paired.reshape(chips, -1, HEAD_DIM), 'seq', 0, 0, axis_ind...]
    all_to_all x0 -> x4, waiting for transfers between devices: none -> 20.7 us  [the longest x2 12.5 us: sum_over_seq(): lax.all_to_all(paired.reshape(chips, -1, HEAD_DIM), 'seq', 0, 0, axis_ind...]
    ppermute x0 -> x4, starting transfers between devices: none -> 10 us  [the longest x2 6.49 us: sum_over_seq(): other = lax.ppermute(gathered, 'seq', swap)]
    dot_general x2, matrix products: 0.89 us -> 5.35 us  [backward_block(): jnp.einsum('bhe,hde->bhd', d_block, state_bf, preferred_element_type=jnp....]
    reshape x0 -> x2, local copies, waits for them, and re-layouts: none -> 4.05 us  [sum_over_seq(): gathered = lax.all_to_all(jnp.broadcast_to(piece[None], pieces.shape), 's...]
    unnamed x82 -> x80, local copies, waits for them, and re-layouts: 52 us -> 51.9 us
  transfers between devices with their start and end apart: 2 -> 8, of which waited for: 2 -> 4; matrix products, arithmetic and copies ran while one was open for 19% -> 38% of each run, Pallas kernels for 0% -> 0%
where the time goes in v1:
time: 195 us; the launch traced here: 193 us
  local copies, waits for them, and re-layouts  63.4 us (33%)
  matrix products  42.7 us (22%)
  starting transfers between devices  30.9 us (16%)
  other arithmetic  24.7 us (13%)
  waiting for transfers between devices  20.7 us (11%)
  blocking collectives  8.62 us (4%)
    unnamed x80, local copies, waits for them, and re-layouts  51.9 us
    all_to_all x2, waiting for transfers between devices, sum_over_seq(): lax.all_to_all(paired.reshape(chips, -1, HEAD_DIM), 'seq', 0, 0, axis_ind...  12.5 us
    all_to_all x2, starting transfers between devices, sum_over_seq(): lax.all_to_all(paired.reshape(chips, -1, HEAD_DIM), 'seq', 0, 0, axis_ind...  12.2 us
    all_to_all x2, starting transfers between devices, sum_over_seq(): lax.all_to_all(jnp.broadcast_to(piece[None], pieces.shape), 'seq', 0, 0,...  8.68 us
    psum x1, blocking collectives, body(): lax.psum((jnp.sum(attended * attended, axis=1), jnp.sum(scaled_cot * atte...  8.62 us
    all_to_all x2, waiting for transfers between devices, sum_over_seq(): lax.all_to_all(jnp.broadcast_to(piece[None], pieces.shape), 'seq', 0, 0,...  8.23 us
    ppermute x2, starting transfers between devices, sum_over_seq(): other = lax.ppermute(gathered, 'seq', swap)  6.49 us
    dot_general x2, matrix products, intra_block(): jnp.einsum('bhd,shd->hbs', q_block, k_block, preferred_element_type=jnp.f...  5.67 us
  transfers between devices with their start and end apart: 8, of which 4 were waited for; matrix products, arithmetic and copies ran while one was open for 38% of the time, Pallas kernels for 0%

profile of v1, /device:TPU:1, one launch (start us, length us, event | category | flops | bytes accessed | tf_op | source)
XLA Modules:
  0.0 192.7 jit_solution(15137900197391011062)
XLA Ops:
  0.7 1.6 copy-done
  2.2 2.5 %fusion.8 = f32[16,128,128]{2,1,0:T(8,128)S(1)} fusion(bf16[512,2048]{1,0:T(8,128)(2,1)} %param.13, bf16[512,2048]{1,0:T(8,128)(2,1)S(1)} %copy-done), kind=kOutput, calls=%fused_computation.18 | convolution fusion | flops 268435456 | bytes 5242880 | tf_op jit(solution)/shard_map/thd,the->hde/dot_general | solution.py:55
  7.6 3.9 %copy.53 = bf16[512,2048]{0,1:T(8,128)(2,1)} copy(bf16[512,2048]{1,0:T(8,128)(2,1)} %param.8) | data formatting | bytes 4194304 | tf_op args[0]
  11.6 3.9 %copy.56 = bf16[512,2048]{0,1:T(8,128)(2,1)} copy(bf16[512,2048]{1,0:T(8,128)(2,1)} %param.9) | data formatting | bytes 4194304 | tf_op args[1]
  15.5 3.9 %copy.55 = bf16[512,2048]{0,1:T(8,128)(2,1)} copy(bf16[512,2048]{1,0:T(8,128)(2,1)} %param.10) | data formatting | bytes 4194304 | tf_op args[2]
  19.4 4.6 %broadcast_multiply_fusion = (bf16[512,2048]{0,1:T(8,128)(2,1)}, bf16[512,2048]{0,1:T(8,128)(2,1)S(1)}, bf16[512,2048]{0,1:T(8,128)(2,1)S(1)}) fusion(bf16[512,2048]{0,1:T(8,128)(2,1)} %copy.56, bf16[512]{0:T(512)(128)(2,1)S(1)} %fusion.39, bf16[512,2048]{0,1:T(8,128)(2,1)} %copy.55, bf16[512,2048]{0,1:T(8,128)(2,1)} %copy.53), kind=kLoop, calls=%fused_computation.51 | loop fusion | flops 3145728 | bytes 12583936 | tf_op jit(solution)/shard_map/mul | solution.py:48
  24.0 2.1 %fusion.47 = (bf16[256,2048]{0,1:T(8,128)(2,1)}, bf16[256,2048]{0,1:T(8,128)(2,1)}, bf16[256,2048]{0,1:T(8,128)(2,1)}, bf16[256,2048]{0,1:T(8,128)(2,1)}) fusion(bf16[512,2048]{0,1:T(8,128)(2,1)S(1)} %get-tuple-element.40, bf16[512,2048]{0,1:T(8,128)(2,1)S(1)} %get-tuple-element.39), kind=kLoop, calls=%fused_computation.81 | loop fusion | bytes 8388608 | tf_op jit(solution)/shard_map/slice | solution.py:71
  26.1 1.9 dynamic-slice_add_fusion.1
  28.0 7.9 %all-to-all-start = ((f32[16,64,128]{2,1,0:T(8,128)}), f32[16,64,128]{2,1,0:T(8,128)}, u32[]{:S(2)}, u32[]{:S(2)}) async-start(f32[16,64,128]{2,1,0:T(8,128)} %bitcast), calls=%async_computation | async-start | bytes 1048576 | tf_op jit(solution)/shard_map/all_to_all | solution.py:26
  35.9 2.7 %fusion.49 = (bf16[256,2048]{0,1:T(8,128)(2,1)S(1)}, bf16[256,2048]{0,1:T(8,128)(2,1)}) fusion(bf16[512,2048]{0,1:T(8,128)(2,1)} %get-tuple-element.38), kind=kLoop, calls=%fused_computation.83 | loop fusion | bytes 4194304 | tf_op jit(solution)/shard_map/slice | solution.py:61
  38.6 7.5 %all-to-all-done = f32[16,64,128]{2,1,0:T(8,128)} async-done(((f32[16,64,128]{2,1,0:T(8,128)}), f32[16,64,128]{2,1,0:T(8,128)}, u32[]{:S(2)}, u32[]{:S(2)}) %all-to-all-start) | async-done | bytes 524320 | tf_op jit(solution)/shard_map/all_to_all | solution.py:26
  48.0 4.4 %all-to-all-start.1 = ((f32[16,64,128]{2,1,0:T(8,128)}), f32[16,64,128]{2,1,0:T(8,128)}, u32[]{:S(2)}, u32[]{:S(2)}) async-start(f32[16,64,128]{2,1,0:T(8,128)} %broadcast_in_dim.6), calls=%async_computation.1 | async-start | bytes 1048576 | tf_op jit(solution)/shard_map/all_to_all | solution.py:30
  52.5 2.1 %multiply_convert_fusion.3 = bf16[16,256,256]{2,1,0:T(8,128)(2,1)S(1)} fusion(bf16[256,16,128]{0,2,1:T(8,128)(2,1)} %bitcast.143, bf16[256,16,128]{0,2,1:T(8,128)(2,1)S(1)} %bitcast.123, f32[256,256]{1,0:T(8,128)S(1)} %fusion.35), kind=kOutput, calls=%fused_computation.15 | convolution fusion | flops 270532608 | bytes 4456448 | tf_op jit(solution)/shard_map/bhd,shd->hbs/dot_general | solution.py:63
  55.9 2.1 %fusion.50 = f32[16,128,256]{2,1,0:T(8,128)} fusion(bf16[256,16,128]{0,2,1:T(8,128)(2,1)S(1)} %bitcast.127, bf16[16,256,256]{2,1,0:T(8,128)(2,1)S(1)} %multiply_convert_fusion.3), kind=kOutput, calls=%fused_computation.84 | convolution fusion | flops 268435456 | bytes 5242880 | tf_op jit(solution)/shard_map/hbs,she->bhe/dot_general | solution.py:65
  58.0 3.7 %all-to-all-done.1 = f32[16,64,128]{2,1,0:T(8,128)} async-done(((f32[16,64,128]{2,1,0:T(8,128)}), f32[16,64,128]{2,1,0:T(8,128)}, u32[]{:S(2)}, u32[]{:S(2)}) %all-to-all-start.1) | async-done | bytes 524320 | tf_op jit(solution)/shard_map/all_to_all | solution.py:30
  61.7 2.0 %copy.51 = f32[8,128,128]{1,2,0:T(8,128)} copy(f32[8,128,128]{2,1,0:T(8,128)} %bitcast.1) | data formatting | bytes 1048576 | tf_op jit(solution)/shard_map/reshape | solution.py:32
  63.8 3.2 %collective-permute-start.1 = (f32[8,128,128]{1,2,0:T(8,128)}, f32[8,128,128]{1,2,0:T(8,128)}, u32[]{:S(2)}, u32[]{:S(2)}) collective-permute-start(f32[8,128,128]{1,2,0:T(8,128)} %copy.51), channel_id=1, source_target_pairs={{0,1},{1,0},{2,3},{3,2},{4,5},{5,4},{6,7},{7,6},{8,9},{9,8},{10,11... | collective-permute-start | bytes 1572872 | tf_op jit(solution)/shard_map/ppermute | solution.py:33
  67.0 3.6 %multiply_convert_fusion.2 = bf16[16,256,256]{2,1,0:T(8,128)(2,1)} fusion(bf16[256,16,128]{0,2,1:T(8,128)(2,1)} %bitcast.139, bf16[256,16,128]{0,2,1:T(8,128)(2,1)} %bitcast.147, f32[256,256]{1,0:T(8,128)S(1)} %fusion.35), kind=kOutput, calls=%fused_computation.14 | convolution fusion | flops 270532608 | bytes 4456448 | tf_op jit(solution)/shard_map/bhd,shd->hbs/dot_general | solution.py:63
  70.6 3.9 %copy.64 = bf16[512,2048]{0,1:T(8,128)(2,1)} copy(bf16[512,2048]{1,0:T(8,128)(2,1)} %param.11) | data formatting | bytes 4194304 | tf_op args[3]
  74.5 2.8 %fusion.51 = f32[16,128,256]{2,1,0:T(8,128)S(1)} fusion(bf16[256,16,128]{0,2,1:T(8,128)(2,1)} %bitcast.150, bf16[16,256,256]{2,1,0:T(8,128)(2,1)} %multiply_convert_fusion.2), kind=kOutput, calls=%fused_computation.85 | convolution fusion | flops 268435456 | bytes 5242880 | tf_op jit(solution)/shard_map/hbs,she->bhe/dot_general | solution.py:65
  85.3 8.6 %all-reduce = (f32[512]{0:T(512)S(1)}, f32[512]{0:T(512)S(1)}) all-reduce(f32[512]{0:T(512)S(1)} %get-tuple-element.22, f32[512]{0:T(512)S(1)} %fusion.2), channel_id=1, replica_groups=mesh['head'=4,'seq'=32] {'head'}, use_global_device_ids=true, to_apply=%region_2.3 | all-reduce | flops 1024 | bytes 8192 | tf_op jit(solution)/shard_map/psum | solution.py:94
  93.9 4.5 %fusion.5 = (bf16[512,2048]{0,1:T(8,128)(2,1)S(1)}, bf16[512,2048]{0,1:T(8,128)(2,1)}) fusion(f32[512,16,128]{0,2,1:T(8,128)} %copy-done.1, f32[512]{0:T(512)S(1)} %get-tuple-element.36, f32[512]{0:T(512)S(1)} %get-tuple-element.19, f32[512]{0:T(512)S(1)} %get-tuple-element.37, f32[2048]{0:T(1024)S(1)} %copy-done.34, bf16[512,2048]{0,1:T(8,128)(2,1)} %copy.64, ...), kind=kLoop, calls=%fused_computation.9 | loop fusion | flops 11534336 | bytes 10501120 | tf_op jit(solution)/shard_map/convert_element_type | solution.py:101
  98.6 1.8 copy-done.17
  106.4 1.8 fusion.57
  111.5 2.1 %collective-permute-start.2 = (f32[8,128,128]{2,1,0:T(8,128)S(1)}, f32[8,128,128]{2,1,0:T(8,128)S(1)}, u32[]{:S(2)}, u32[]{:S(2)}) collective-permute-start(f32[8,128,128]{2,1,0:T(8,128)S(1)} %constant_dynamic-slice_fusion), channel_id=1, source_target_pairs={{0,1},{1,0},{2,3},{3,2},{4,5},{5,4},{6,7},{7,6},{8,9},{9,8},{10,11... | collective-permute-start | bytes 1572872 | tf_op jit(solution)/shard_map/ppermute | solution.py:25
  113.6 1.5 fusion.24
  116.5 2.2 %fusion.52 = f32[16,128,256]{2,1,0:T(8,128)} fusion(bf16[256,16,128]{0,2,1:T(8,128)(2,1)S(1)} %bitcast.125, bf16[16,256,256]{2,1,0:T(8,128)(2,1)S(1)} %multiply_convert_fusion.1), kind=kOutput, calls=%fused_computation.86 | convolution fusion | flops 268435456 | bytes 5242880 | tf_op jit(solution)/shard_map/hbs,shd->bhd/dot_general | solution.py:115
  119.6 4.3 %all-to-all-start.2 = ((f32[16,64,128]{2,1,0:T(8,128)}), f32[16,64,128]{2,1,0:T(8,128)}, u32[]{:S(2)}, u32[]{:S(2)}) async-start(f32[16,64,128]{2,1,0:T(8,128)} %bitcast.158), calls=%async_computation.2 | async-start | bytes 1048576 | tf_op jit(solution)/shard_map/all_to_all | solution.py:26
  123.8 3.9 %fusion.23 = bf16[256,16,128]{0,2,1:T(8,128)(2,1)} fusion(f32[16,128,256]{2,1,0:T(8,128)} %fusion.52, bf16[256,16,128]{0,2,1:T(8,128)(2,1)} %bitcast.134, f32[8,128,128]{1,2,0:T(8,128)} %copy-done.23, f32[8,128,128]{1,2,0:T(8,128)} %copy-done.22), kind=kOutput, calls=%fused_computation.40 | convolution fusion | flops 135528448 | bytes 5242880 | tf_op jit(solution)/shard_map/bhe,hde->bhd/dot_general | solution.py:113
  127.7 1.5 fusion.27
  129.2 5.0 %all-to-all-done.2 = f32[16,64,128]{2,1,0:T(8,128)} async-done(((f32[16,64,128]{2,1,0:T(8,128)}), f32[16,64,128]{2,1,0:T(8,128)}, u32[]{:S(2)}, u32[]{:S(2)}) %all-to-all-start.2) | async-done | bytes 524320 | tf_op jit(solution)/shard_map/all_to_all | solution.py:26
  136.1 4.2 %all-to-all-start.3 = ((f32[16,64,128]{2,1,0:T(8,128)}), f32[16,64,128]{2,1,0:T(8,128)}, u32[]{:S(2)}, u32[]{:S(2)}) async-start(f32[16,64,128]{2,1,0:T(8,128)} %broadcast_in_dim.8), calls=%async_computation.3 | async-start | bytes 1048576 | tf_op jit(solution)/shard_map/all_to_all | solution.py:30
  140.4 2.9 %pad_maximum_fusion.3 = bf16[512,16,128]{0,2,1:T(8,128)(2,1)} fusion(bf16[256,16,128]{0,2,1:T(8,128)(2,1)} %fusion.28, bf16[256,16,128]{0,2,1:T(8,128)(2,1)S(1)} %copy-done.29), kind=kLoop, calls=%fused_computation.25 | loop fusion | flops 4194304 | bytes 4194304 | tf_op jit(solution)/shard_map/concatenate | solution.py:154
  143.3 1.8 fusion.55
  145.0 4.5 %all-to-all-done.3 = f32[16,64,128]{2,1,0:T(8,128)} async-done(((f32[16,64,128]{2,1,0:T(8,128)}), f32[16,64,128]{2,1,0:T(8,128)}, u32[]{:S(2)}, u32[]{:S(2)}) %all-to-all-start.3) | async-done | bytes 524320 | tf_op jit(solution)/shard_map/all_to_all | solution.py:30
  149.5 2.0 %copy.82 = f32[8,128,128]{1,2,0:T(8,128)} copy(f32[8,128,128]{2,1,0:T(8,128)} %bitcast.24) | data formatting | bytes 1048576 | tf_op jit(solution)/shard_map/reshape | solution.py:32
  151.6 3.3 %collective-permute-start.3 = (f32[8,128,128]{1,2,0:T(8,128)}, f32[8,128,128]{1,2,0:T(8,128)}, u32[]{:S(2)}, u32[]{:S(2)}) collective-permute-start(f32[8,128,128]{1,2,0:T(8,128)} %copy.82), channel_id=1, source_target_pairs={{0,1},{1,0},{2,3},{3,2},{4,5},{5,4},{6,7},{7,6},{8,9},{9,8},{10,11... | collective-permute-start | bytes 1572872 | tf_op jit(solution)/shard_map/ppermute | solution.py:33
  154.8 2.7 %pad_maximum_fusion.1 = bf16[512,16,128]{0,2,1:T(8,128)(2,1)} fusion(bf16[256,16,128]{0,2,1:T(8,128)(2,1)} %fusion.24, bf16[256,16,128]{0,2,1:T(8,128)(2,1)S(1)} %copy-done.28), kind=kLoop, calls=%fused_computation.23 | loop fusion | flops 4194304 | bytes 4194304 | tf_op jit(solution)/shard_map/concatenate | solution.py:152
  157.6 3.9 %copy.90 = bf16[512,2048]{1,0:T(8,128)(2,1)} copy(bf16[512,2048]{0,1:T(8,128)(2,1)} %bitcast.153) | data formatting | bytes 4194304
  161.5 4.0 %copy.88 = bf16[512,2048]{1,0:T(8,128)(2,1)} copy(bf16[512,2048]{0,1:T(8,128)(2,1)} %bitcast.154) | data formatting | bytes 4194304
  165.5 2.4 %fusion.25 = bf16[256,16,128]{0,2,1:T(8,128)(2,1)S(1)} fusion(f32[16,128,256]{2,1,0:T(8,128)} %fusion.55, bf16[256,16,128]{0,2,1:T(8,128)(2,1)S(1)} %bitcast.130, f32[16,128,128]{2,1,0:T(8,128)} %copy-done.18), kind=kOutput, calls=%fused_computation.42 | convolution fusion | flops 135528448 | bytes 5242880 | tf_op jit(solution)/shard_map/bhe,hde->bhd/dot_general | solution.py:116
  167.9 1.5 pad_maximum_fusion.2
  169.4 3.9 %copy.89 = bf16[512,2048]{1,0:T(8,128)(2,1)} copy(bf16[512,2048]{0,1:T(8,128)(2,1)} %bitcast.157) | data formatting | bytes 4194304
  173.3 4.0 %copy.87 = bf16[512,2048]{1,0:T(8,128)(2,1)} copy(bf16[512,2048]{0,1:T(8,128)(2,1)} %get-tuple-element.21) | data formatting | bytes 4194304
  178.5 3.2 %fusion.13 = bf16[16,128,512]{2,1,0:T(8,128)(2,1)} fusion(f32[8,128,128]{1,2,0:T(8,128)S(1)} %get-tuple-element.33, f32[8,128,128]{1,2,0:T(8,128)S(1)} %get-tuple-element.32, bf16[512,2048]{1,0:T(8,128)(2,1)S(1)} %copy-done), kind=kOutput, calls=%fused_computation.34 | convolution fusion | flops 1611923456 | bytes 5242880 | tf_op jit(solution)/shard_map/thd,hde->the/dot_general | solution.py:149
  181.6 3.2 %fusion.16 = bf16[16,128,512]{2,1,0:T(8,128)(2,1)} fusion(f32[8,128,128]{1,2,0:T(8,128)S(1)} %get-tuple-element.33, f32[8,128,128]{1,2,0:T(8,128)S(1)} %get-tuple-element.32, bf16[512,2048]{1,0:T(8,128)(2,1)S(1)} %copy-done.33), kind=kOutput, calls=%fused_computation.35 | convolution fusion | flops 1611923456 | bytes 5242880 | tf_op jit(solution)/shard_map/the,hde->thd/dot_general | solution.py:146
  184.9 3.9 %copy.92 = bf16[512,2048]{1,0:T(8,128)(2,1)} copy(bf16[512,2048]{0,1:T(8,128)(2,1)} %bitcast.156) | data formatting | bytes 4194304
  188.8 3.9 %copy.91 = bf16[512,2048]{1,0:T(8,128)(2,1)} copy(bf16[512,2048]{0,1:T(8,128)(2,1)} %bitcast.155) | data formatting | bytes 4194304
  (100 shorter events, 28.2 us)
Async XLA Ops:
  0.6 1.6 copy-start
  5.5 20.6 %collective-permute-start = (f32[8,128,128]{2,1,0:T(8,128)}, f32[8,128,128]{2,1,0:T(8,128)}, u32[]{:S(2)}, u32[]{:S(2)}) collective-permute-start(f32[8,128,128]{2,1,0:T(8,128)} %constant_dynamic-slice_fusion.1), channel_id=1, source_target_pairs={{0,1},{1,0},{2,3},{3,2},{4,5},{5,4},{6,7},{7,6},{8,9},{9,8},{10,11... | collective-permute-start | bytes 1572872 | tf_op jit(solution)/shard_map/ppermute | solution.py:25
  28.0 18.1 %all-to-all-start = ((f32[16,64,128]{2,1,0:T(8,128)}), f32[16,64,128]{2,1,0:T(8,128)}, u32[]{:S(2)}, u32[]{:S(2)}) async-start(f32[16,64,128]{2,1,0:T(8,128)} %bitcast), calls=%async_computation | async-start | bytes 1048576 | tf_op jit(solution)/shard_map/all_to_all | solution.py:26
  48.0 13.7 %all-to-all-start.1 = ((f32[16,64,128]{2,1,0:T(8,128)}), f32[16,64,128]{2,1,0:T(8,128)}, u32[]{:S(2)}, u32[]{:S(2)}) async-start(f32[16,64,128]{2,1,0:T(8,128)} %broadcast_in_dim.6), calls=%async_computation.1 | async-start | bytes 1048576 | tf_op jit(solution)/shard_map/all_to_all | solution.py:30
  52.5 3.4 %copy-start.2 = (bf16[256,2048]{0,1:T(8,128)(2,1)S(1)}, bf16[256,2048]{0,1:T(8,128)(2,1)}, u32[]{:S(2)}) copy-start(bf16[256,2048]{0,1:T(8,128)(2,1)} %get-tuple-element.42) | copy-start | bytes 3145732
  54.5 1.3 copy-start.13
  63.8 13.5 %collective-permute-start.1 = (f32[8,128,128]{1,2,0:T(8,128)}, f32[8,128,128]{1,2,0:T(8,128)}, u32[]{:S(2)}, u32[]{:S(2)}) collective-permute-start(f32[8,128,128]{1,2,0:T(8,128)} %copy.51), channel_id=1, source_target_pairs={{0,1},{1,0},{2,3},{3,2},{4,5},{5,4},{6,7},{7,6},{8,9},{9,8},{10,11... | collective-permute-start | bytes 1572872 | tf_op jit(solution)/shard_map/ppermute | solution.py:33
  74.5 2.8 %copy-start.32 = (f32[8,128,128]{1,2,0:T(8,128)S(1)}, f32[8,128,128]{1,2,0:T(8,128)}, u32[]{:S(2)}) copy-start(f32[8,128,128]{1,2,0:T(8,128)} %copy.51) | copy-start | bytes 1572868
  77.3 1.4 copy-start.3
  78.6 2.8 %copy-start.22 = (f32[8,128,128]{1,2,0:T(8,128)}, f32[8,128,128]{1,2,0:T(8,128)S(1)}, u32[]{:S(2)}) copy-start(f32[8,128,128]{1,2,0:T(8,128)S(1)} %get-tuple-element.34) | copy-start | bytes 1572868
  78.6 2.8 %copy-start.23 = (f32[8,128,128]{1,2,0:T(8,128)}, f32[8,128,128]{1,2,0:T(8,128)S(1)}, u32[]{:S(2)}) copy-start(f32[8,128,128]{1,2,0:T(8,128)S(1)} %get-tuple-element.35) | copy-start | bytes 1572868
  78.6 1.6 copy-start.9
  78.6 2.3 %copy-start.24 = (f32[16,128,256]{2,1,0:T(8,128)S(1)}, f32[16,128,256]{2,1,0:T(8,128)}, u32[]{:S(2)}) copy-start(f32[16,128,256]{2,1,0:T(8,128)} %fusion.50) | copy-start | bytes 6291460
  80.9 0.8 copy-start.26
  80.9 1.4 copy-start.7
  82.7 1.7 copy-start.12
  82.7 1.7 copy-start.34
  83.3 2.0 %copy-start.1 = (f32[512,16,128]{0,2,1:T(8,128)}, f32[512,16,128]{0,2,1:T(8,128)S(1)}, u32[]{:S(2)}) copy-start(f32[512,16,128]{0,2,1:T(8,128)S(1)} %get-tuple-element.23) | copy-start | bytes 12582916
  98.4 2.0 %copy-start.17 = (bf16[16,256,256]{2,1,0:T(8,128)(2,1)S(1)}, bf16[16,256,256]{2,1,0:T(8,128)(2,1)}, u32[]{:S(2)}) copy-start(bf16[16,256,256]{2,1,0:T(8,128)(2,1)} %multiply_convert_fusion.2) | copy-start | bytes 6291460
  98.5 11.9 %copy-start.6 = (bf16[256,2048]{0,1:T(8,128)(2,1)}, bf16[256,2048]{0,1:T(8,128)(2,1)S(1)}, u32[]{:S(2)}) copy-start(bf16[256,2048]{0,1:T(8,128)(2,1)S(1)} %get-tuple-element.24) | copy-start | bytes 3145732
  100.4 1.2 copy-start.8
  101.6 1.2 copy-start.21
  102.8 7.6 %copy-start.18 = (f32[16,128,128]{2,1,0:T(8,128)}, f32[16,128,128]{2,1,0:T(8,128)S(1)}, u32[]{:S(2)}) copy-start(f32[16,128,128]{2,1,0:T(8,128)S(1)} %fusion.54) | copy-start | bytes 3145732
  103.6 1.2 copy-start.20
  104.8 1.6 copy-start.14
  106.4 1.8 copy-start.4
  109.0 7.5 %copy-start.15 = (bf16[16,256,256]{2,1,0:T(8,128)(2,1)}, bf16[16,256,256]{2,1,0:T(8,128)(2,1)S(1)}, u32[]{:S(2)}) copy-start(bf16[16,256,256]{2,1,0:T(8,128)(2,1)S(1)} %multiply_convert_fusion.1) | copy-start | bytes 6291460
  109.0 2.0 %copy-start.10 = (bf16[256,2048]{0,1:T(8,128)(2,1)S(1)}, bf16[256,2048]{0,1:T(8,128)(2,1)}, u32[]{:S(2)}) copy-start(bf16[256,2048]{0,1:T(8,128)(2,1)} %get-tuple-element.26) | copy-start | bytes 3145732
  111.0 2.6 %copy-start.27 = (bf16[16,128,128]{1,2,0:T(8,128)(2,1)S(1)}, bf16[16,128,128]{1,2,0:T(8,128)(2,1)}, u32[]{:S(2)}) copy-start(bf16[16,128,128]{1,2,0:T(8,128)(2,1)} %copy-done.26) | copy-start | bytes 1572868
  111.5 7.2 %collective-permute-start.2 = (f32[8,128,128]{2,1,0:T(8,128)S(1)}, f32[8,128,128]{2,1,0:T(8,128)S(1)}, u32[]{:S(2)}, u32[]{:S(2)}) collective-permute-start(f32[8,128,128]{2,1,0:T(8,128)S(1)} %constant_dynamic-slice_fusion), channel_id=1, source_target_pairs={{0,1},{1,0},{2,3},{3,2},{4,5},{5,4},{6,7},{7,6},{8,9},{9,8},{10,11... | collective-permute-start | bytes 1572872 | tf_op jit(solution)/shard_map/ppermute | solution.py:25
  119.6 14.6 %all-to-all-start.2 = ((f32[16,64,128]{2,1,0:T(8,128)}), f32[16,64,128]{2,1,0:T(8,128)}, u32[]{:S(2)}, u32[]{:S(2)}) async-start(f32[16,64,128]{2,1,0:T(8,128)} %bitcast.158), calls=%async_computation.2 | async-start | bytes 1048576 | tf_op jit(solution)/shard_map/all_to_all | solution.py:26
  123.8 3.9 %copy-start.19 = (f32[16,128,128]{2,1,0:T(8,128)S(1)}, f32[16,128,128]{2,1,0:T(8,128)}, u32[]{:S(2)}) copy-start(f32[16,128,128]{2,1,0:T(8,128)} %copy-done.18) | copy-start | bytes 3145732
  123.8 3.9 %copy-start.25 = (f32[16,128,256]{2,1,0:T(8,128)S(1)}, f32[16,128,256]{2,1,0:T(8,128)}, u32[]{:S(2)}) copy-start(f32[16,128,256]{2,1,0:T(8,128)} %fusion.57) | copy-start | bytes 6291460
  129.2 11.2 %copy-start.29 = (bf16[256,16,128]{0,2,1:T(8,128)(2,1)S(1)}, bf16[256,16,128]{0,2,1:T(8,128)(2,1)}, u32[]{:S(2)}) copy-start(bf16[256,16,128]{0,2,1:T(8,128)(2,1)} %fusion.27) | copy-start | bytes 3145732
  136.1 13.4 %all-to-all-start.3 = ((f32[16,64,128]{2,1,0:T(8,128)}), f32[16,64,128]{2,1,0:T(8,128)}, u32[]{:S(2)}, u32[]{:S(2)}) async-start(f32[16,64,128]{2,1,0:T(8,128)} %broadcast_in_dim.8), calls=%async_computation.3 | async-start | bytes 1048576 | tf_op jit(solution)/shard_map/all_to_all | solution.py:30
  140.4 2.9 %copy-start.11 = (bf16[256,2048]{0,1:T(8,128)(2,1)S(1)}, bf16[256,2048]{0,1:T(8,128)(2,1)}, u32[]{:S(2)}) copy-start(bf16[256,2048]{0,1:T(8,128)(2,1)} %get-tuple-element.26) | copy-start | bytes 3145732
  140.4 2.9 %copy-start.16 = (bf16[16,256,256]{2,1,0:T(8,128)(2,1)S(1)}, bf16[16,256,256]{2,1,0:T(8,128)(2,1)}, u32[]{:S(2)}) copy-start(bf16[16,256,256]{2,1,0:T(8,128)(2,1)} %copy-done.15) | copy-start | bytes 6291460
  143.3 11.6 %copy-start.28 = (bf16[256,16,128]{0,2,1:T(8,128)(2,1)S(1)}, bf16[256,16,128]{0,2,1:T(8,128)(2,1)}, u32[]{:S(2)}) copy-start(bf16[256,16,128]{0,2,1:T(8,128)(2,1)} %fusion.23) | copy-start | bytes 3145732
  151.6 25.7 %collective-permute-start.3 = (f32[8,128,128]{1,2,0:T(8,128)}, f32[8,128,128]{1,2,0:T(8,128)}, u32[]{:S(2)}, u32[]{:S(2)}) collective-permute-start(f32[8,128,128]{1,2,0:T(8,128)} %copy.82), channel_id=1, source_target_pairs={{0,1},{1,0},{2,3},{3,2},{4,5},{5,4},{6,7},{7,6},{8,9},{9,8},{10,11... | collective-permute-start | bytes 1572872 | tf_op jit(solution)/shard_map/ppermute | solution.py:33
  161.5 4.0 %copy-start.5 = (bf16[256,2048]{0,1:T(8,128)(2,1)S(1)}, bf16[256,2048]{0,1:T(8,128)(2,1)}, u32[]{:S(2)}) copy-start(bf16[256,2048]{0,1:T(8,128)(2,1)} %get-tuple-element.42) | copy-start | bytes 3145732
  165.5 2.4 %copy-start.30 = (bf16[256,16,128]{0,2,1:T(8,128)(2,1)S(1)}, bf16[256,16,128]{0,2,1:T(8,128)(2,1)}, u32[]{:S(2)}) copy-start(bf16[256,16,128]{0,2,1:T(8,128)(2,1)} %fusion.26) | copy-start | bytes 3145732
  173.3 4.0 %copy-start.31 = (f32[8,128,128]{1,2,0:T(8,128)S(1)}, f32[8,128,128]{1,2,0:T(8,128)}, u32[]{:S(2)}) copy-start(f32[8,128,128]{1,2,0:T(8,128)} %copy.82) | copy-start | bytes 1572868
  178.4 3.2 %copy-start.33 = (bf16[512,2048]{1,0:T(8,128)(2,1)S(1)}, bf16[512,2048]{1,0:T(8,128)(2,1)}, u32[]{:S(2)}) copy-start(bf16[512,2048]{1,0:T(8,128)(2,1)} %param.13) | copy-start | bytes 6291460

commit v2 on v0

v2 whole, which is shorter than its diff:
```python
import functools

import jax
import jax.numpy as jnp
from jax import lax
from jax.experimental import pallas as pl
from jax.experimental.pallas import tpu as pltpu
from jax.sharding import PartitionSpec as P

H = 64
HEAD_DIM = 128
BLOCK = 256
WIDTH = H * HEAD_DIM
EPSILON = 1e-06

GROUP = 2
VMEM_LIMIT = 24 * 1024 * 1024

F32 = jnp.float32
BF16 = jnp.bfloat16


def dot_nn(a, b):
    return lax.dot_general(a, b, (((1,), (0,)), ((), ())), preferred_element_type=F32)


def dot_nt(a, b):
    return lax.dot_general(a, b, (((1,), (1,)), ((), ())), preferred_element_type=F32)


def dot_tn(a, b):
    return lax.dot_general(a, b, (((0,), (0,)), ((), ())), preferred_element_type=F32)


def lanes(head):
    return slice(head * HEAD_DIM, (head + 1) * HEAD_DIM)


def rows(block):
    return slice(block * BLOCK, (block + 1) * BLOCK)


def block_mask(upper):
    row = lax.broadcasted_iota(jnp.int32, (BLOCK, BLOCK), 0)
    column = lax.broadcasted_iota(jnp.int32, (BLOCK, BLOCK), 1)
    return column >= row if upper else row >= column


def prefix_state_kernel(meta, k_ref, v_ref, s_ref):
    for h in range(GROUP):
        s_ref[h] = dot_tn(k_ref[:, lanes(h)], v_ref[:, lanes(h)])


def intra_kernel(meta, q_ref, k_ref, v_ref, o_ref, kv_ref, qt_ref):
    lower = block_mask(False)
    for h in range(GROUP):
        for b in range(q_ref.shape[0] // BLOCK):
            q, k, v = (ref[rows(b), lanes(h)] for ref in (q_ref, k_ref, v_ref))
            scores = jnp.where(lower, dot_nt(q, k), 0.0).astype(BF16)
            o_ref[rows(b), lanes(h)] = dot_nn(scores, v)
        kv_ref[h] = dot_tn(k_ref[rows(0), lanes(h)], v_ref[rows(0), lanes(h)])
        qt_ref[h] = q_ref[:, lanes(h)].T


def spread_sum_kernel(pieces_ref, out_ref):
    total = jnp.sum(pieces_ref[...], axis=0)
    for i in range(out_ref.shape[0]):
        out_ref[i] = total


def forward_kernel(meta, q_ref, intra_ref, s_ref, kv_ref, dy_ref, gain_ref, *rest):
    *before, o_ref, m_ref, stats_ref, square_acc, inner_acc = rest

    @pl.when(pl.program_id(0) == 0)
    def _():
        square_acc[...] = jnp.zeros_like(square_acc)
        inner_acc[...] = jnp.zeros_like(inner_acc)

    for h in range(GROUP):
        state = s_ref[h]
        gain = gain_ref[:, lanes(h)]
        for b, m in enumerate((state.astype(BF16), (state + kv_ref[h]).astype(BF16))):
            m_ref[h, b] = m
            o = intra_ref[rows(b), lanes(h)] + dot_nn(q_ref[rows(b), lanes(h)], m)
            o_ref[rows(b), lanes(h)] = o
            square_acc[rows(b)] += o * o
            inner_acc[rows(b)] += gain * dy_ref[rows(b), lanes(h)].astype(F32) * o

    @pl.when(pl.program_id(0) == pl.num_programs(0) - 1)
    def _():
        for i, acc in enumerate((square_acc, inner_acc)):
            row = jnp.sum(acc[...].T, axis=0, keepdims=True)
            if before:
                row = row + before[0][i : i + 1]
            stats_ref[i : i + 1] = row


def out_grad(dy_ref, o_ref, gain_ref, inv_ref, coef_ref, h):
    scaled = gain_ref[:, lanes(h)] * dy_ref[:, lanes(h)].astype(F32)
    return (scaled * inv_ref[...] - o_ref[:, lanes(h)] * coef_ref[...]).astype(BF16)


def state_grad_kernel(first, meta, dy_ref, o_ref, gain_ref, qt_ref, *rest):
    if first:
        *stats, ds_ref, g_ref, inv_ref, coef_ref = rest

        @pl.when(pl.program_id(0) == 0)
        def _():
            total = sum(ref[...] for ref in stats[1:]) + stats[0][...]
            inv = 1.0 / jnp.sqrt(total[0:1] / WIDTH + EPSILON)
            coef = total[1:2] * (inv * inv * inv) / WIDTH
            live = lax.broadcasted_iota(jnp.int32, inv.shape, 1) < meta[1]
            for value, ref in ((inv, inv_ref), (coef, coef_ref)):
                value = jnp.where(live, value, 0.0)
                for n in range(value.shape[1] // HEAD_DIM):
                    square = jnp.broadcast_to(value[:, lanes(n)], (HEAD_DIM, HEAD_DIM))
                    ref[n * HEAD_DIM : (n + 1) * HEAD_DIM] = square.T

    else:
        inv_ref, coef_ref, ds_ref, g_ref = rest
    for h in range(GROUP):
        do = out_grad(dy_ref, o_ref, gain_ref, inv_ref, coef_ref, h)
        later = dot_nn(qt_ref[h][:, rows(1)], do[rows(1)])
        ds_ref[h] = later + dot_nn(qt_ref[h][:, rows(0)], do[rows(0)])
        g_ref[h] = later.astype(BF16)


def backward_kernel(
    meta, q_ref, k_ref, v_ref, dy_ref, o_ref, gain_ref, m_ref, g_ref, inv_ref, coef_ref, *rest
):
    normed_ref, dq_ref, dk_ref, dv_ref = rest[-4:]
    lower, upper = block_mask(False), block_mask(True)
    for h in range(GROUP):
        normed_ref[:, lanes(h)] = (
            gain_ref[:, lanes(h)] * o_ref[:, lanes(h)] * inv_ref[...]
        ).astype(BF16)
        do_all = out_grad(dy_ref, o_ref, gain_ref, inv_ref, coef_ref, h)
        for b in range(2):
            q, k, v = (ref[rows(b), lanes(h)] for ref in (q_ref, k_ref, v_ref))
            do = do_all[rows(b)]
            p = jnp.where(lower, dot_nt(do, v), 0.0).astype(BF16)
            p_t = jnp.where(upper, dot_nt(v, do), 0.0).astype(BF16)
            scores_t = jnp.where(upper, dot_nt(k, q), 0.0).astype(BF16)
            dq = dot_nt(do, m_ref[h, b]) + dot_nn(p, k)
            dk = dot_nn(p_t, q)
            dv = dot_nn(scores_t, do)
            if b == 0:
                dk = dk + dot_nt(v, g_ref[h])
                dv = dv + dot_nn(k, g_ref[h])
            dq_ref[rows(b), lanes(h)] = dq.astype(BF16)
            dk_ref[rows(b), lanes(h)] = dk.astype(BF16)
            dv_ref[rows(b), lanes(h)] = dv.astype(BF16)


def prefix_grad_kernel(meta, k_ref, v_ref, ds_ref, *rest):
    dk_ref, dv_ref = rest[-2:]
    for h in range(GROUP):
        ds = ds_ref[h]
        high = ds.astype(BF16)
        low = (ds - high.astype(F32)).astype(BF16)
        k, v = k_ref[:, lanes(h)], v_ref[:, lanes(h)]
        dk = dot_nt(jnp.concatenate([v, v], 1), jnp.concatenate([high, low], 1))
        dv = dot_nn(jnp.concatenate([k, k], 1), jnp.concatenate([high, low], 0))
        dk_ref[:, lanes(h)] = dk.astype(BF16)
        dv_ref[:, lanes(h)] = dv.astype(BF16)


def body(queries, keys, values, cotangent, prefix_keys, prefix_values, gain, lengths):
    tok_rows, tok_cols = queries.shape
    pre_rows = prefix_keys.shape[0]
    half = tok_cols // HEAD_DIM // 2
    steps = half // GROUP
    seq_size = lax.axis_size("seq")
    head_size = lax.axis_size("head")
    chips = seq_size // 2
    core = lax.axis_index("seq") % 2
    swap = [(i, i ^ 1) for i in range(seq_size)]
    chip_groups = [list(range(c, seq_size, 2)) for c in range(2)]
    meta = jnp.stack([core.astype(jnp.int32), lengths[0]])
    gain_row = gain[None]
    OWN, OTHER = 0, steps

    def call(kernel, part, ins, outs, flops, scratch=(), aliased=()):
        def column(i, meta):
            return (0, lax.rem(meta[0] * steps + part + i, 2 * steps))

        def spec(kind, shape):
            if kind == "wide":
                return pl.BlockSpec((shape[0], GROUP * HEAD_DIM), column)
            if kind == "half":
                return pl.BlockSpec((shape[0], GROUP * HEAD_DIM), lambda i, meta: (0, i))
            if kind == "heads":
                return pl.BlockSpec(
                    (GROUP,) + shape[1:], lambda i, meta: (i,) + (0,) * (len(shape) - 1)
                )
            return pl.BlockSpec(shape, lambda i, meta: (0,) * len(shape))

        arrays = [a for _, a in ins]
        moved = sum(a.size * a.dtype.itemsize for a in arrays) + sum(
            functools.reduce(lambda x, y: x * y, s) * jnp.dtype(d).itemsize for _, s, d in outs
        )
        return pl.pallas_call(
            kernel,
            grid_spec=pltpu.PrefetchScalarGridSpec(
                num_scalar_prefetch=1,
                grid=(steps,),
                in_specs=[spec(kind, a.shape) for kind, a in ins]
                + [pl.BlockSpec(memory_space=pl.ANY) for _ in aliased],
                out_specs=[spec(kind, s) for kind, s, _ in outs],
                scratch_shapes=scratch,
            ),
            out_shape=[jax.ShapeDtypeStruct(s, d) for _, s, d in outs],
            input_output_aliases={1 + len(arrays) + i: i for i in range(len(aliased))},
            cost_estimate=pl.CostEstimate(flops=flops, bytes_accessed=moved, transcendentals=0),
            compiler_params=pltpu.CompilerParams(vmem_limit_bytes=VMEM_LIMIT),
        )(meta, *arrays, *aliased)

    square = HEAD_DIM * HEAD_DIM
    states = (half, HEAD_DIM, HEAD_DIM)
    wide, narrow = (tok_rows, tok_cols), (tok_rows, tok_cols // 2)
    unit = 2 * half * tok_rows * square

    def exchange(value):
        return lax.all_to_all(
            value, "seq", 0, 0, axis_index_groups=chip_groups, tiled=True
        )

    def spread_sum(pieces):
        return pl.pallas_call(
            spread_sum_kernel,
            out_shape=jax.ShapeDtypeStruct(pieces.shape, F32),
            compiler_params=pltpu.CompilerParams(vmem_limit_bytes=VMEM_LIMIT),
        )(pieces)

    def sum_over_seq(mine, theirs):
        paired = mine + lax.ppermute(theirs, "seq", swap)
        pieces = exchange(paired.reshape(chips, -1, HEAD_DIM))
        gathered = exchange(spread_sum(pieces)).reshape(states)
        return gathered, lax.ppermute(gathered, "seq", swap)

    def prefix_state(part):
        return call(
            prefix_state_kernel,
            part,
            [("wide", prefix_keys), ("wide", prefix_values)],
            [("heads", states, F32)],
            unit,
        )[0]

    theirs = prefix_state(OTHER)
    mine = prefix_state(OWN)
    sums = sum_over_seq(mine, theirs)

    intra = [
        call(
            intra_kernel,
            part,
            [("wide", queries), ("wide", keys), ("wide", values)],
            [
                ("half", narrow, F32),
                ("heads", states, F32),
                ("heads", (half, HEAD_DIM, tok_rows), BF16),
            ],
            9 * unit // 2,
        )
        for part in (OWN, OTHER)
    ]

    forward = []
    for i, part in enumerate((OWN, OTHER)):
        forward.append(
            call(
                forward_kernel,
                part,
                [
                    ("wide", queries),
                    ("half", intra[i][0]),
                    ("heads", sums[i]),
                    ("heads", intra[i][1]),
                    ("wide", cotangent),
                    ("wide", gain_row),
                ]
                + [("whole", f[2]) for f in forward],
                [
                    ("half", narrow, F32),
                    ("heads", (half, 2, HEAD_DIM, HEAD_DIM), BF16),
                    ("whole", (2, tok_rows), F32),
                ],
                unit,
                scratch=[pltpu.VMEM((tok_rows, HEAD_DIM), F32)] * 2,
            )
        )
    stats = forward[1][2]
    all_stats = [stats] + [
        lax.ppermute(stats, "head", [(i, (i + k) % head_size) for i in range(head_size)])
        for k in range(1, head_size)
    ]

    def state_grad(i, part, scalars):
        first = len(scalars) > 2
        scalar = (tok_rows, HEAD_DIM)
        return call(
            functools.partial(state_grad_kernel, first),
            part,
            [
                ("wide", cotangent),
                ("half", forward[i][0]),
                ("wide", gain_row),
                ("heads", intra[i][2]),
            ]
            + [("whole", a) for a in scalars],
            [("heads", states, F32), ("heads", states, BF16)]
            + [("whole", scalar, F32), ("whole", scalar, F32)] * first,
            unit,
        )

    theirs, later_other, inv, coef = state_grad(1, OTHER, all_stats)
    mine, later_own = state_grad(0, OWN, [inv, coef])
    sums = sum_over_seq(mine, theirs)

    grads = ()
    for i, (part, later) in enumerate(((OWN, later_own), (OTHER, later_other))):
        grads = call(
            backward_kernel,
            part,
            [
                ("wide", queries),
                ("wide", keys),
                ("wide", values),
                ("wide", cotangent),
                ("half", forward[i][0]),
                ("wide", gain_row),
                ("heads", forward[i][1]),
                ("heads", later),
                ("whole", inv),
                ("whole", coef),
            ],
            [("wide", wide, BF16)] * 4,
            16 * unit,
            aliased=grads,
        )

    prefix_grads = ()
    for part, total in ((OWN, sums[0]), (OTHER, sums[1])):
        prefix_grads = call(
            prefix_grad_kernel,
            part,
            [("wide", prefix_keys), ("wide", prefix_values), ("heads", total)],
            [("wide", (pre_rows, tok_cols), BF16)] * 2,
            4 * unit,
            aliased=prefix_grads,
        )
    return (*grads, *prefix_grads)


def solution(mesh):
    spread = P("seq", "head")
    return jax.shard_map(
        body,
        mesh=mesh,
        in_specs=(spread,) * 6 + (P("head"), P("seq")),
        out_specs=(spread,) * 6,
        check_vma=False,
    )
```

time: 294 us -> 125 us (0.43)
  waiting for transfers between devices: 152 us -> 1.42 us
  local copies, waits for them, and re-layouts: 53.5 us -> 3.22 us
  matrix products: 50 us -> 0 us
  blocking collectives: 8.75 us -> 57.5 us
  Pallas kernels: 0 us -> 45.9 us
  starting transfers between devices: 0.08 us -> 15 us
  between operations: 15 us -> 1.46 us
  other arithmetic: 13.6 us -> 0.2 us
    psum x2 -> x0, waiting for transfers between devices: 152 us -> none  [the longest x1 77.5 us: summed_prefix(): return lax.psum(partial_state, 'seq')]
    all_to_all x0 -> x4, blocking collectives: none -> 57.5 us  [exchange(): lax.all_to_all(value, 'seq', 0, 0, axis_index_groups=chip_groups, tiled=T...]
    dot_general x26 -> x0, matrix products: 50 us -> none  [the longest x2 6.21 us: intra_block(): jnp.einsum('hbs,she->bhe', scores, v_block, preferred_element_type=jnp.fl...]
    unnamed x82 -> x18, local copies, waits for them, and re-layouts: 52 us -> 3.22 us
    pallas_call x0 -> x14, Pallas kernels: none -> 45.9 us  [the longest x12 45.8 us: call(): pl.pallas_call(kernel, grid_spec=pltpu.PrefetchScalarGridSpec(num_scalar_...]
    ppermute x0 -> x7, starting transfers between devices: none -> 15 us  [the longest x2 6.9 us: sum_over_seq(): return (gathered, lax.ppermute(gathered, 'seq', swap))]
    psum x1 -> x0, blocking collectives: 8.75 us -> none  [body(): lax.psum((jnp.sum(attended * attended, axis=1), jnp.sum(scaled_cot * atte...]
    concatenate x3 -> x0, other arithmetic: 4.53 us -> none  [the longest x1 1.51 us: body(): key_grad = jnp.concatenate(key_parts, axis=0).reshape(tok_rows, tok_cols)]
  transfers between devices with their start and end apart: 2 -> 7, of which waited for: 2 -> 2; matrix products, arithmetic and copies ran while one was open for 19% -> 0% of each run, Pallas kernels for 0% -> 28%
where the time goes in v2:
time: 125 us
  blocking collectives  57.5 us (46%)
  Pallas kernels  45.9 us (37%)
  starting transfers between devices  15 us (12%)
  local copies, waits for them, and re-layouts  3.22 us (3%)
  between operations  1.46 us (1%)
  waiting for transfers between devices  1.42 us (1%)
    all_to_all x4, blocking collectives, exchange(): lax.all_to_all(value, 'seq', 0, 0, axis_index_groups=chip_groups, tiled=T...  57.5 us
    pallas_call x12, Pallas kernels, call(): pl.pallas_call(kernel, grid_spec=pltpu.PrefetchScalarGridSpec(num_scalar_...  45.8 us
    ppermute x2, starting transfers between devices, sum_over_seq(): return (gathered, lax.ppermute(gathered, 'seq', swap))  6.9 us
    ppermute x3, starting transfers between devices, body(): lax.ppermute(stats, 'head', [(i, (i + k) % head_size) for i in range(head...  4.88 us
    unnamed x18, local copies, waits for them, and re-layouts  3.22 us
    ppermute x2, starting transfers between devices, sum_over_seq(): paired = mine + lax.ppermute(theirs, 'seq', swap)  3.2 us
  transfers between devices with their start and end apart: 7, of which 2 were waited for; matrix products, arithmetic and copies ran while one was open for 0% of the time, Pallas kernels for 28%

profile of v2, /device:TPU:1, one launch (start us, length us, event | category | flops | bytes accessed | tf_op | source)
XLA Modules:
  0.0 124.6 jit_solution(13513305758730670428)
XLA Ops:
  1.3 0.1 pad_add_fusion.meta
  1.4 1.6 %copy-done.2 = bf16[512,2048]{1,0:T(8,128)(2,1)S(1)} copy-done((bf16[512,2048]{1,0:T(8,128)(2,1)S(1)}, bf16[512,2048]{1,0:T(8,128)(2,1)}, u32[]{:S(2)}) %copy-start.2) | copy-done | bytes 2097176
  3.0 1.6 %copy-done.4 = bf16[512,2048]{1,0:T(8,128)(2,1)S(1)} copy-done((bf16[512,2048]{1,0:T(8,128)(2,1)S(1)}, bf16[512,2048]{1,0:T(8,128)(2,1)}, u32[]{:S(2)}) %copy-start.4) | copy-done | bytes 2097176
  4.5 2.1 %shard_map.129 = f32[8,128,128]{2,1,0:T(8,128)S(1)} custom-call(s32[2]{0:T(128)S(1)} %pad_add_fusion.meta, bf16[512,2048]{1,0:T(8,128)(2,1)S(1)} %copy-done.2, bf16[512,2048]{1,0:T(8,128)(2,1)S(1)} %copy-done.4), custom_call_target="tpu_custom_call" | custom-call | flops 134217728 | bytes 4718592 | tf_op jit(solution)/shard_map/pallas_call | solution.py:202
  6.6 1.5 %collective-permute-start = (f32[8,128,128]{2,1,0:T(8,128)S(1)}, f32[8,128,128]{2,1,0:T(8,128)S(1)}, u32[]{:S(2)}, u32[]{:S(2)}) collective-permute-start(f32[8,128,128]{2,1,0:T(8,128)S(1)} %shard_map.129), channel_id=1, source_target_pairs={{0,1},{1,0},{2,3},{3,2},{4,5},{5,4},{6,7},{7,6},{8,9},{9,8},{10,11... | collective-permute-start | bytes 1572872 | tf_op jit(solution)/shard_map/ppermute | solution.py:236
  8.1 2.1 %shard_map.128 = f32[8,128,128]{2,1,0:T(8,128)S(1)} custom-call(s32[2]{0:T(128)S(1)} %pad_add_fusion.meta, bf16[512,2048]{1,0:T(8,128)(2,1)S(1)} %copy-done.2, bf16[512,2048]{1,0:T(8,128)(2,1)S(1)} %copy-done.4), custom_call_target="tpu_custom_call" | custom-call | flops 134217728 | bytes 4718592 | tf_op jit(solution)/shard_map/pallas_call | solution.py:202
  10.2 0.0 copy-start
  10.2 0.0 copy-start.6
  10.2 0.0 collective-permute-done
  10.2 0.1 add.11
  10.3 18.0 %all_to_all.20.pieces_ref = f32[16,64,128]{2,1,0:T(8,128)S(1)} all-to-all(f32[16,64,128]{2,1,0:T(8,128)S(1)} %bitcast.16), channel_id=1, replica_groups={{0,2,4,6,8,10,12,14,16,18,20,22,24,26,28,30},{1,3,5,7,9,11,13,15,17,19,..., dimensions={0} | all-to-all | bytes 1048576 | tf_op jit(solution)/shard_map/all_to_all | solution.py:224
  28.4 0.1 shard_map.130
  28.4 13.1 %all_to_all.21 = f32[16,64,128]{2,1,0:T(8,128)S(1)} all-to-all(f32[16,64,128]{2,1,0:T(8,128)S(1)} %shard_map.130), channel_id=1, replica_groups={{0,2,4,6,8,10,12,14,16,18,20,22,24,26,28,30},{1,3,5,7,9,11,13,15,17,19,..., dimensions={0} | all-to-all | bytes 1048576 | tf_op jit(solution)/shard_map/all_to_all | solution.py:224
  41.6 3.5 %collective-permute-start.1 = (f32[8,128,128]{2,1,0:T(8,128)S(1)}, f32[8,128,128]{2,1,0:T(8,128)S(1)}, u32[]{:S(2)}, u32[]{:S(2)}) collective-permute-start(f32[8,128,128]{2,1,0:T(8,128)S(1)} %bitcast.8), channel_id=1, source_target_pairs={{0,1},{1,0},{2,3},{3,2},{4,5},{5,4},{6,7},{7,6},{8,9},{9,8},{10,11... | collective-permute-start | bytes 1572872 | tf_op jit(solution)/shard_map/ppermute | solution.py:239
  45.0 0.0 copy-done.7
  45.0 0.0 copy-done
  45.0 0.0 copy-done.6
  45.0 4.4 %shard_map.127 = (f32[512,1024]{1,0:T(8,128)S(1)}, f32[8,128,128]{2,1,0:T(8,128)S(1)}, bf16[8,128,512]{2,1,0:T(8,128)(2,1)S(1)}) custom-call(s32[2]{0:T(128)S(1)} %pad_add_fusion.meta, bf16[512,2048]{1,0:T(8,128)(2,1)S(1)} %copy-done, bf16[512,2048]{1,0:T(8,128)(2,1)S(1)} %copy-done.6, bf16[512,2048]{1,0:T(8,128)(2,1)S(1)} %copy-done.7), custom_call_target="tpu_custom_call" | custom-call | flops 603979776 | bytes 9961472 | tf_op jit(solution)/shard_map/pallas_call | solution.py:202
  49.4 0.0 copy-start.1
  49.4 0.0 copy-start.8
  49.5 4.4 %shard_map.131 = (f32[512,1024]{1,0:T(8,128)S(1)}, f32[8,128,128]{2,1,0:T(8,128)S(1)}, bf16[8,128,512]{2,1,0:T(8,128)(2,1)S(1)}) custom-call(s32[2]{0:T(128)S(1)} %pad_add_fusion.meta, bf16[512,2048]{1,0:T(8,128)(2,1)S(1)} %copy-done, bf16[512,2048]{1,0:T(8,128)(2,1)S(1)} %copy-done.6, bf16[512,2048]{1,0:T(8,128)(2,1)S(1)} %copy-done.7), custom_call_target="tpu_custom_call" | custom-call | flops 603979776 | bytes 9961472 | tf_op jit(solution)/shard_map/pallas_call | solution.py:202
  53.9 0.0 copy-done.1
  53.9 0.0 copy-done.8
  53.9 2.7 %shard_map.132 = (f32[512,1024]{1,0:T(8,128)S(1)}, bf16[8,2,128,128]{3,2,1,0:T(8,128)(2,1)S(1)}, f32[2,512]{1,0:T(2,128)S(1)}) custom-call(s32[2]{0:T(128)S(1)} %pad_add_fusion.meta, bf16[512,2048]{1,0:T(8,128)(2,1)S(1)} %copy-done, f32[512,1024]{1,0:T(8,128)S(1)} %get-tuple-element.38.intra_ref, f32[8,128,128]{2,1,0:T(8,128)S(1)} %bitcast.9, ...), custom_call_target="tpu_custom_call" | custom-call | flops 134217728 | bytes 9973760 | tf_op jit(solution)/shard_map/pallas_call | solution.py:202
  56.6 0.0 collective-permute-done.1.s_ref
  56.6 2.7 %shard_map.133 = (f32[512,1024]{1,0:T(8,128)S(1)}, bf16[8,2,128,128]{3,2,1,0:T(8,128)(2,1)S(1)}, f32[2,512]{1,0:T(2,128)S(1)}) custom-call(s32[2]{0:T(128)S(1)} %pad_add_fusion.meta, bf16[512,2048]{1,0:T(8,128)(2,1)S(1)} %copy-done, f32[512,1024]{1,0:T(8,128)S(1)} %get-tuple-element.36.intra_ref, f32[8,128,128]{2,1,0:T(8,128)S(1)} %collective-permute-done.1.s_ref, ...), custom_call_target="tpu_custom_call" | custom-call | flops 134217728 | bytes 9977856 | tf_op jit(solution)/shard_map/pallas_call | solution.py:202
  59.3 1.3 %collective-permute-start.2 = (f32[2,512]{1,0:T(2,128)S(1)}, f32[2,512]{1,0:T(2,128)S(1)}, u32[]{:S(2)}, u32[]{:S(2)}) collective-permute-start(f32[2,512]{1,0:T(2,128)S(1)} %get-tuple-element.44.rest_0_), channel_id=1, source_target_pairs={{0,32},{32,64},{64,96},{96,0},{1,33},{33,65},{65,97},{97,1},{2,34}... | collective-permute-start | bytes 12296 | tf_op jit(solution)/shard_map/ppermute | solution.py:295
  60.5 2.4 %collective-permute-start.3 = (f32[2,512]{1,0:T(2,128)S(1)}, f32[2,512]{1,0:T(2,128)S(1)}, u32[]{:S(2)}, u32[]{:S(2)}) collective-permute-start(f32[2,512]{1,0:T(2,128)S(1)} %get-tuple-element.44.rest_0_), channel_id=1, source_target_pairs={{0,64},{32,96},{64,0},{96,32},{1,65},{33,97},{65,1},{97,33},{2,66}... | collective-permute-start | bytes 12296 | tf_op jit(solution)/shard_map/ppermute | solution.py:295
  63.0 1.2 collective-permute-start.4
  64.1 0.0 collective-permute-done.2.rest_1_
  64.1 0.4 collective-permute-done.3.rest_2_
  64.5 1.1 collective-permute-done.4.rest_3_
  65.6 2.5 %shard_map.134 = (f32[8,128,128]{2,1,0:T(8,128)S(1)}, bf16[8,128,128]{2,1,0:T(8,128)(2,1)S(1)}, f32[512,128]{1,0:T(8,128)S(1)}, f32[512,128]{1,0:T(8,128)S(1)}) custom-call(s32[2]{0:T(128)S(1)} %pad_add_fusion.meta, bf16[512,2048]{1,0:T(8,128)(2,1)S(1)} %copy-done.1, f32[512,1024]{1,0:T(8,128)S(1)} %get-tuple-element.41.o_ref, f32[1,2048]{1,0:T(1,128)S(1)} %bitcast.12, ...), custom_call_target="tpu_custom_call" | custom-call | flops 134217728 | bytes 6578176 | tf_op jit(solution)/shard_map/pallas_call | solution.py:202
  68.0 1.7 %collective-permute-start.5 = (f32[8,128,128]{2,1,0:T(8,128)S(1)}, f32[8,128,128]{2,1,0:T(8,128)S(1)}, u32[]{:S(2)}, u32[]{:S(2)}) collective-permute-start(f32[8,128,128]{2,1,0:T(8,128)S(1)} %get-tuple-element.61), channel_id=1, source_target_pairs={{0,1},{1,0},{2,3},{3,2},{4,5},{5,4},{6,7},{7,6},{8,9},{9,8},{10,11... | collective-permute-start | bytes 1572872 | tf_op jit(solution)/shard_map/ppermute | solution.py:236
  69.7 2.3 %shard_map.135 = (f32[8,128,128]{2,1,0:T(8,128)S(1)}, bf16[8,128,128]{2,1,0:T(8,128)(2,1)S(1)}) custom-call(s32[2]{0:T(128)S(1)} %pad_add_fusion.meta, bf16[512,2048]{1,0:T(8,128)(2,1)S(1)} %copy-done.1, f32[512,1024]{1,0:T(8,128)S(1)} %get-tuple-element.48.o_ref, f32[1,2048]{1,0:T(1,128)S(1)} %bitcast.13, ...), custom_call_target="tpu_custom_call" | custom-call | flops 134217728 | bytes 6561792 | tf_op jit(solution)/shard_map/pallas_call | solution.py:202
  72.0 0.0 collective-permute-done.5
  72.0 0.1 add.12
  72.1 13.1 %all_to_all.22.pieces_ref = f32[16,64,128]{2,1,0:T(8,128)S(1)} all-to-all(f32[16,64,128]{2,1,0:T(8,128)S(1)} %bitcast.17), channel_id=1, replica_groups={{0,2,4,6,8,10,12,14,16,18,20,22,24,26,28,30},{1,3,5,7,9,11,13,15,17,19,..., dimensions={0} | all-to-all | bytes 1048576 | tf_op jit(solution)/shard_map/all_to_all | solution.py:224
  85.2 0.1 shard_map.138
  85.2 13.2 %all_to_all.23 = f32[16,64,128]{2,1,0:T(8,128)S(1)} all-to-all(f32[16,64,128]{2,1,0:T(8,128)S(1)} %shard_map.138), channel_id=1, replica_groups={{0,2,4,6,8,10,12,14,16,18,20,22,24,26,28,30},{1,3,5,7,9,11,13,15,17,19,..., dimensions={0} | all-to-all | bytes 1048576 | tf_op jit(solution)/shard_map/all_to_all | solution.py:224
  98.4 3.4 %collective-permute-start.6 = (f32[8,128,128]{2,1,0:T(8,128)S(1)}, f32[8,128,128]{2,1,0:T(8,128)S(1)}, u32[]{:S(2)}, u32[]{:S(2)}) collective-permute-start(f32[8,128,128]{2,1,0:T(8,128)S(1)} %bitcast.6), channel_id=1, source_target_pairs={{0,1},{1,0},{2,3},{3,2},{4,5},{5,4},{6,7},{7,6},{8,9},{9,8},{10,11... | collective-permute-start | bytes 1572872 | tf_op jit(solution)/shard_map/ppermute | solution.py:239
  101.9 7.6 %shard_map.136 = (bf16[512,2048]{1,0:T(8,128)(2,1)}, bf16[512,2048]{1,0:T(8,128)(2,1)}, bf16[512,2048]{1,0:T(8,128)(2,1)}, bf16[512,2048]{1,0:T(8,128)(2,1)}) custom-call(s32[2]{0:T(128)S(1)} %pad_add_fusion.meta, bf16[512,2048]{1,0:T(8,128)(2,1)S(1)} %copy-done, bf16[512,2048]{1,0:T(8,128)(2,1)S(1)} %copy-done.6, bf16[512,2048]{1,0:T(8,128)(2,1)S(1)} %copy-done.7, ...), custom_call_target="tpu_custom_call" | custom-call | flops 2147483648 | bytes 20193280 | tf_op jit(solution)/shard_map/pallas_call | solution.py:202
  109.5 7.6 %shard_map.137 = (bf16[512,2048]{1,0:T(8,128)(2,1)}, bf16[512,2048]{1,0:T(8,128)(2,1)}, bf16[512,2048]{1,0:T(8,128)(2,1)}, bf16[512,2048]{1,0:T(8,128)(2,1)}) custom-call(s32[2]{0:T(128)S(1)} %pad_add_fusion.meta, bf16[512,2048]{1,0:T(8,128)(2,1)S(1)} %copy-done, ...), custom_call_target="tpu_custom_call", output_to_operand_aliasing={{0}: (11, {}), {1}: (12, {}), {2}: (13, {}), {3}: (14, {})} | custom-call | flops 2147483648 | bytes 20193280 | tf_op jit(solution)/shard_map/pallas_call | solution.py:202
  117.1 0.0 copy-done.3
  117.1 0.0 copy-done.5
  117.1 3.8 %shard_map.139 = (bf16[512,2048]{1,0:T(8,128)(2,1)}, bf16[512,2048]{1,0:T(8,128)(2,1)}) custom-call(s32[2]{0:T(128)S(1)} %pad_add_fusion.meta, bf16[512,2048]{1,0:T(8,128)(2,1)S(1)} %copy-done.3, bf16[512,2048]{1,0:T(8,128)(2,1)S(1)} %copy-done.5, f32[8,128,128]{2,1,0:T(8,128)S(1)} %bitcast.7), custom_call_target="tpu_custom_call" | custom-call | flops 536870912 | bytes 8912896 | tf_op jit(solution)/shard_map/pallas_call | solution.py:202
  120.9 0.0 collective-permute-done.6.ds_ref
  120.9 3.8 %shard_map.140 = (bf16[512,2048]{1,0:T(8,128)(2,1)}, bf16[512,2048]{1,0:T(8,128)(2,1)}) custom-call(s32[2]{0:T(128)S(1)} %pad_add_fusion.meta, bf16[512,2048]{1,0:T(8,128)(2,1)S(1)} %copy-done.3, bf16[512,2048]{1,0:T(8,128)(2,1)S(1)} %copy-done.5, f32[8,128,128]{2,1,0:T(8,128)S(1)} %collective-permute-done.6.ds_ref, ...), custom_call_target="tpu_custom_call", output_to_operand_aliasing={{0}: (4, {}), {1}: (5, {})} | custom-call | flops 536870912 | bytes 8912896 | tf_op jit(solution)/shard_map/pallas_call | solution.py:202
  (5 shorter events, 0.0 us)
Async XLA Ops:
  1.4 1.6 %copy-start.2 = (bf16[512,2048]{1,0:T(8,128)(2,1)S(1)}, bf16[512,2048]{1,0:T(8,128)(2,1)}, u32[]{:S(2)}) copy-start(bf16[512,2048]{1,0:T(8,128)(2,1)} %k_ref.15) | copy-start | bytes 6291460
  3.0 1.6 %copy-start.4 = (bf16[512,2048]{1,0:T(8,128)(2,1)S(1)}, bf16[512,2048]{1,0:T(8,128)(2,1)}, u32[]{:S(2)}) copy-start(bf16[512,2048]{1,0:T(8,128)(2,1)} %v_ref.15) | copy-start | bytes 6291460
  6.6 3.6 %collective-permute-start = (f32[8,128,128]{2,1,0:T(8,128)S(1)}, f32[8,128,128]{2,1,0:T(8,128)S(1)}, u32[]{:S(2)}, u32[]{:S(2)}) collective-permute-start(f32[8,128,128]{2,1,0:T(8,128)S(1)} %shard_map.129), channel_id=1, source_target_pairs={{0,1},{1,0},{2,3},{3,2},{4,5},{5,4},{6,7},{7,6},{8,9},{9,8},{10,11... | collective-permute-start | bytes 1572872 | tf_op jit(solution)/shard_map/ppermute | solution.py:236
  8.1 36.9 %copy-start.7 = (bf16[512,2048]{1,0:T(8,128)(2,1)S(1)}, bf16[512,2048]{1,0:T(8,128)(2,1)}, u32[]{:S(2)}) copy-start(bf16[512,2048]{1,0:T(8,128)(2,1)} %v_ref.13) | copy-start | bytes 6291460
  10.2 34.8 %copy-start = (bf16[512,2048]{1,0:T(8,128)(2,1)S(1)}, bf16[512,2048]{1,0:T(8,128)(2,1)}, u32[]{:S(2)}) copy-start(bf16[512,2048]{1,0:T(8,128)(2,1)} %q_ref.11) | copy-start | bytes 6291460
  10.2 34.8 %copy-start.6 = (bf16[512,2048]{1,0:T(8,128)(2,1)S(1)}, bf16[512,2048]{1,0:T(8,128)(2,1)}, u32[]{:S(2)}) copy-start(bf16[512,2048]{1,0:T(8,128)(2,1)} %k_ref.13) | copy-start | bytes 6291460
  41.6 15.0 %collective-permute-start.1 = (f32[8,128,128]{2,1,0:T(8,128)S(1)}, f32[8,128,128]{2,1,0:T(8,128)S(1)}, u32[]{:S(2)}, u32[]{:S(2)}) collective-permute-start(f32[8,128,128]{2,1,0:T(8,128)S(1)} %bitcast.8), channel_id=1, source_target_pairs={{0,1},{1,0},{2,3},{3,2},{4,5},{5,4},{6,7},{7,6},{8,9},{9,8},{10,11... | collective-permute-start | bytes 1572872 | tf_op jit(solution)/shard_map/ppermute | solution.py:239
  49.4 4.4 %copy-start.1 = (bf16[512,2048]{1,0:T(8,128)(2,1)S(1)}, bf16[512,2048]{1,0:T(8,128)(2,1)}, u32[]{:S(2)}) copy-start(bf16[512,2048]{1,0:T(8,128)(2,1)} %dy_ref.11) | copy-start | bytes 6291460
  49.4 4.4 %copy-start.8 = (f32[2048]{0:T(1024)S(1)}, f32[2048]{0:T(1024)}, u32[]{:S(2)}) copy-start(f32[2048]{0:T(1024)} %param.14) | copy-start | bytes 24580
  59.3 4.9 %collective-permute-start.2 = (f32[2,512]{1,0:T(2,128)S(1)}, f32[2,512]{1,0:T(2,128)S(1)}, u32[]{:S(2)}, u32[]{:S(2)}) collective-permute-start(f32[2,512]{1,0:T(2,128)S(1)} %get-tuple-element.44.rest_0_), channel_id=1, source_target_pairs={{0,32},{32,64},{64,96},{96,0},{1,33},{33,65},{65,97},{97,1},{2,34}... | collective-permute-start | bytes 12296 | tf_op jit(solution)/shard_map/ppermute | solution.py:295
  60.5 4.0 %collective-permute-start.3 = (f32[2,512]{1,0:T(2,128)S(1)}, f32[2,512]{1,0:T(2,128)S(1)}, u32[]{:S(2)}, u32[]{:S(2)}) collective-permute-start(f32[2,512]{1,0:T(2,128)S(1)} %get-tuple-element.44.rest_0_), channel_id=1, source_target_pairs={{0,64},{32,96},{64,0},{96,32},{1,65},{33,97},{65,1},{97,33},{2,66}... | collective-permute-start | bytes 12296 | tf_op jit(solution)/shard_map/ppermute | solution.py:295
  63.0 2.6 %collective-permute-start.4 = (f32[2,512]{1,0:T(2,128)S(1)}, f32[2,512]{1,0:T(2,128)S(1)}, u32[]{:S(2)}, u32[]{:S(2)}) collective-permute-start(f32[2,512]{1,0:T(2,128)S(1)} %get-tuple-element.44.rest_0_), channel_id=1, source_target_pairs={{0,96},{32,0},{64,32},{96,64},{1,97},{33,1},{65,33},{97,65},{2,98}... | collective-permute-start | bytes 12296 | tf_op jit(solution)/shard_map/ppermute | solution.py:295
  68.0 4.0 %collective-permute-start.5 = (f32[8,128,128]{2,1,0:T(8,128)S(1)}, f32[8,128,128]{2,1,0:T(8,128)S(1)}, u32[]{:S(2)}, u32[]{:S(2)}) collective-permute-start(f32[8,128,128]{2,1,0:T(8,128)S(1)} %get-tuple-element.61), channel_id=1, source_target_pairs={{0,1},{1,0},{2,3},{3,2},{4,5},{5,4},{6,7},{7,6},{8,9},{9,8},{10,11... | collective-permute-start | bytes 1572872 | tf_op jit(solution)/shard_map/ppermute | solution.py:236
  98.4 22.5 %collective-permute-start.6 = (f32[8,128,128]{2,1,0:T(8,128)S(1)}, f32[8,128,128]{2,1,0:T(8,128)S(1)}, u32[]{:S(2)}, u32[]{:S(2)}) collective-permute-start(f32[8,128,128]{2,1,0:T(8,128)S(1)} %bitcast.6), channel_id=1, source_target_pairs={{0,1},{1,0},{2,3},{3,2},{4,5},{5,4},{6,7},{7,6},{8,9},{9,8},{10,11... | collective-permute-start | bytes 1572872 | tf_op jit(solution)/shard_map/ppermute | solution.py:239
  109.5 7.6 %copy-start.3 = (bf16[512,2048]{1,0:T(8,128)(2,1)S(1)}, bf16[512,2048]{1,0:T(8,128)(2,1)}, u32[]{:S(2)}) copy-start(bf16[512,2048]{1,0:T(8,128)(2,1)} %k_ref.15) | copy-start | bytes 6291460
  109.5 7.6 %copy-start.5 = (bf16[512,2048]{1,0:T(8,128)(2,1)S(1)}, bf16[512,2048]{1,0:T(8,128)(2,1)}, u32[]{:S(2)}) copy-start(bf16[512,2048]{1,0:T(8,128)(2,1)} %v_ref.15) | copy-start | bytes 6291460

commit v3 on v0

v3 whole, which is shorter than its diff:
```python
import functools

import jax
import jax.numpy as jnp
from jax import lax
from jax.experimental import pallas as pl
from jax.experimental.pallas import tpu as pltpu
from jax.sharding import PartitionSpec as P

H = 64
HEAD_DIM = 128
BLOCK = 256
WIDTH = H * HEAD_DIM
EPSILON = 1e-06

GROUP = 2
SLAB = GROUP * HEAD_DIM
MIB = 1024 * 1024

F32 = jnp.float32
BF16 = jnp.bfloat16


def dot_nn(a, b):
    return lax.dot_general(a, b, (((1,), (0,)), ((), ())), preferred_element_type=F32)


def dot_nt(a, b):
    return lax.dot_general(a, b, (((1,), (1,)), ((), ())), preferred_element_type=F32)


def dot_tn(a, b):
    return lax.dot_general(a, b, (((0,), (0,)), ((), ())), preferred_element_type=F32)


def lanes(head):
    return slice(head * HEAD_DIM, (head + 1) * HEAD_DIM)


def rows(block):
    return slice(block * BLOCK, (block + 1) * BLOCK)


def block_mask(upper):
    row = lax.broadcasted_iota(jnp.int32, (BLOCK, BLOCK), 0)
    column = lax.broadcasted_iota(jnp.int32, (BLOCK, BLOCK), 1)
    return column >= row if upper else row >= column


class Slabs:
    def __init__(self, ref, buffers, semaphores, other, out=False):
        core = lax.axis_index("seq") % 2
        self.half = 1 - core if other else core
        self.ref, self.buffers, self.semaphores, self.out = ref, buffers, semaphores, out

    def copy(self, g):
        if len(self.ref.shape) == 2:
            start = pl.multiple_of(self.half * (self.buffers.shape[0] * SLAB) + g * SLAB, SLAB)
            there = self.ref.at[:, pl.ds(start, SLAB)]
        else:
            there = self.ref.at[pl.ds(g * GROUP, GROUP)]
        here = self.buffers.at[g]
        source, target = (here, there) if self.out else (there, here)
        return pltpu.make_async_copy(source, target, self.semaphores.at[g])

    def __getitem__(self, index):
        return self.buffers[index]

    def __setitem__(self, index, value):
        self.buffers[index] = value


def buffer_shape(shape):
    if len(shape) == 2:
        return (shape[1] // 2 // SLAB, shape[0], SLAB)
    return (shape[0] // GROUP, GROUP) + tuple(shape[1:])


def streamed(kernel, other, half, ins, outs, late, rest, groups):
    for g in range(groups):
        for slab in ins:
            slab.copy(g).start()
    for g in range(groups):
        for slab in late:
            slab.copy(g).start()
    steps = kernel(half, ins, outs, rest)
    step = next(steps)

    def one(g, carry):
        for slab in ins:
            slab.copy(g).wait()
        step(g)
        for slab in outs:
            slab.copy(g).start()
        return carry

    lax.fori_loop(0, groups, one, 0)
    for _ in steps:
        pass
    for g in range(groups):
        for slab in (*outs, *late):
            slab.copy(g).wait()


def prefix_state_kernel(half, ins, outs, rest):
    k, v = ins
    (s_ref,) = rest

    def step(g):
        for h in range(GROUP):
            s_ref[g * GROUP + h] = dot_tn(k[g, :, lanes(h)], v[g, :, lanes(h)])

    yield step


def intra_kernel(half, ins, outs, rest):
    o_all, kv_all, qt_all = outs
    lower = block_mask(False)

    def step(g):
        for h in range(GROUP):
            for b in range(2):
                q, k, v = (slab[g, rows(b), lanes(h)] for slab in ins)
                scores = jnp.where(lower, dot_nt(q, k), 0.0).astype(BF16)
                o_all[g, h, rows(b)] = dot_nn(scores, v)
                if b == 0:
                    kv_all[g, h] = dot_tn(k, v)
            qt_all[g, h] = ins[0][g, :, lanes(h)].T

    yield step


def spread_sum_kernel(pieces_ref, out_ref):
    total = jnp.sum(pieces_ref[...], axis=0)
    for i in range(out_ref.shape[0]):
        out_ref[i] = total


def forward_kernel(half, ins, outs, rest):
    q, dy, intra, kv = ins
    (m_all,) = outs
    s_ref, gain_ref, *before = rest[:-4]
    o_ref, stats_ref, square_acc, inner_acc = rest[-4:]
    heads = o_ref.shape[0]
    square_acc[...] = jnp.zeros_like(square_acc)
    inner_acc[...] = jnp.zeros_like(inner_acc)

    def step(g):
        for b in range(2):
            square = inner = 0.0
            for h in range(GROUP):
                head = g * GROUP + h
                state = s_ref[head] if b == 0 else s_ref[head] + kv[g, h]
                m = state.astype(BF16)
                m_all[g, h, b] = m
                o = intra[g, h, rows(b)] + dot_nn(q[g, rows(b), lanes(h)], m)
                o_ref[head, rows(b)] = o
                gain = gain_ref[half * heads + head]
                square = square + o * o
                inner = inner + gain * dy[g, rows(b), lanes(h)].astype(F32) * o
            square_acc[rows(b)] += square
            inner_acc[rows(b)] += inner

    yield step
    for i, acc in enumerate((square_acc, inner_acc)):
        row = jnp.sum(acc[...].T, axis=0, keepdims=True)
        if before:
            row = row + before[0][i : i + 1]
        stats_ref[i : i + 1] = row


def state_grad_kernel(first, half, ins, outs, rest):
    (g_all,) = outs
    dy_ref, o_ref, gain_ref, qt_ref, *rest = rest
    if first:
        length_ref, *stats, ds_ref, inv_ref, coef_ref = rest
        total = sum(ref[...] for ref in stats[1:]) + stats[0][...]
        inv = 1.0 / jnp.sqrt(total[0:1] / WIDTH + EPSILON)
        coef = total[1:2] * (inv * inv * inv) / WIDTH
        live = lax.broadcasted_iota(jnp.int32, inv.shape, 1) < length_ref[0]
        for value, ref in ((inv, inv_ref), (coef, coef_ref)):
            value = jnp.where(live, value, 0.0)
            for n in range(value.shape[1] // HEAD_DIM):
                square = jnp.broadcast_to(value[:, lanes(n)], (HEAD_DIM, HEAD_DIM))
                ref[n * HEAD_DIM : (n + 1) * HEAD_DIM] = square.T
    else:
        inv_ref, coef_ref, ds_ref = rest
    heads = o_ref.shape[0]

    def step(g):
        for h in range(GROUP):
            head = g * GROUP + h
            scaled = gain_ref[half * heads + head] * dy_ref[g, :, lanes(h)].astype(F32)
            do = (scaled * inv_ref[...] - o_ref[head] * coef_ref[...]).astype(BF16)
            later = dot_nn(qt_ref[g, h, :, rows(1)], do[rows(1)])
            ds_ref[head] = later + dot_nn(qt_ref[g, h, :, rows(0)], do[rows(0)])
            g_all[g, h] = later.astype(BF16)

    yield step


def backward_kernel(half, ins, outs, rest):
    q_all, k_all, v_all, dy, o_all, m_all, g_all = ins
    normed, dq_all, dk_all, dv_all = outs
    gain_ref, inv_ref, coef_ref = rest[:3]
    heads = gain_ref.shape[0] // 2
    lower, upper = block_mask(False), block_mask(True)

    def step(g):
        for h in range(GROUP):
            o = o_all[g, h]
            gain = gain_ref[half * heads + g * GROUP + h]
            normed[g, :, lanes(h)] = (gain * o * inv_ref[...]).astype(BF16)
            scaled = gain * dy[g, :, lanes(h)].astype(F32)
            do_all = (scaled * inv_ref[...] - o * coef_ref[...]).astype(BF16)
            later = g_all[g, h]
            for b in range(2):
                q, k, v = (slab[g, rows(b), lanes(h)] for slab in (q_all, k_all, v_all))
                do = do_all[rows(b)]
                p = jnp.where(lower, dot_nt(do, v), 0.0).astype(BF16)
                p_t = jnp.where(upper, dot_nt(v, do), 0.0).astype(BF16)
                scores_t = jnp.where(upper, dot_nt(k, q), 0.0).astype(BF16)
                dq = dot_nt(do, m_all[g, h, b]) + dot_nn(p, k)
                dk = dot_nn(p_t, q)
                dv = dot_nn(scores_t, do)
                if b == 0:
                    dk = dk + dot_nt(v, later)
                    dv = dv + dot_nn(k, later)
                for slab, value in ((dq_all, dq), (dk_all, dk), (dv_all, dv)):
                    slab[g, rows(b), lanes(h)] = value.astype(BF16)

    yield step


def prefix_grad_kernel(half, ins, outs, rest):
    dk, dv = outs
    k_ref, v_ref, ds_ref = rest[:3]

    def step(g):
        for h in range(GROUP):
            ds = ds_ref[g * GROUP + h]
            high = ds.astype(BF16)
            low = (ds - high.astype(F32)).astype(BF16)
            k, v = k_ref[g, :, lanes(h)], v_ref[g, :, lanes(h)]
            dk[g, :, lanes(h)] = dot_nt(
                jnp.concatenate([v, v], 1), jnp.concatenate([high, low], 1)
            ).astype(BF16)
            dv[g, :, lanes(h)] = dot_nn(
                jnp.concatenate([k, k], 1), jnp.concatenate([high, low], 0)
            ).astype(BF16)

    yield step


HBM = pl.BlockSpec(memory_space=pltpu.HBM)
VMEM = pl.BlockSpec(memory_space=pltpu.VMEM)
SMEM = pl.BlockSpec(memory_space=pltpu.SMEM)


def in_hbm(array):
    return pltpu.with_memory_space_constraint(array, pltpu.HBM)


def in_vmem(array):
    return pltpu.with_memory_space_constraint(array, pltpu.VMEM)


def body(queries, keys, values, cotangent, prefix_keys, prefix_values, gain, lengths):
    tok_rows, tok_cols = queries.shape
    half = tok_cols // HEAD_DIM // 2
    seq_size = lax.axis_size("seq")
    head_size = lax.axis_size("head")
    chips = seq_size // 2
    swap = [(i, i ^ 1) for i in range(seq_size)]
    chip_groups = [list(range(c, seq_size, 2)) for c in range(2)]
    gains = gain.reshape(2 * half, 1, HEAD_DIM)
    OWN, OTHER = False, True

    def call(kernel, other, streams, held, outs, out_streams, flops, scratch=(), aliased=(), late=(), keep=()):
        n_in, n_out, n_late = len(streams), len(out_streams), len(late)
        fetched = [*streams, *(a for a, _ in late)]
        kept = [pltpu.VMEM(buffer_shape(streams[i].shape), streams[i].dtype) for i in keep]
        kept += [pltpu.VMEM(buffer_shape(a.shape), a.dtype) for a, _ in late]
        in_scratch = [i for i in range(n_in) if i not in keep]
        buffers = [pltpu.VMEM(buffer_shape(streams[i].shape), streams[i].dtype) for i in in_scratch]
        buffers += [pltpu.VMEM(buffer_shape(s), d) for s, d in out_streams]
        results = [pltpu.VMEM(s, d) for s, d in outs] + kept
        results += [pltpu.HBM(s, d) for s, d in out_streams]
        groups = half // GROUP
        size = sum(a.size * a.dtype.itemsize for a in (*fetched, *held))

        def run(*refs):
            refs = list(refs)

            def take(count):
                taken = refs[:count]
                del refs[:count]
                return taken

            sources, late_sources, held_refs, _ = (
                take(n) for n in (n_in, n_late, len(held), len(aliased))
            )
            out_refs, kept_refs, late_buffers, targets = (
                take(n) for n in (len(outs), len(keep), n_late, n_out)
            )
            scratch_refs, loose, out_buffers = (
                take(n) for n in (len(scratch), len(in_scratch), n_out)
            )
            (sems,) = refs
            in_buffers = dict(zip(keep, kept_refs)) | dict(zip(in_scratch, loose))
            ins = [Slabs(sources[i], in_buffers[i], sems.at[i], other) for i in range(n_in)]
            brought = [
                Slabs(late_sources[i], late_buffers[i], sems.at[n_in + i], late[i][1])
                for i in range(n_late)
            ]
            written = [
                Slabs(targets[i], out_buffers[i], sems.at[n_in + n_late + i], other, True)
                for i in range(n_out)
            ]
            core = lax.axis_index("seq") % 2
            rest = [*held_refs, *out_refs, *scratch_refs]
            streamed(kernel, other, 1 - core if other else core, ins, written, brought, rest, groups)

        integer = [jnp.issubdtype(a.dtype, jnp.integer) for a in held]
        first_aliased = len(fetched) + len(held)
        return pl.pallas_call(
            run,
            in_specs=[HBM] * len(fetched)
            + [SMEM if i else VMEM for i in integer]
            + [HBM] * len(aliased),
            out_specs=[VMEM] * (len(outs) + len(kept)) + [HBM] * n_out,
            out_shape=results,
            scratch_shapes=[
                *scratch,
                *buffers,
                pltpu.SemaphoreType.DMA((n_in + n_late + n_out, groups)),
            ],
            input_output_aliases={
                first_aliased + i: len(outs) + len(kept) + i for i in range(len(aliased))
            },
            cost_estimate=pl.CostEstimate(flops=flops, bytes_accessed=size, transcendentals=0),
            compiler_params=pltpu.CompilerParams(vmem_limit_bytes=VMEM_LIMIT),
        )(
            *(in_hbm(a) for a in fetched),
            *(a if i else in_vmem(a) for a, i in zip(held, integer)),
            *(in_hbm(a) for a in aliased),
        )

    square = HEAD_DIM * HEAD_DIM
    states = (half, HEAD_DIM, HEAD_DIM)
    tokens = (half, tok_rows, HEAD_DIM)
    scalar = (tok_rows, HEAD_DIM)
    unit = 2 * half * tok_rows * square

    def exchange(value):
        return lax.all_to_all(value, "seq", 0, 0, axis_index_groups=chip_groups, tiled=True)

    def spread_sum(pieces):
        return pl.pallas_call(
            spread_sum_kernel,
            in_specs=[VMEM],
            out_specs=VMEM,
            out_shape=jax.ShapeDtypeStruct(pieces.shape, F32),
            compiler_params=pltpu.CompilerParams(vmem_limit_bytes=VMEM_LIMIT),
        )(pieces)

    def sum_over_seq(mine, theirs, beside_sum, beside_gather):
        paired = mine + lax.ppermute(theirs, "seq", swap)
        pieces = exchange(paired.reshape(chips, -1, HEAD_DIM))
        pieces, first = lax.optimization_barrier((pieces, beside_sum()))
        gathered = exchange(spread_sum(pieces)).reshape(states)
        gathered, second = lax.optimization_barrier((gathered, beside_gather(first)))
        return gathered, lax.ppermute(gathered, "seq", swap), first, second

    def prefix_state(other):
        return call(
            prefix_state_kernel, other, [prefix_keys, prefix_values], [], [(states, F32)], [], unit
        )[0]

    def intra_of(other):
        outs = [(tokens, F32), (states, F32), ((half, HEAD_DIM, tok_rows), BF16)]
        return call(intra_kernel, other, [queries, keys, values], [], [], outs, 9 * unit // 2)

    theirs = prefix_state(OTHER)
    mine = prefix_state(OWN)
    *sums, intra_own, intra_other = sum_over_seq(
        mine, theirs, lambda: intra_of(OWN), lambda _: intra_of(OTHER)
    )

    forward = []
    for other, total, (o, kv, qt) in ((OWN, sums[0], intra_own), (OTHER, sums[1], intra_other)):
        forward.append(
            call(
                forward_kernel,
                other,
                [queries, cotangent, o, kv],
                [total, gains] + [f[1] for f in forward],
                [(tokens, F32), ((2, tok_rows), F32)],
                [((half, 2, HEAD_DIM, HEAD_DIM), BF16)],
                unit,
                scratch=[pltpu.VMEM(scalar, F32)] * 2,
                keep=[1],
                late=[(qt, other)],
            )
        )
    stats = forward[1][1]
    all_stats = [stats] + [
        lax.ppermute(stats, "head", [(i, (i + k) % head_size) for i in range(head_size)])
        for k in range(1, head_size)
    ]

    def state_grad(i, other, scalars):
        o, _, dy, qt, _ = forward[i]
        first = len(scalars) > 2
        outs = [(states, F32)] + [(scalar, F32), (scalar, F32)] * first
        kernel = functools.partial(state_grad_kernel, first)
        held = [dy, o, gains, qt, *scalars]
        return call(kernel, other, [], held, outs, [(states, BF16)], unit)

    theirs, inv, coef, later_other = state_grad(1, OTHER, [lengths, *all_stats])
    mine, later_own = state_grad(0, OWN, [inv, coef])

    def backward_of(i, other, later, before=(), late=()):
        o, _, _, _, m = forward[i]
        return call(
            backward_kernel,
            other,
            [queries, keys, values, cotangent, o, m, later],
            [gains, inv, coef],
            [],
            [(queries.shape, BF16)] * 4,
            16 * unit,
            aliased=before,
            late=late,
        )

    *sums, _, (pre_k, pre_v, *grads) = sum_over_seq(
        mine,
        theirs,
        lambda: backward_of(0, OWN, later_own),
        lambda before: backward_of(
            1, OTHER, later_other, before, [(prefix_keys, OWN), (prefix_values, OWN)]
        ),
    )

    def prefix_grad(other, k, v, total, before=(), late=()):
        return call(
            prefix_grad_kernel,
            other,
            [],
            [k, v, total],
            [],
            [(prefix_keys.shape, BF16)] * 2,
            4 * unit,
            aliased=before,
            late=late,
        )

    pre_k, pre_v, *prefix_grads = prefix_grad(
        OWN, pre_k, pre_v, sums[0], late=[(prefix_keys, OTHER), (prefix_values, OTHER)]
    )
    prefix_grads = prefix_grad(OTHER, pre_k, pre_v, sums[1], prefix_grads)
    return (*grads, *prefix_grads)


VMEM_LIMIT = 14 * MIB


def solution(mesh):
    spread = P("seq", "head")
    return jax.shard_map(
        body,
        mesh=mesh,
        in_specs=(spread,) * 6 + (P("head"), P("seq")),
        out_specs=(spread,) * 6,
        check_vma=False,
    )
```

time: 294 us -> 103 us (0.35)
  waiting for transfers between devices: 152 us -> 14.9 us
  local copies, waits for them, and re-layouts: 53.5 us -> 2.21 us
  matrix products: 50 us -> 0 us
  Pallas kernels: 0 us -> 47.8 us
  starting transfers between devices: 0.08 us -> 33.8 us
  between operations: 15 us -> 1.49 us
  other arithmetic: 13.6 us -> 1.71 us
  blocking collectives: 8.75 us -> 0 us
    psum x2 -> x0, waiting for transfers between devices: 152 us -> none  [the longest x1 77.5 us: summed_prefix(): return lax.psum(partial_state, 'seq')]
    dot_general x26 -> x0, matrix products: 50 us -> none  [the longest x2 6.21 us: intra_block(): jnp.einsum('hbs,she->bhe', scores, v_block, preferred_element_type=jnp.fl...]
    unnamed x82 -> x10, local copies, waits for them, and re-layouts: 52 us -> 2.21 us
    pallas_call x0 -> x14, Pallas kernels: none -> 47.8 us  [the longest x12 46.1 us: call(): pl.pallas_call(run, in_specs=[HBM] * len(fetched) + [SMEM if i else VMEM...]
    all_to_all x0 -> x4, starting transfers between devices: none -> 19.8 us  [exchange(): lax.all_to_all(value, 'seq', 0, 0, axis_index_groups=chip_groups, tiled=T...]
    ppermute x0 -> x7, starting transfers between devices: none -> 14 us  [the longest x2 7.03 us: sum_over_seq(): return (gathered, lax.ppermute(gathered, 'seq', swap), first, second)]
    all_to_all x0 -> x4, waiting for transfers between devices: none -> 12.5 us  [exchange(): lax.all_to_all(value, 'seq', 0, 0, axis_index_groups=chip_groups, tiled=T...]
    psum x1 -> x0, blocking collectives: 8.75 us -> none  [body(): lax.psum((jnp.sum(attended * attended, axis=1), jnp.sum(scaled_cot * atte...]
  transfers between devices with their start and end apart: 2 -> 11, of which waited for: 2 -> 6; matrix products, arithmetic and copies ran while one was open for 19% -> 0% of each run, Pallas kernels for 0% -> 34%
where the time goes in v3:
time: 103 us; the launch traced here: 102 us
  Pallas kernels  47.8 us (46%)
  starting transfers between devices  33.8 us (33%)
  waiting for transfers between devices  14.9 us (14%)
  local copies, waits for them, and re-layouts  2.21 us (2%)
  other arithmetic  1.71 us (2%)
  between operations  1.49 us (1%)
    pallas_call x12, Pallas kernels, call(): pl.pallas_call(run, in_specs=[HBM] * len(fetched) + [SMEM if i else VMEM...  46.1 us
    all_to_all x4, starting transfers between devices, exchange(): lax.all_to_all(value, 'seq', 0, 0, axis_index_groups=chip_groups, tiled=T...  19.8 us
    all_to_all x4, waiting for transfers between devices, exchange(): lax.all_to_all(value, 'seq', 0, 0, axis_index_groups=chip_groups, tiled=T...  12.5 us
    ppermute x2, starting transfers between devices, sum_over_seq(): return (gathered, lax.ppermute(gathered, 'seq', swap), first, second)  7.03 us
    ppermute x3, starting transfers between devices, body(): lax.ppermute(stats, 'head', [(i, (i + k) % head_size) for i in range(head...  3.67 us
    ppermute x2, starting transfers between devices, sum_over_seq(): paired = mine + lax.ppermute(theirs, 'seq', swap)  3.3 us
    ppermute x3, waiting for transfers between devices, body(): lax.ppermute(stats, 'head', [(i, (i + k) % head_size) for i in range(head...  2.4 us
    unnamed x10, local copies, waits for them, and re-layouts  2.21 us
  transfers between devices with their start and end apart: 11, of which 6 were waited for; matrix products, arithmetic and copies ran while one was open for 0% of the time, Pallas kernels for 34%

profile of v3, /device:TPU:1, one launch (start us, length us, event | category | flops | bytes accessed | tf_op | source)
XLA Modules:
  0.0 101.9 jit_solution(15457072797170701030)
XLA Ops:
  0.6 2.2 %shard_map.128 = f32[8,128,128]{2,1,0:T(8,128)S(1)} custom-call(bf16[512,2048]{1,0:T(8,128)(2,1)} %refs_0_.17, bf16[512,2048]{1,0:T(8,128)(2,1)} %refs_1_.17), custom_call_target="tpu_custom_call" | custom-call | flops 134217728 | bytes 4194304 | tf_op jit(solution)/shard_map/pallas_call | solution.py:326
  2.9 1.5 %collective-permute-start = (f32[8,128,128]{2,1,0:T(8,128)S(1)}, f32[8,128,128]{2,1,0:T(8,128)S(1)}, u32[]{:S(2)}, u32[]{:S(2)}) collective-permute-start(f32[8,128,128]{2,1,0:T(8,128)S(1)} %shard_map.128), channel_id=1, source_target_pairs={{0,1},{1,0},{2,3},{3,2},{4,5},{5,4},{6,7},{7,6},{8,9},{9,8},{10,11... | collective-permute-start | bytes 1572872 | tf_op jit(solution)/shard_map/ppermute | solution.py:368
  4.4 2.2 %shard_map.127 = f32[8,128,128]{2,1,0:T(8,128)S(1)} custom-call(bf16[512,2048]{1,0:T(8,128)(2,1)} %refs_0_.17, bf16[512,2048]{1,0:T(8,128)(2,1)} %refs_1_.17), custom_call_target="tpu_custom_call" | custom-call | flops 134217728 | bytes 4194304 | tf_op jit(solution)/shard_map/pallas_call | solution.py:326
  6.6 0.0 collective-permute-done
  6.6 0.9 add.6
  7.4 7.9 %all-to-all-start = ((f32[16,64,128]{2,1,0:T(8,128)}), f32[16,64,128]{2,1,0:T(8,128)S(1)}, u32[]{:S(2)}, u32[]{:S(2)}) async-start(f32[16,64,128]{2,1,0:T(8,128)} %bitcast), calls=%async_computation | async-start | bytes 1048576 | tf_op jit(solution)/shard_map/all_to_all | solution.py:356
  15.3 5.0 %shard_map.129 = (f32[8,512,128]{2,1,0:T(8,128)}, f32[8,128,128]{2,1,0:T(8,128)}, bf16[8,128,512]{2,1,0:T(8,128)(2,1)}) custom-call(bf16[512,2048]{1,0:T(8,128)(2,1)} %refs_0_.16, bf16[512,2048]{1,0:T(8,128)(2,1)} %refs_1_.16, bf16[512,2048]{1,0:T(8,128)(2,1)} %refs_2_.7), custom_call_target="tpu_custom_call" | custom-call | flops 603979776 | bytes 6291456 | tf_op jit(solution)/shard_map/pallas_call | solution.py:326
  20.4 5.1 %all-to-all-done.pieces_ref = f32[16,64,128]{2,1,0:T(8,128)S(1)} async-done(((f32[16,64,128]{2,1,0:T(8,128)}), f32[16,64,128]{2,1,0:T(8,128)S(1)}, u32[]{:S(2)}, u32[]{:S(2)}) %all-to-all-start) | async-done | bytes 524320 | tf_op jit(solution)/shard_map/all_to_all | solution.py:356
  25.4 0.9 shard_map.130
  26.3 4.3 %all-to-all-start.1 = ((f32[16,64,128]{2,1,0:T(8,128)}), f32[16,64,128]{2,1,0:T(8,128)S(1)}, u32[]{:S(2)}, u32[]{:S(2)}) async-start(f32[16,64,128]{2,1,0:T(8,128)} %shard_map.130), calls=%async_computation.1 | async-start | bytes 1048576 | tf_op jit(solution)/shard_map/all_to_all | solution.py:356
  30.7 0.0 copy-start.4
  30.7 5.0 %shard_map.131 = (f32[8,512,128]{2,1,0:T(8,128)}, f32[8,128,128]{2,1,0:T(8,128)}, bf16[8,128,512]{2,1,0:T(8,128)(2,1)}) custom-call(bf16[512,2048]{1,0:T(8,128)(2,1)} %refs_0_.16, bf16[512,2048]{1,0:T(8,128)(2,1)} %refs_1_.16, bf16[512,2048]{1,0:T(8,128)(2,1)} %refs_2_.7), custom_call_target="tpu_custom_call" | custom-call | flops 603979776 | bytes 6291456 | tf_op jit(solution)/shard_map/pallas_call | solution.py:326
  35.7 3.8 %all-to-all-done.1 = f32[16,64,128]{2,1,0:T(8,128)S(1)} async-done(((f32[16,64,128]{2,1,0:T(8,128)}), f32[16,64,128]{2,1,0:T(8,128)S(1)}, u32[]{:S(2)}, u32[]{:S(2)}) %all-to-all-start.1) | async-done | bytes 524320 | tf_op jit(solution)/shard_map/all_to_all | solution.py:356
  39.6 3.6 %collective-permute-start.1 = (f32[8,128,128]{2,1,0:T(8,128)S(1)}, f32[8,128,128]{2,1,0:T(8,128)S(1)}, u32[]{:S(2)}, u32[]{:S(2)}) collective-permute-start(f32[8,128,128]{2,1,0:T(8,128)S(1)} %bitcast.5), channel_id=1, source_target_pairs={{0,1},{1,0},{2,3},{3,2},{4,5},{5,4},{6,7},{7,6},{8,9},{9,8},{10,11... | collective-permute-start | bytes 1572872 | tf_op jit(solution)/shard_map/ppermute | solution.py:373
  43.1 0.0 copy-done.4
  43.1 3.3 %shard_map.132 = (f32[8,512,128]{2,1,0:T(8,128)S(1)}, f32[2,512]{1,0:T(2,128)S(1)}, bf16[4,512,256]{2,1,0:T(8,128)(2,1)S(1)}, bf16[4,2,128,512]{3,2,1,0:T(8,128)(2,1)S(1)}, bf16[8,2,128,128]{3,2,1,0:T(8,128)(2,1)}) custom-call(bf16[512,2048]{1,0:T(8,128)(2,1)} %refs_0_.16, bf16[512,2048]{1,0:T(8,128)(2,1)} %refs_3_.3, ...), custom_call_target="tpu_custom_call" | custom-call | flops 134217728 | bytes 8396800 | tf_op jit(solution)/shard_map/pallas_call | solution.py:326
  46.4 0.0 copy-start
  46.4 0.0 collective-permute-done.1.refs_5_
  46.4 4.0 %shard_map.133 = (f32[8,512,128]{2,1,0:T(8,128)S(1)}, f32[2,512]{1,0:T(2,128)S(1)}, bf16[4,512,256]{2,1,0:T(8,128)(2,1)S(1)}, bf16[4,2,128,512]{3,2,1,0:T(8,128)(2,1)S(1)}, bf16[8,2,128,128]{3,2,1,0:T(8,128)(2,1)}) custom-call(bf16[512,2048]{1,0:T(8,128)(2,1)} %refs_0_.16, bf16[512,2048]{1,0:T(8,128)(2,1)} %refs_3_.3, ...), custom_call_target="tpu_custom_call" | custom-call | flops 134217728 | bytes 8400896 | tf_op jit(solution)/shard_map/pallas_call | solution.py:326
  50.5 0.0 copy-start.1
  50.5 2.5 %collective-permute-start.4 = (f32[2,512]{1,0:T(2,128)S(1)}, f32[2,512]{1,0:T(2,128)S(1)}, u32[]{:S(2)}, u32[]{:S(2)}) collective-permute-start(f32[2,512]{1,0:T(2,128)S(1)} %get-tuple-element.85.refs_5_), channel_id=1, source_target_pairs={{0,96},{32,0},{64,32},{96,64},{1,97},{33,1},{65,33},{97,65},{2,98}... | collective-permute-start | bytes 12296 | tf_op jit(solution)/shard_map/ppermute | solution.py:408
  53.0 0.5 collective-permute-start.3
  53.5 0.6 collective-permute-start.2
  54.8 0.0 collective-permute-done.4.refs_8_
  54.8 2.2 %collective-permute-done.3.refs_7_ = f32[2,512]{1,0:T(2,128)S(1)} collective-permute-done((f32[2,512]{1,0:T(2,128)S(1)}, f32[2,512]{1,0:T(2,128)S(1)}, u32[]{:S(2)}, u32[]{:S(2)}) %collective-permute-start.3) | collective-permute-done | bytes 4128 | tf_op jit(solution)/shard_map/ppermute | solution.py:408
  57.0 0.2 collective-permute-done.2.refs_6_
  57.2 2.1 %shard_map.134 = (f32[8,128,128]{2,1,0:T(8,128)S(1)}, f32[512,128]{1,0:T(8,128)S(1)}, f32[512,128]{1,0:T(8,128)S(1)}, bf16[8,128,128]{2,1,0:T(8,128)(2,1)}) custom-call(bf16[4,512,256]{2,1,0:T(8,128)(2,1)S(1)} %get-tuple-element.82.refs_0_, f32[8,512,128]{2,1,0:T(8,128)S(1)} %get-tuple-element.83.refs_1_.refs_4_, f32[16,1,128]{2,1,0:T(1,128)S(1)} %bitcast.11, ...), custom_call_target="tpu_custom_call" | custom-call | flops 134217728 | bytes 4218884 | tf_op jit(solution)/shard_map/pallas_call | solution.py:326
  59.3 0.0 copy-done.1
  59.3 1.8 %collective-permute-start.5 = (f32[8,128,128]{2,1,0:T(8,128)S(1)}, f32[8,128,128]{2,1,0:T(8,128)S(1)}, u32[]{:S(2)}, u32[]{:S(2)}) collective-permute-start(f32[8,128,128]{2,1,0:T(8,128)S(1)} %get-tuple-element.89), channel_id=1, source_target_pairs={{0,1},{1,0},{2,3},{3,2},{4,5},{5,4},{6,7},{7,6},{8,9},{9,8},{10,11... | collective-permute-start | bytes 1572872 | tf_op jit(solution)/shard_map/ppermute | solution.py:368
  61.1 0.0 copy-done
  61.1 1.8 %shard_map.135 = (f32[8,128,128]{2,1,0:T(8,128)S(1)}, bf16[8,128,128]{2,1,0:T(8,128)(2,1)}) custom-call(bf16[4,512,256]{2,1,0:T(8,128)(2,1)S(1)} %get-tuple-element.75.refs_0_, f32[8,512,128]{2,1,0:T(8,128)S(1)} %get-tuple-element.76.refs_1_.refs_4_, f32[16,1,128]{2,1,0:T(1,128)S(1)} %bitcast.12, bf16[4,2,128,512]{3,2,1,0:T(8,128)(2,1)S(1)} %get-tuple-element.77.refs_3_, ...), custom_call_target="tpu_custom_call" | custom-call | flops 134217728 | bytes 4726784 | tf_op jit(solution)/shard_map/pallas_call | solution.py:326
  62.9 0.0 collective-permute-done.5
  62.9 0.9 add.7
  63.8 3.6 %all-to-all-start.2 = ((f32[16,64,128]{2,1,0:T(8,128)}), f32[16,64,128]{2,1,0:T(8,128)S(1)}, u32[]{:S(2)}, u32[]{:S(2)}) async-start(f32[16,64,128]{2,1,0:T(8,128)} %bitcast.3), calls=%async_computation.2 | async-start | bytes 1048576 | tf_op jit(solution)/shard_map/all_to_all | solution.py:356
  67.4 7.5 %shard_map.136 = (bf16[512,2048]{1,0:T(8,128)(2,1)}, bf16[512,2048]{1,0:T(8,128)(2,1)}, bf16[512,2048]{1,0:T(8,128)(2,1)}, bf16[512,2048]{1,0:T(8,128)(2,1)}) custom-call(bf16[512,2048]{1,0:T(8,128)(2,1)} %refs_0_.16, bf16[512,2048]{1,0:T(8,128)(2,1)} %refs_1_.16, bf16[512,2048]{1,0:T(8,128)(2,1)} %refs_2_.7, bf16[512,2048]{1,0:T(8,128)(2,1)} %refs_3_.3, ...), custom_call_target="tpu_custom_call" | custom-call | flops 2147483648 | bytes 11804672 | tf_op jit(solution)/shard_map/pallas_call | solution.py:326
  74.8 3.1 %all-to-all-done.2.pieces_ref = f32[16,64,128]{2,1,0:T(8,128)S(1)} async-done(((f32[16,64,128]{2,1,0:T(8,128)}), f32[16,64,128]{2,1,0:T(8,128)S(1)}, u32[]{:S(2)}, u32[]{:S(2)}) %all-to-all-start.2) | async-done | bytes 524320 | tf_op jit(solution)/shard_map/all_to_all | solution.py:356
  78.0 0.9 shard_map.137
  78.8 4.0 %all-to-all-start.3 = ((f32[16,64,128]{2,1,0:T(8,128)}), f32[16,64,128]{2,1,0:T(8,128)S(1)}, u32[]{:S(2)}, u32[]{:S(2)}) async-start(f32[16,64,128]{2,1,0:T(8,128)} %shard_map.137), calls=%async_computation.3 | async-start | bytes 1048576 | tf_op jit(solution)/shard_map/all_to_all | solution.py:356
  82.9 7.5 %shard_map.138 = (bf16[4,512,256]{2,1,0:T(8,128)(2,1)S(1)}, bf16[4,512,256]{2,1,0:T(8,128)(2,1)S(1)}, bf16[512,2048]{1,0:T(8,128)(2,1)}, bf16[512,2048]{1,0:T(8,...) custom-call(bf16[512,2048]{1,0:T(8,128)(2,1)} %refs_0_.16, ...), custom_call_target="tpu_custom_call", output_to_operand_aliasing={{2}: (12, {}), {3}: (13, {}), {4}: (14, {}), {5}: (15, {})} | custom-call | flops 2147483648 | bytes 15998976 | tf_op jit(solution)/shard_map/pallas_call | solution.py:326
  90.4 0.0 copy-start.2
  90.4 1.0 copy-done.2
  91.4 0.5 all-to-all-done.3
  91.8 3.5 %collective-permute-start.6 = (f32[8,128,128]{2,1,0:T(8,128)S(1)}, f32[8,128,128]{2,1,0:T(8,128)S(1)}, u32[]{:S(2)}, u32[]{:S(2)}) collective-permute-start(f32[8,128,128]{2,1,0:T(8,128)S(1)} %bitcast.7), channel_id=1, source_target_pairs={{0,1},{1,0},{2,3},{3,2},{4,5},{5,4},{6,7},{7,6},{8,9},{9,8},{10,11... | collective-permute-start | bytes 1572872 | tf_op jit(solution)/shard_map/ppermute | solution.py:373
  95.3 0.0 copy-start.3
  95.3 1.2 %copy-done.3 = bf16[4,512,256]{2,1,0:T(8,128)(2,1)S(1)} copy-done((bf16[4,512,256]{2,1,0:T(8,128)(2,1)S(1)}, bf16[4,512,256]{2,1,0:T(8,128)(2,1)}, u32[]{:S(2)}) %copy-start.3) | copy-done | bytes 1048600
  96.5 2.7 %shard_map.139 = (bf16[4,512,256]{2,1,0:T(8,128)(2,1)S(1)}, bf16[4,512,256]{2,1,0:T(8,128)(2,1)S(1)}, bf16[512,2048]{1,0:T(8,128)(2,1)}, bf16[512,2048]{1,0:T(8,128)(2,1)}) custom-call(bf16[512,2048]{1,0:T(8,128)(2,1)} %refs_0_.17, bf16[512,2048]{1,0:T(8,128)(2,1)} %refs_1_.17, bf16[4,512,256]{2,1,0:T(8,128)(2,1)S(1)} %get-tuple-element.113.refs_2_, ...), custom_call_target="tpu_custom_call" | custom-call | flops 536870912 | bytes 6815744 | tf_op jit(solution)/shard_map/pallas_call | solution.py:326
  99.2 0.0 collective-permute-done.6.refs_2_
  99.2 2.6 %shard_map.140 = (bf16[512,2048]{1,0:T(8,128)(2,1)}, bf16[512,2048]{1,0:T(8,128)(2,1)}) custom-call(bf16[4,512,256]{2,1,0:T(8,128)(2,1)S(1)} %get-tuple-element.116.refs_0_, bf16[4,512,256]{2,1,0:T(8,128)(2,1)S(1)} %get-tuple-element.117.refs_1_, f32[8,128,128]{2,1,0:T(8,128)S(1)} %collective-permute-done.6.refs_2_, ...), custom_call_target="tpu_custom_call", output_to_operand_aliasing={{0}: (3, {}), {1}: (4, {})} | custom-call | flops 536870912 | bytes 2621440 | tf_op jit(solution)/shard_map/pallas_call | solution.py:326
Async XLA Ops:
  2.9 3.7 %collective-permute-start = (f32[8,128,128]{2,1,0:T(8,128)S(1)}, f32[8,128,128]{2,1,0:T(8,128)S(1)}, u32[]{:S(2)}, u32[]{:S(2)}) collective-permute-start(f32[8,128,128]{2,1,0:T(8,128)S(1)} %shard_map.128), channel_id=1, source_target_pairs={{0,1},{1,0},{2,3},{3,2},{4,5},{5,4},{6,7},{7,6},{8,9},{9,8},{10,11... | collective-permute-start | bytes 1572872 | tf_op jit(solution)/shard_map/ppermute | solution.py:368
  7.4 18.0 %all-to-all-start = ((f32[16,64,128]{2,1,0:T(8,128)}), f32[16,64,128]{2,1,0:T(8,128)S(1)}, u32[]{:S(2)}, u32[]{:S(2)}) async-start(f32[16,64,128]{2,1,0:T(8,128)} %bitcast), calls=%async_computation | async-start | bytes 1048576 | tf_op jit(solution)/shard_map/all_to_all | solution.py:356
  26.3 13.2 %all-to-all-start.1 = ((f32[16,64,128]{2,1,0:T(8,128)}), f32[16,64,128]{2,1,0:T(8,128)S(1)}, u32[]{:S(2)}, u32[]{:S(2)}) async-start(f32[16,64,128]{2,1,0:T(8,128)} %shard_map.130), calls=%async_computation.1 | async-start | bytes 1048576 | tf_op jit(solution)/shard_map/all_to_all | solution.py:356
  30.7 12.4 %copy-start.4 = (f32[2048]{0:T(1024)S(1)}, f32[2048]{0:T(1024)}, u32[]{:S(2)}) copy-start(f32[2048]{0:T(1024)} %param.14) | copy-start | bytes 24580
  39.6 6.9 %collective-permute-start.1 = (f32[8,128,128]{2,1,0:T(8,128)S(1)}, f32[8,128,128]{2,1,0:T(8,128)S(1)}, u32[]{:S(2)}, u32[]{:S(2)}) collective-permute-start(f32[8,128,128]{2,1,0:T(8,128)S(1)} %bitcast.5), channel_id=1, source_target_pairs={{0,1},{1,0},{2,3},{3,2},{4,5},{5,4},{6,7},{7,6},{8,9},{9,8},{10,11... | collective-permute-start | bytes 1572872 | tf_op jit(solution)/shard_map/ppermute | solution.py:373
  46.4 14.7 %copy-start = (f32[8,512,128]{2,1,0:T(8,128)}, f32[8,512,128]{2,1,0:T(8,128)S(1)}, u32[]{:S(2)}) copy-start(f32[8,512,128]{2,1,0:T(8,128)S(1)} %get-tuple-element.76.refs_1_.refs_4_) | copy-start | bytes 6291460
  50.5 8.8 %copy-start.1 = (f32[8,512,128]{2,1,0:T(8,128)}, f32[8,512,128]{2,1,0:T(8,128)S(1)}, u32[]{:S(2)}) copy-start(f32[8,512,128]{2,1,0:T(8,128)S(1)} %get-tuple-element.83.refs_1_.refs_4_) | copy-start | bytes 6291460
  50.5 4.3 %collective-permute-start.4 = (f32[2,512]{1,0:T(2,128)S(1)}, f32[2,512]{1,0:T(2,128)S(1)}, u32[]{:S(2)}, u32[]{:S(2)}) collective-permute-start(f32[2,512]{1,0:T(2,128)S(1)} %get-tuple-element.85.refs_5_), channel_id=1, source_target_pairs={{0,96},{32,0},{64,32},{96,64},{1,97},{33,1},{65,33},{97,65},{2,98}... | collective-permute-start | bytes 12296 | tf_op jit(solution)/shard_map/ppermute | solution.py:408
  53.0 4.0 %collective-permute-start.3 = (f32[2,512]{1,0:T(2,128)S(1)}, f32[2,512]{1,0:T(2,128)S(1)}, u32[]{:S(2)}, u32[]{:S(2)}) collective-permute-start(f32[2,512]{1,0:T(2,128)S(1)} %get-tuple-element.85.refs_5_), channel_id=1, source_target_pairs={{0,64},{32,96},{64,0},{96,32},{1,65},{33,97},{65,1},{97,33},{2,66}... | collective-permute-start | bytes 12296 | tf_op jit(solution)/shard_map/ppermute | solution.py:408
  53.5 3.7 %collective-permute-start.2 = (f32[2,512]{1,0:T(2,128)S(1)}, f32[2,512]{1,0:T(2,128)S(1)}, u32[]{:S(2)}, u32[]{:S(2)}) collective-permute-start(f32[2,512]{1,0:T(2,128)S(1)} %get-tuple-element.85.refs_5_), channel_id=1, source_target_pairs={{0,32},{32,64},{64,96},{96,0},{1,33},{33,65},{65,97},{97,1},{2,34}... | collective-permute-start | bytes 12296 | tf_op jit(solution)/shard_map/ppermute | solution.py:408
  59.3 3.6 %collective-permute-start.5 = (f32[8,128,128]{2,1,0:T(8,128)S(1)}, f32[8,128,128]{2,1,0:T(8,128)S(1)}, u32[]{:S(2)}, u32[]{:S(2)}) collective-permute-start(f32[8,128,128]{2,1,0:T(8,128)S(1)} %get-tuple-element.89), channel_id=1, source_target_pairs={{0,1},{1,0},{2,3},{3,2},{4,5},{5,4},{6,7},{7,6},{8,9},{9,8},{10,11... | collective-permute-start | bytes 1572872 | tf_op jit(solution)/shard_map/ppermute | solution.py:368
  63.8 14.2 %all-to-all-start.2 = ((f32[16,64,128]{2,1,0:T(8,128)}), f32[16,64,128]{2,1,0:T(8,128)S(1)}, u32[]{:S(2)}, u32[]{:S(2)}) async-start(f32[16,64,128]{2,1,0:T(8,128)} %bitcast.3), calls=%async_computation.2 | async-start | bytes 1048576 | tf_op jit(solution)/shard_map/all_to_all | solution.py:356
  78.8 13.0 %all-to-all-start.3 = ((f32[16,64,128]{2,1,0:T(8,128)}), f32[16,64,128]{2,1,0:T(8,128)S(1)}, u32[]{:S(2)}, u32[]{:S(2)}) async-start(f32[16,64,128]{2,1,0:T(8,128)} %shard_map.137), calls=%async_computation.3 | async-start | bytes 1048576 | tf_op jit(solution)/shard_map/all_to_all | solution.py:356
  90.4 1.0 copy-start.2
  91.8 7.4 %collective-permute-start.6 = (f32[8,128,128]{2,1,0:T(8,128)S(1)}, f32[8,128,128]{2,1,0:T(8,128)S(1)}, u32[]{:S(2)}, u32[]{:S(2)}) collective-permute-start(f32[8,128,128]{2,1,0:T(8,128)S(1)} %bitcast.7), channel_id=1, source_target_pairs={{0,1},{1,0},{2,3},{3,2},{4,5},{5,4},{6,7},{7,6},{8,9},{9,8},{10,11... | collective-permute-start | bytes 1572872 | tf_op jit(solution)/shard_map/ppermute | solution.py:373
  95.3 1.2 %copy-start.3 = (bf16[4,512,256]{2,1,0:T(8,128)(2,1)S(1)}, bf16[4,512,256]{2,1,0:T(8,128)(2,1)}, u32[]{:S(2)}) copy-start(bf16[4,512,256]{2,1,0:T(8,128)(2,1)} %copy-done.2) | copy-start | bytes 3145732

commit v4 on v3

--- a/solution.py
+++ b/solution.py
@@ -13,8 +13,7 @@
 WIDTH = H * HEAD_DIM
 EPSILON = 1e-06
 
-GROUP = 2
-SLAB = GROUP * HEAD_DIM
+LARGE, SMALL = 4, 2
 MIB = 1024 * 1024
 
 F32 = jnp.float32
@@ -52,17 +51,25 @@
         core = lax.axis_index("seq") % 2
         self.half = 1 - core if other else core
         self.ref, self.buffers, self.semaphores, self.out = ref, buffers, semaphores, out
+        self.started = set()
 
     def copy(self, g):
         if len(self.ref.shape) == 2:
-            start = pl.multiple_of(self.half * (self.buffers.shape[0] * SLAB) + g * SLAB, SLAB)
-            there = self.ref.at[:, pl.ds(start, SLAB)]
+            slab = self.buffers.shape[-1]
+            start = pl.multiple_of(self.half * (self.buffers.shape[0] * slab) + g * slab, slab)
+            there = self.ref.at[:, pl.ds(start, slab)]
         else:
-            there = self.ref.at[pl.ds(g * GROUP, GROUP)]
+            group = self.buffers.shape[1]
+            there = self.ref.at[pl.ds(g * group, group)]
         here = self.buffers.at[g]
         source, target = (here, there) if self.out else (there, here)
         return pltpu.make_async_copy(source, target, self.semaphores.at[g])
 
+    def start(self, g):
+        if g not in self.started:
+            self.started.add(g)
+            self.copy(g).start()
+
     def __getitem__(self, index):
         return self.buffers[index]
 
@@ -70,55 +77,70 @@
         self.buffers[index] = value
 
 
-def buffer_shape(shape):
+class Below:
+    def __init__(self, ref, first):
+        self.ref, self.first = ref, first
+
+    def __getitem__(self, index):
+        return self.ref[(*index, slice(self.first, None))]
+
+    def __setitem__(self, index, value):
+        self.ref[(*index, slice(self.first, None))] = value
+
+
+def buffer_shape(shape, group):
     if len(shape) == 2:
-        return (shape[1] // 2 // SLAB, shape[0], SLAB)
-    return (shape[0] // GROUP, GROUP) + tuple(shape[1:])
-
-
-def streamed(kernel, other, half, ins, outs, late, rest, groups):
+        slab = group * HEAD_DIM
+        return (shape[1] // 2 // slab, shape[0], slab)
+    return (shape[0] // group, group) + tuple(shape[1:])
+
+
+def streamed(kernel, half, group, groups, whole, ins, outs, late, rest):
+    for copy in whole:
+        copy.start()
+    for slabs in (ins, late):
+        for g in range(max([slab.buffers.shape[0] for slab in slabs], default=0)):
+            for slab in slabs:
+                if g < slab.buffers.shape[0]:
+                    slab.copy(g).start()
+    steps = kernel(half, group, ins, outs, rest)
+    step = next(steps)
+    for copy in whole:
+        copy.wait()
     for g in range(groups):
-        for slab in ins:
-            slab.copy(g).start()
-    for g in range(groups):
-        for slab in late:
-            slab.copy(g).start()
-    steps = kernel(half, ins, outs, rest)
-    step = next(steps)
-
-    def one(g, carry):
         for slab in ins:
             slab.copy(g).wait()
         step(g)
         for slab in outs:
-            slab.copy(g).start()
-        return carry
-
-    lax.fori_loop(0, groups, one, 0)
+            slab.start(g)
     for _ in steps:
         pass
-    for g in range(groups):
-        for slab in (*outs, *late):
+    for slab in (*outs, *late):
+        for g in range(slab.buffers.shape[0]):
             slab.copy(g).wait()
 
 
-def prefix_state_kernel(half, ins, outs, rest):
-    k, v = ins
-    (s_ref,) = rest
+def prefix_state_kernel(half, group, ins, outs, rest):
+    k, v, s_ref = (*ins, *rest)
 
     def step(g):
-        for h in range(GROUP):
-            s_ref[g * GROUP + h] = dot_tn(k[g, :, lanes(h)], v[g, :, lanes(h)])
+        for h in range(group):
+            s_ref[g * group + h] = dot_tn(k[g, :, lanes(h)], v[g, :, lanes(h)])
 
     yield step
 
 
-def intra_kernel(half, ins, outs, rest):
-    o_all, kv_all, qt_all = outs
+def bring_kernel(half, group, ins, outs, rest):
+    yield lambda g: None
+
+
+def intra_kernel(half, group, ins, outs, rest):
+    tok_rows = ins[0].buffers.shape[1]
+    o_all, kv_all, qt_all = (rest[0], Below(rest[0], tok_rows), *outs) if rest else outs
     lower = block_mask(False)
 
     def step(g):
-        for h in range(GROUP):
+        for h in range(group):
             for b in range(2):
                 q, k, v = (slab[g, rows(b), lanes(h)] for slab in ins)
                 scores = jnp.where(lower, dot_nt(q, k), 0.0).astype(BF16)
@@ -136,10 +158,13 @@
         out_ref[i] = total
 
 
-def forward_kernel(half, ins, outs, rest):
-    q, dy, intra, kv = ins
+def forward_kernel(half, group, ins, outs, rest):
     (m_all,) = outs
-    s_ref, gain_ref, *before = rest[:-4]
+    if ins:
+        intra, s_ref, gain_ref, *before = rest[:-4]
+        (q, dy), kv = ins, Below(intra, ins[0].buffers.shape[1])
+    else:
+        q, dy, kv, intra, s_ref, gain_ref, *before = rest[:-4]
     o_ref, stats_ref, square_acc, inner_acc = rest[-4:]
     heads = o_ref.shape[0]
     square_acc[...] = jnp.zeros_like(square_acc)
@@ -148,8 +173,8 @@
     def step(g):
         for b in range(2):
             square = inner = 0.0
-            for h in range(GROUP):
-                head = g * GROUP + h
+            for h in range(group):
+                head = g * group + h
                 state = s_ref[head] if b == 0 else s_ref[head] + kv[g, h]
                 m = state.astype(BF16)
                 m_all[g, h, b] = m
@@ -169,7 +194,7 @@
         stats_ref[i : i + 1] = row
 
 
-def state_grad_kernel(first, half, ins, outs, rest):
+def state_grad_kernel(first, half, group, ins, outs, rest):
     (g_all,) = outs
     dy_ref, o_ref, gain_ref, qt_ref, *rest = rest
     if first:
@@ -188,8 +213,8 @@
     heads = o_ref.shape[0]
 
     def step(g):
-        for h in range(GROUP):
-            head = g * GROUP + h
+        for h in range(group):
+            head = g * group + h
             scaled = gain_ref[half * heads + head] * dy_ref[g, :, lanes(h)].astype(F32)
             do = (scaled * inv_ref[...] - o_ref[head] * coef_ref[...]).astype(BF16)
             later = dot_nn(qt_ref[g, h, :, rows(1)], do[rows(1)])
@@ -199,17 +224,17 @@
     yield step
 
 
-def backward_kernel(half, ins, outs, rest):
+def backward_kernel(half, group, ins, outs, rest):
     q_all, k_all, v_all, dy, o_all, m_all, g_all = ins
     normed, dq_all, dk_all, dv_all = outs
-    gain_ref, inv_ref, coef_ref = rest[:3]
+    gain_ref, inv_ref, coef_ref = rest
     heads = gain_ref.shape[0] // 2
     lower, upper = block_mask(False), block_mask(True)
 
     def step(g):
-        for h in range(GROUP):
+        for h in range(group):
             o = o_all[g, h]
-            gain = gain_ref[half * heads + g * GROUP + h]
+            gain = gain_ref[half * heads + g * group + h]
             normed[g, :, lanes(h)] = (gain * o * inv_ref[...]).astype(BF16)
             scaled = gain * dy[g, :, lanes(h)].astype(F32)
             do_all = (scaled * inv_ref[...] - o * coef_ref[...]).astype(BF16)
@@ -232,24 +257,39 @@
     yield step
 
 
-def prefix_grad_kernel(half, ins, outs, rest):
+def prefix_grad_kernel(half, group, ins, outs, rest):
     dk, dv = outs
-    k_ref, v_ref, ds_ref = rest[:3]
-
-    def step(g):
-        for h in range(GROUP):
-            ds = ds_ref[g * GROUP + h]
-            high = ds.astype(BF16)
-            low = (ds - high.astype(F32)).astype(BF16)
-            k, v = k_ref[g, :, lanes(h)], v_ref[g, :, lanes(h)]
-            dk[g, :, lanes(h)] = dot_nt(
-                jnp.concatenate([v, v], 1), jnp.concatenate([high, low], 1)
-            ).astype(BF16)
-            dv[g, :, lanes(h)] = dot_nn(
-                jnp.concatenate([k, k], 1), jnp.concatenate([high, low], 0)
-            ).astype(BF16)
-
-    yield step
+    k, ds_ref, v = (*rest, *ins)
+
+    def split(head):
+        ds = ds_ref[head]
+        high = ds.astype(BF16)
+        return high, (ds - high.astype(F32)).astype(BF16)
+
+    def value_grad(g):
+        for h in range(group):
+            part = k[g, :, lanes(h)]
+            both = jnp.concatenate(split(g * group + h), 0)
+            dv[g, :, lanes(h)] = dot_nn(jnp.concatenate([part, part], 1), both).astype(BF16)
+
+    def key_grad(g):
+        for h in range(group):
+            part = v[g, :, lanes(h)]
+            both = jnp.concatenate(split(g * group + h), 1)
+            dk[g, :, lanes(h)] = dot_nt(jnp.concatenate([part, part], 1), both).astype(BF16)
+
+    if ins:
+        for g in range(rest[0].shape[0]):
+            value_grad(g)
+            dv.start(g)
+        yield key_grad
+    else:
+
+        def step(g):
+            value_grad(g)
+            key_grad(g)
+
+        yield step
 
 
 HBM = pl.BlockSpec(memory_space=pltpu.HBM)
@@ -276,17 +316,20 @@
     gains = gain.reshape(2 * half, 1, HEAD_DIM)
     OWN, OTHER = False, True
 
-    def call(kernel, other, streams, held, outs, out_streams, flops, scratch=(), aliased=(), late=(), keep=()):
+    def call(kernel, other, streams, held, outs, out_streams, flops, group=LARGE, scratch=(), aliased=(), late=(), keep=(), whole=()):
         n_in, n_out, n_late = len(streams), len(out_streams), len(late)
-        fetched = [*streams, *(a for a, _ in late)]
-        kept = [pltpu.VMEM(buffer_shape(streams[i].shape), streams[i].dtype) for i in keep]
-        kept += [pltpu.VMEM(buffer_shape(a.shape), a.dtype) for a, _ in late]
+        fetched = [*streams, *(a for a, *_ in late), *whole]
+        kept = [pltpu.VMEM(buffer_shape(streams[i].shape, group), streams[i].dtype) for i in keep]
+        kept += [pltpu.VMEM(buffer_shape(a.shape, n), a.dtype) for a, _, n in late]
         in_scratch = [i for i in range(n_in) if i not in keep]
-        buffers = [pltpu.VMEM(buffer_shape(streams[i].shape), streams[i].dtype) for i in in_scratch]
-        buffers += [pltpu.VMEM(buffer_shape(s), d) for s, d in out_streams]
+        buffers = [
+            pltpu.VMEM(buffer_shape(streams[i].shape, group), streams[i].dtype) for i in in_scratch
+        ]
+        buffers += [pltpu.VMEM(buffer_shape(s, group), d) for s, d in out_streams]
+        buffers += [pltpu.VMEM(a.shape, a.dtype) for a in whole]
         results = [pltpu.VMEM(s, d) for s, d in outs] + kept
         results += [pltpu.HBM(s, d) for s, d in out_streams]
-        groups = half // GROUP
+        groups = half // group
         size = sum(a.size * a.dtype.itemsize for a in (*fetched, *held))
 
         def run(*refs):
@@ -297,16 +340,20 @@
                 del refs[:count]
                 return taken
 
-            sources, late_sources, held_refs, _ = (
-                take(n) for n in (n_in, n_late, len(held), len(aliased))
+            sources, late_sources, whole_sources, held_refs, _ = (
+                take(n) for n in (n_in, n_late, len(whole), len(held), len(aliased))
             )
             out_refs, kept_refs, late_buffers, targets = (
                 take(n) for n in (len(outs), len(keep), n_late, n_out)
             )
-            scratch_refs, loose, out_buffers = (
-                take(n) for n in (len(scratch), len(in_scratch), n_out)
+            scratch_refs, loose, out_buffers, whole_refs = (
+                take(n) for n in (len(scratch), len(in_scratch), n_out, len(whole))
             )
             (sems,) = refs
+            copies = [
+                pltpu.make_async_copy(a, b, sems.at[n_in + n_late + n_out + i, 0])
+                for i, (a, b) in enumerate(zip(whole_sources, whole_refs))
+            ]
             in_buffers = dict(zip(keep, kept_refs)) | dict(zip(in_scratch, loose))
             ins = [Slabs(sources[i], in_buffers[i], sems.at[i], other) for i in range(n_in)]
             brought = [
@@ -318,8 +365,9 @@
                 for i in range(n_out)
             ]
             core = lax.axis_index("seq") % 2
-            rest = [*held_refs, *out_refs, *scratch_refs]
-            streamed(kernel, other, 1 - core if other else core, ins, written, brought, rest, groups)
+            this_half = 1 - core if other else core
+            rest = [*held_refs, *whole_refs, *out_refs, *scratch_refs]
+            streamed(kernel, this_half, group, groups, copies, ins, written, brought, rest)
 
         integer = [jnp.issubdtype(a.dtype, jnp.integer) for a in held]
         first_aliased = len(fetched) + len(held)
@@ -333,7 +381,7 @@
             scratch_shapes=[
                 *scratch,
                 *buffers,
-                pltpu.SemaphoreType.DMA((n_in + n_late + n_out, groups)),
+                pltpu.SemaphoreType.DMA((n_in + n_late + n_out + len(whole), half // SMALL)),
             ],
             input_output_aliases={
                 first_aliased + i: len(outs) + len(kept) + i for i in range(len(aliased))
@@ -372,56 +420,76 @@
         gathered, second = lax.optimization_barrier((gathered, beside_gather(first)))
         return gathered, lax.ppermute(gathered, "seq", swap), first, second
 
-    def prefix_state(other):
+    (theirs,) = call(
+        prefix_state_kernel,
+        OTHER,
+        [prefix_keys, prefix_values],
+        [],
+        [(states, F32)],
+        [],
+        unit,
+    )
+    (mine,) = call(prefix_state_kernel, OWN, [prefix_keys, prefix_values], [], [(states, F32)], [], unit)
+
+    kv_qt = [(states, F32), ((half, HEAD_DIM, tok_rows), BF16)]
+    token_parts = [queries, keys, values]
+
+    def intra_other():
+        outs = [(tokens, F32), *kv_qt]
+        return call(intra_kernel, OTHER, token_parts, [], [], outs, 9 * unit // 2)
+
+    def intra_own(_):
+        both = (half, tok_rows + HEAD_DIM, HEAD_DIM)
+        outs = [(buffer_shape(both, LARGE), F32)]
+        return call(intra_kernel, OWN, token_parts, [], outs, kv_qt[1:], 9 * unit // 2)
+
+    total_own, total_other, (o_other, kv_other, qt_other), (o_own, qt_own) = sum_over_seq(
+        mine, theirs, intra_other, intra_own
+    )
+
+    def forward(other, streams, held, **options):
         return call(
-            prefix_state_kernel, other, [prefix_keys, prefix_values], [], [(states, F32)], [], unit
-        )[0]
-
-    def intra_of(other):
-        outs = [(tokens, F32), (states, F32), ((half, HEAD_DIM, tok_rows), BF16)]
-        return call(intra_kernel, other, [queries, keys, values], [], [], outs, 9 * unit // 2)
-
-    theirs = prefix_state(OTHER)
-    mine = prefix_state(OWN)
-    *sums, intra_own, intra_other = sum_over_seq(
-        mine, theirs, lambda: intra_of(OWN), lambda _: intra_of(OTHER)
-    )
-
-    forward = []
-    for other, total, (o, kv, qt) in ((OWN, sums[0], intra_own), (OTHER, sums[1], intra_other)):
-        forward.append(
-            call(
-                forward_kernel,
-                other,
-                [queries, cotangent, o, kv],
-                [total, gains] + [f[1] for f in forward],
-                [(tokens, F32), ((2, tok_rows), F32)],
-                [((half, 2, HEAD_DIM, HEAD_DIM), BF16)],
-                unit,
-                scratch=[pltpu.VMEM(scalar, F32)] * 2,
-                keep=[1],
-                late=[(qt, other)],
-            )
+            forward_kernel,
+            other,
+            streams,
+            held,
+            [(tokens, F32), ((2, tok_rows), F32)],
+            [((half, 2, HEAD_DIM, HEAD_DIM), BF16)],
+            unit,
+            scratch=[pltpu.VMEM(scalar, F32)] * 2,
+            **options,
         )
-    stats = forward[1][1]
+
+    o_own, stats, dy_own, q_other, dy_other, kv_other, o_other, m_own = forward(
+        OWN,
+        [queries, cotangent],
+        [o_own, total_own, gains],
+        keep=[1],
+        late=[(a, OTHER, LARGE) for a in (queries, cotangent, kv_other, o_other)],
+    )
+    o_other, stats, m_other = forward(
+        OTHER, [], [q_other, dy_other, kv_other, o_other, total_other, gains, stats]
+    )
     all_stats = [stats] + [
         lax.ppermute(stats, "head", [(i, (i + k) % head_size) for i in range(head_size)])
         for k in range(1, head_size)
     ]
-
-    def state_grad(i, other, scalars):
-        o, _, dy, qt, _ = forward[i]
+    qts = call(bring_kernel, OWN, [], [stats], [], [], 0, late=[(qt_own, OWN, LARGE), (qt_other, OTHER, LARGE)])
+    all_stats, (qt_own, qt_other) = lax.optimization_barrier((all_stats, qts))
+
+    def state_grad(other, dy, o, qt, scalars):
         first = len(scalars) > 2
         outs = [(states, F32)] + [(scalar, F32), (scalar, F32)] * first
         kernel = functools.partial(state_grad_kernel, first)
         held = [dy, o, gains, qt, *scalars]
         return call(kernel, other, [], held, outs, [(states, BF16)], unit)
 
-    theirs, inv, coef, later_other = state_grad(1, OTHER, [lengths, *all_stats])
-    mine, later_own = state_grad(0, OWN, [inv, coef])
-
-    def backward_of(i, other, later, before=(), late=()):
-        o, _, _, _, m = forward[i]
+    theirs, inv, coef, later_other = state_grad(
+        OTHER, dy_other, o_other, qt_other, [lengths, *all_stats]
+    )
+    mine, later_own = state_grad(OWN, dy_own, o_own, qt_own, [inv, coef])
+
+    def backward(other, o, m, later, before=(), late=()):
         return call(
             backward_kernel,
             other,
@@ -430,36 +498,30 @@
             [],
             [(queries.shape, BF16)] * 4,
             16 * unit,
+            group=SMALL,
             aliased=before,
             late=late,
         )
 
-    *sums, _, (pre_k, pre_v, *grads) = sum_over_seq(
+    total_own, total_other, _, (pre_k, *grads) = sum_over_seq(
         mine,
         theirs,
-        lambda: backward_of(0, OWN, later_own),
-        lambda before: backward_of(
-            1, OTHER, later_other, before, [(prefix_keys, OWN), (prefix_values, OWN)]
+        lambda: backward(OWN, o_own, m_own, later_own),
+        lambda before: backward(
+            OTHER, o_other, m_other, later_other, before, [(prefix_keys, OWN, LARGE)]
         ),
     )
 
-    def prefix_grad(other, k, v, total, before=(), late=()):
-        return call(
-            prefix_grad_kernel,
-            other,
-            [],
-            [k, v, total],
-            [],
-            [(prefix_keys.shape, BF16)] * 2,
-            4 * unit,
-            aliased=before,
-            late=late,
-        )
+    def prefix_grad(other, streams, held, **options):
+        outs = [(prefix_keys.shape, BF16)] * 2
+        return call(prefix_grad_kernel, other, streams, held, [], outs, 4 * unit, **options)
 
     pre_k, pre_v, *prefix_grads = prefix_grad(
-        OWN, pre_k, pre_v, sums[0], late=[(prefix_keys, OTHER), (prefix_values, OTHER)]
-    )
-    prefix_grads = prefix_grad(OTHER, pre_k, pre_v, sums[1], prefix_grads)
+        OWN, [prefix_values], [pre_k, total_own], late=[(a, OTHER, SMALL) for a in (prefix_keys, prefix_values)]
+    )
+    prefix_grads = prefix_grad(
+        OTHER, [], [pre_k, total_other, pre_v], group=SMALL, aliased=prefix_grads
+    )
     return (*grads, *prefix_grads)
 
 

time: 103 us -> 97.4 us (0.946)
  Pallas kernels: 47.8 us -> 45.4 us
  local copies, waits for them, and re-layouts: 2.21 us -> 0.02 us
  waiting for transfers between devices: 14.9 us -> 13.6 us
    pallas_call x12 -> x13, Pallas kernels: 46.1 us -> 43.7 us  [call(): pl.pallas_call(run, in_specs=[HBM] * len(fetched) + [SMEM if i else VMEM...]
    unnamed x10 -> x6, local copies, waits for them, and re-layouts: 2.21 us -> 0.02 us
    ppermute x3, waiting for transfers between devices: 2.4 us -> 0.8 us  [body(): lax.ppermute(stats, 'head', [(i, (i + k) % head_size) for i in range(head...]
  transfers between devices with their start and end apart: 11 -> 11, of which waited for: 6 -> 6; matrix products, arithmetic and copies ran while one was open for 0% -> 0% of each run, Pallas kernels for 34% -> 38%
where the time goes in v4:
time: 97.4 us; the launch traced here: 96.8 us
  Pallas kernels  45.4 us (47%)
  starting transfers between devices  34.3 us (35%)
  waiting for transfers between devices  13.6 us (14%)
  other arithmetic  1.72 us (2%)
  between operations  1.67 us (2%)
    pallas_call x13, Pallas kernels, call(): pl.pallas_call(run, in_specs=[HBM] * len(fetched) + [SMEM if i else VMEM...  43.7 us
    all_to_all x4, starting transfers between devices, exchange(): lax.all_to_all(value, 'seq', 0, 0, axis_index_groups=chip_groups, tiled=T...  20.2 us
    all_to_all x4, waiting for transfers between devices, exchange(): lax.all_to_all(value, 'seq', 0, 0, axis_index_groups=chip_groups, tiled=T...  12.8 us
    ppermute x2, starting transfers between devices, sum_over_seq(): return (gathered, lax.ppermute(gathered, 'seq', swap), first, second)  7.15 us
    ppermute x3, starting transfers between devices, body(): lax.ppermute(stats, 'head', [(i, (i + k) % head_size) for i in range(head...  3.68 us
    ppermute x2, starting transfers between devices, sum_over_seq(): paired = mine + lax.ppermute(theirs, 'seq', swap)  3.3 us
  transfers between devices with their start and end apart: 11, of which 6 were waited for; matrix products, arithmetic and copies ran while one was open for 0% of the time, Pallas kernels for 38%

profile of v4, /device:TPU:1, one launch (start us, length us, event | category | flops | bytes accessed | tf_op | source)
XLA Modules:
  0.0 96.8 jit_solution(2366442446340915797)
XLA Ops:
  0.6 2.0 %shard_map.128 = f32[8,128,128]{2,1,0:T(8,128)S(1)} custom-call(bf16[512,2048]{1,0:T(8,128)(2,1)} %refs_1_.15, bf16[512,2048]{1,0:T(8,128)(2,1)} %refs_2_.11), custom_call_target="tpu_custom_call" | custom-call | flops 134217728 | bytes 4194304 | tf_op jit(solution)/shard_map/pallas_call | solution.py:374
  2.6 1.5 %collective-permute-start = (f32[8,128,128]{2,1,0:T(8,128)S(1)}, f32[8,128,128]{2,1,0:T(8,128)S(1)}, u32[]{:S(2)}, u32[]{:S(2)}) collective-permute-start(f32[8,128,128]{2,1,0:T(8,128)S(1)} %shard_map.128), channel_id=1, source_target_pairs={{0,1},{1,0},{2,3},{3,2},{4,5},{5,4},{6,7},{7,6},{8,9},{9,8},{10,11... | collective-permute-start | bytes 1572872 | tf_op jit(solution)/shard_map/ppermute | solution.py:416
  4.1 2.0 %shard_map.127 = f32[8,128,128]{2,1,0:T(8,128)S(1)} custom-call(bf16[512,2048]{1,0:T(8,128)(2,1)} %refs_1_.15, bf16[512,2048]{1,0:T(8,128)(2,1)} %refs_2_.11), custom_call_target="tpu_custom_call" | custom-call | flops 134217728 | bytes 4194304 | tf_op jit(solution)/shard_map/pallas_call | solution.py:374
  6.1 0.0 collective-permute-done
  6.1 0.9 add.6
  7.0 7.9 %all-to-all-start = ((f32[16,64,128]{2,1,0:T(8,128)}), f32[16,64,128]{2,1,0:T(8,128)S(1)}, u32[]{:S(2)}, u32[]{:S(2)}) async-start(f32[16,64,128]{2,1,0:T(8,128)} %bitcast), calls=%async_computation | async-start | bytes 1048576 | tf_op jit(solution)/shard_map/all_to_all | solution.py:404
  14.8 5.3 %shard_map.129 = (f32[8,512,128]{2,1,0:T(8,128)}, f32[8,128,128]{2,1,0:T(8,128)}, bf16[8,128,512]{2,1,0:T(8,128)(2,1)}) custom-call(bf16[512,2048]{1,0:T(8,128)(2,1)} %refs_0_.14, bf16[512,2048]{1,0:T(8,128)(2,1)} %refs_1_.14, bf16[512,2048]{1,0:T(8,128)(2,1)} %refs_2_.10), custom_call_target="tpu_custom_call" | custom-call | flops 603979776 | bytes 6291456 | tf_op jit(solution)/shard_map/pallas_call | solution.py:374
  20.2 4.8 %all-to-all-done.pieces_ref = f32[16,64,128]{2,1,0:T(8,128)S(1)} async-done(((f32[16,64,128]{2,1,0:T(8,128)}), f32[16,64,128]{2,1,0:T(8,128)S(1)}, u32[]{:S(2)}, u32[]{:S(2)}) %all-to-all-start) | async-done | bytes 524320 | tf_op jit(solution)/shard_map/all_to_all | solution.py:404
  25.0 0.9 shard_map.130
  25.8 4.3 %all-to-all-start.1 = ((f32[16,64,128]{2,1,0:T(8,128)}), f32[16,64,128]{2,1,0:T(8,128)S(1)}, u32[]{:S(2)}, u32[]{:S(2)}) async-start(f32[16,64,128]{2,1,0:T(8,128)} %shard_map.130), calls=%async_computation.1 | async-start | bytes 1048576 | tf_op jit(solution)/shard_map/all_to_all | solution.py:404
  30.2 0.0 copy-start.2
  30.2 4.8 %shard_map.131 = (f32[2,4,640,128]{3,2,1,0:T(8,128)S(1)}, bf16[8,128,512]{2,1,0:T(8,128)(2,1)}) custom-call(bf16[512,2048]{1,0:T(8,128)(2,1)} %refs_0_.14, bf16[512,2048]{1,0:T(8,128)(2,1)} %refs_1_.14, bf16[512,2048]{1,0:T(8,128)(2,1)} %refs_2_.10), custom_call_target="tpu_custom_call" | custom-call | flops 603979776 | bytes 6291456 | tf_op jit(solution)/shard_map/pallas_call | solution.py:374
  35.0 4.1 %all-to-all-done.1 = f32[16,64,128]{2,1,0:T(8,128)S(1)} async-done(((f32[16,64,128]{2,1,0:T(8,128)}), f32[16,64,128]{2,1,0:T(8,128)S(1)}, u32[]{:S(2)}, u32[]{:S(2)}) %all-to-all-start.1) | async-done | bytes 524320 | tf_op jit(solution)/shard_map/all_to_all | solution.py:404
  39.1 3.6 %collective-permute-start.1 = (f32[8,128,128]{2,1,0:T(8,128)S(1)}, f32[8,128,128]{2,1,0:T(8,128)S(1)}, u32[]{:S(2)}, u32[]{:S(2)}) collective-permute-start(f32[8,128,128]{2,1,0:T(8,128)S(1)} %bitcast.5), channel_id=1, source_target_pairs={{0,1},{1,0},{2,3},{3,2},{4,5},{5,4},{6,7},{7,6},{8,9},{9,8},{10,11... | collective-permute-start | bytes 1572872 | tf_op jit(solution)/shard_map/ppermute | solution.py:421
  42.6 0.0 copy-done.2
  42.6 3.4 %shard_map.132 = (f32[8,512,128]{2,1,0:T(8,128)S(1)}, f32[2,512]{1,0:T(2,128)S(1)}, bf16[2,512,512]{2,1,0:T(8,128)(2,1)S(1)}, bf16[2,512,512]{2,1,0:T(8,128)(2,1...) custom-call(bf16[512,2048]{1,0:T(8,128)(2,1)} %refs_0_.14, ...), custom_call_target="tpu_custom_call" | custom-call | flops 134217728 | bytes 14163968 | tf_op jit(solution)/shard_map/pallas_call | solution.py:374
  46.1 0.0 copy-start.1
  46.1 0.0 collective-permute-done.1.refs_4_
  46.1 1.6 %shard_map.133 = (f32[8,512,128]{2,1,0:T(8,128)S(1)}, f32[2,512]{1,0:T(2,128)S(1)}, bf16[8,2,128,128]{3,2,1,0:T(8,128)(2,1)}) custom-call(bf16[2,512,512]{2,1,0:T(8,128)(2,1)S(1)} %get-tuple-element.81.refs_0_, bf16[2,512,512]{2,1,0:T(8,128)(2,1)S(1)} %get-tuple-element.82.refs_1_.refs_0_, f32[2,4,128,128]{3,2,1,0:T(8,128)S(1)} %get-tuple-element.83.refs_2_, ...), custom_call_target="tpu_custom_call" | custom-call | flops 134217728 | bytes 5255168 | tf_op jit(solution)/shard_map/pallas_call | solution.py:374
  47.7 0.0 copy-start
  47.7 2.5 %collective-permute-start.4 = (f32[2,512]{1,0:T(2,128)S(1)}, f32[2,512]{1,0:T(2,128)S(1)}, u32[]{:S(2)}, u32[]{:S(2)}) collective-permute-start(f32[2,512]{1,0:T(2,128)S(1)} %get-tuple-element.94.refs_2_.refs_5_), channel_id=1, source_target_pairs={{0,96},{32,0},{64,32},{96,64},{1,97},{33,1},{65,33},{97,65},{2,98}... | collective-permute-start | bytes 12296 | tf_op jit(solution)/shard_map/ppermute | solution.py:474
  50.2 0.5 collective-permute-start.3
  50.8 0.6 collective-permute-start.2
  52.0 1.6 %shard_map.134 = (bf16[2,4,128,512]{3,2,1,0:T(8,128)(2,1)S(1)}, bf16[2,4,128,512]{3,2,1,0:T(8,128)(2,1)S(1)}) custom-call(bf16[8,128,512]{2,1,0:T(8,128)(2,1)} %get-tuple-element.87.refs_0_, bf16[8,128,512]{2,1,0:T(8,128)(2,1)} %get-tuple-element.88.refs_1_, f32[2,512]{1,0:T(2,128)S(1)} %get-tuple-element.94.refs_2_.refs_5_), custom_call_target="tpu_custom_call" | custom-call | bytes 2101248 | tf_op jit(solution)/shard_map/pallas_call | solution.py:374
  53.6 0.0 collective-permute-done.4.refs_8_
  53.6 0.6 collective-permute-done.3.refs_7_
  54.2 0.2 collective-permute-done.2.refs_6_
  54.4 1.5 %shard_map.135 = (f32[8,128,128]{2,1,0:T(8,128)S(1)}, f32[512,128]{1,0:T(8,128)S(1)}, f32[512,128]{1,0:T(8,128)S(1)}, bf16[8,128,128]{2,1,0:T(8,128)(2,1)}) custom-call(bf16[2,512,512]{2,1,0:T(8,128)(2,1)S(1)} %get-tuple-element.82.refs_1_.refs_0_, f32[8,512,128]{2,1,0:T(8,128)S(1)} %get-tuple-element.92.refs_1_.refs_4_, f32[16,1,128]{2,1,0:T(1,128)S(1)} %bitcast.11, ...), custom_call_target="tpu_custom_call" | custom-call | flops 134217728 | bytes 4218884 | tf_op jit(solution)/shard_map/pallas_call | solution.py:374
  55.9 0.0 copy-done
  56.0 1.8 %collective-permute-start.5 = (f32[8,128,128]{2,1,0:T(8,128)S(1)}, f32[8,128,128]{2,1,0:T(8,128)S(1)}, u32[]{:S(2)}, u32[]{:S(2)}) collective-permute-start(f32[8,128,128]{2,1,0:T(8,128)S(1)} %get-tuple-element.101), channel_id=1, source_target_pairs={{0,1},{1,0},{2,3},{3,2},{4,5},{5,4},{6,7},{7,6},{8,9},{9,8},{10,11... | collective-permute-start | bytes 1572872 | tf_op jit(solution)/shard_map/ppermute | solution.py:416
  57.8 0.0 copy-done.1
  57.8 1.5 %shard_map.136 = (f32[8,128,128]{2,1,0:T(8,128)S(1)}, bf16[8,128,128]{2,1,0:T(8,128)(2,1)}) custom-call(bf16[2,512,512]{2,1,0:T(8,128)(2,1)S(1)} %get-tuple-element.79.refs_0_, f32[8,512,128]{2,1,0:T(8,128)S(1)} %get-tuple-element.80.refs_1_.refs_4_, f32[16,1,128]{2,1,0:T(1,128)S(1)} %bitcast.12, bf16[2,4,128,512]{3,2,1,0:T(8,128)(2,1)S(1)} %get-tuple-element.91.refs_3_, ...), custom_call_target="tpu_custom_call" | custom-call | flops 134217728 | bytes 4726784 | tf_op jit(solution)/shard_map/pallas_call | solution.py:374
  59.3 0.0 collective-permute-done.5
  59.3 0.9 add.7
  60.2 3.8 %all-to-all-start.2 = ((f32[16,64,128]{2,1,0:T(8,128)}), f32[16,64,128]{2,1,0:T(8,128)S(1)}, u32[]{:S(2)}, u32[]{:S(2)}) async-start(f32[16,64,128]{2,1,0:T(8,128)} %bitcast.3), calls=%async_computation.2 | async-start | bytes 1048576 | tf_op jit(solution)/shard_map/all_to_all | solution.py:404
  64.0 7.5 %shard_map.137 = (bf16[512,2048]{1,0:T(8,128)(2,1)}, bf16[512,2048]{1,0:T(8,128)(2,1)}, bf16[512,2048]{1,0:T(8,128)(2,1)}, bf16[512,2048]{1,0:T(8,128)(2,1)}) custom-call(bf16[512,2048]{1,0:T(8,128)(2,1)} %refs_0_.14, bf16[512,2048]{1,0:T(8,128)(2,1)} %refs_1_.14, bf16[512,2048]{1,0:T(8,128)(2,1)} %refs_2_.10, bf16[512,2048]{1,0:T(8,128)(2,1)} %refs_3_.5, ...), custom_call_target="tpu_custom_call" | custom-call | flops 2147483648 | bytes 11804672 | tf_op jit(solution)/shard_map/pallas_call | solution.py:374
  71.4 2.5 %all-to-all-done.2.pieces_ref = f32[16,64,128]{2,1,0:T(8,128)S(1)} async-done(((f32[16,64,128]{2,1,0:T(8,128)}), f32[16,64,128]{2,1,0:T(8,128)S(1)}, u32[]{:S(2)}, u32[]{:S(2)}) %all-to-all-start.2) | async-done | bytes 524320 | tf_op jit(solution)/shard_map/all_to_all | solution.py:404
  73.9 0.9 shard_map.138
  74.8 4.2 %all-to-all-start.3 = ((f32[16,64,128]{2,1,0:T(8,128)}), f32[16,64,128]{2,1,0:T(8,128)S(1)}, u32[]{:S(2)}, u32[]{:S(2)}) async-start(f32[16,64,128]{2,1,0:T(8,128)} %shard_map.138), calls=%async_computation.3 | async-start | bytes 1048576 | tf_op jit(solution)/shard_map/all_to_all | solution.py:404
  79.1 7.5 %shard_map.139 = (bf16[2,512,512]{2,1,0:T(8,128)(2,1)S(1)}, bf16[512,2048]{1,0:T(8,128)(2,1)}, bf16[512,2048]{1,0:T(8,128)(2,1)}, bf16[512,2048]{1,0:T(8,128)(2,1)}, bf16[512,2048]{1,0:T(8,128)(2,1)}) custom-call(bf16[512,2048]{1,0:T(8,128)(2,1)} %refs_0_.14, ...), custom_call_target="tpu_custom_call", output_to_operand_aliasing={{1}: (11, {}), {2}: (12, {}), {3}: (13, {}), {4}: (14, {})} | custom-call | flops 2147483648 | bytes 13901824 | tf_op jit(solution)/shard_map/pallas_call | solution.py:374
  86.6 1.4 %all-to-all-done.3 = f32[16,64,128]{2,1,0:T(8,128)S(1)} async-done(((f32[16,64,128]{2,1,0:T(8,128)}), f32[16,64,128]{2,1,0:T(8,128)S(1)}, u32[]{:S(2)}, u32[]{:S(2)}) %all-to-all-start.3) | async-done | bytes 524320 | tf_op jit(solution)/shard_map/all_to_all | solution.py:404
  87.9 3.6 %collective-permute-start.6 = (f32[8,128,128]{2,1,0:T(8,128)S(1)}, f32[8,128,128]{2,1,0:T(8,128)S(1)}, u32[]{:S(2)}, u32[]{:S(2)}) collective-permute-start(f32[8,128,128]{2,1,0:T(8,128)S(1)} %bitcast.7), channel_id=1, source_target_pairs={{0,1},{1,0},{2,3},{3,2},{4,5},{5,4},{6,7},{7,6},{8,9},{9,8},{10,11... | collective-permute-start | bytes 1572872 | tf_op jit(solution)/shard_map/ppermute | solution.py:421
  91.5 2.9 %shard_map.140 = (bf16[4,512,256]{2,1,0:T(8,128)(2,1)S(1)}, bf16[4,512,256]{2,1,0:T(8,128)(2,1)S(1)}, bf16[512,2048]{1,0:T(8,128)(2,1)}, bf16[512,2048]{1,0:T(8,128)(2,1)}) custom-call(bf16[512,2048]{1,0:T(8,128)(2,1)} %refs_2_.11, bf16[512,2048]{1,0:T(8,128)(2,1)} %refs_1_.15, bf16[512,2048]{1,0:T(8,128)(2,1)} %refs_2_.11, ...), custom_call_target="tpu_custom_call" | custom-call | flops 536870912 | bytes 7864320 | tf_op jit(solution)/shard_map/pallas_call | solution.py:374
  94.4 0.0 collective-permute-done.6.refs_1_
  94.5 2.1 %shard_map.141 = (bf16[512,2048]{1,0:T(8,128)(2,1)}, bf16[512,2048]{1,0:T(8,128)(2,1)}) custom-call(bf16[4,512,256]{2,1,0:T(8,128)(2,1)S(1)} %get-tuple-element.126.refs_0_, f32[8,128,128]{2,1,0:T(8,128)S(1)} %collective-permute-done.6.refs_1_, bf16[4,512,256]{2,1,0:T(8,128)(2,1)S(1)} %get-tuple-element.127.refs_2_, ...), custom_call_target="tpu_custom_call", output_to_operand_aliasing={{0}: (3, {}), {1}: (4, {})} | custom-call | flops 536870912 | bytes 2621440 | tf_op jit(solution)/shard_map/pallas_call | solution.py:374
Async XLA Ops:
  2.6 3.5 %collective-permute-start = (f32[8,128,128]{2,1,0:T(8,128)S(1)}, f32[8,128,128]{2,1,0:T(8,128)S(1)}, u32[]{:S(2)}, u32[]{:S(2)}) collective-permute-start(f32[8,128,128]{2,1,0:T(8,128)S(1)} %shard_map.128), channel_id=1, source_target_pairs={{0,1},{1,0},{2,3},{3,2},{4,5},{5,4},{6,7},{7,6},{8,9},{9,8},{10,11... | collective-permute-start | bytes 1572872 | tf_op jit(solution)/shard_map/ppermute | solution.py:416
  7.0 18.0 %all-to-all-start = ((f32[16,64,128]{2,1,0:T(8,128)}), f32[16,64,128]{2,1,0:T(8,128)S(1)}, u32[]{:S(2)}, u32[]{:S(2)}) async-start(f32[16,64,128]{2,1,0:T(8,128)} %bitcast), calls=%async_computation | async-start | bytes 1048576 | tf_op jit(solution)/shard_map/all_to_all | solution.py:404
  25.8 13.2 %all-to-all-start.1 = ((f32[16,64,128]{2,1,0:T(8,128)}), f32[16,64,128]{2,1,0:T(8,128)S(1)}, u32[]{:S(2)}, u32[]{:S(2)}) async-start(f32[16,64,128]{2,1,0:T(8,128)} %shard_map.130), calls=%async_computation.1 | async-start | bytes 1048576 | tf_op jit(solution)/shard_map/all_to_all | solution.py:404
  30.2 12.4 %copy-start.2 = (f32[2048]{0:T(1024)S(1)}, f32[2048]{0:T(1024)}, u32[]{:S(2)}) copy-start(f32[2048]{0:T(1024)} %param.14) | copy-start | bytes 24580
  39.1 7.0 %collective-permute-start.1 = (f32[8,128,128]{2,1,0:T(8,128)S(1)}, f32[8,128,128]{2,1,0:T(8,128)S(1)}, u32[]{:S(2)}, u32[]{:S(2)}) collective-permute-start(f32[8,128,128]{2,1,0:T(8,128)S(1)} %bitcast.5), channel_id=1, source_target_pairs={{0,1},{1,0},{2,3},{3,2},{4,5},{5,4},{6,7},{7,6},{8,9},{9,8},{10,11... | collective-permute-start | bytes 1572872 | tf_op jit(solution)/shard_map/ppermute | solution.py:421
  46.1 11.7 %copy-start.1 = (f32[8,512,128]{2,1,0:T(8,128)}, f32[8,512,128]{2,1,0:T(8,128)S(1)}, u32[]{:S(2)}) copy-start(f32[8,512,128]{2,1,0:T(8,128)S(1)} %get-tuple-element.80.refs_1_.refs_4_) | copy-start | bytes 6291460
  47.7 8.3 %copy-start = (f32[8,512,128]{2,1,0:T(8,128)}, f32[8,512,128]{2,1,0:T(8,128)S(1)}, u32[]{:S(2)}) copy-start(f32[8,512,128]{2,1,0:T(8,128)S(1)} %get-tuple-element.92.refs_1_.refs_4_) | copy-start | bytes 6291460
  47.7 5.9 %collective-permute-start.4 = (f32[2,512]{1,0:T(2,128)S(1)}, f32[2,512]{1,0:T(2,128)S(1)}, u32[]{:S(2)}, u32[]{:S(2)}) collective-permute-start(f32[2,512]{1,0:T(2,128)S(1)} %get-tuple-element.94.refs_2_.refs_5_), channel_id=1, source_target_pairs={{0,96},{32,0},{64,32},{96,64},{1,97},{33,1},{65,33},{97,65},{2,98}... | collective-permute-start | bytes 12296 | tf_op jit(solution)/shard_map/ppermute | solution.py:474
  50.2 4.0 %collective-permute-start.3 = (f32[2,512]{1,0:T(2,128)S(1)}, f32[2,512]{1,0:T(2,128)S(1)}, u32[]{:S(2)}, u32[]{:S(2)}) collective-permute-start(f32[2,512]{1,0:T(2,128)S(1)} %get-tuple-element.94.refs_2_.refs_5_), channel_id=1, source_target_pairs={{0,64},{32,96},{64,0},{96,32},{1,65},{33,97},{65,1},{97,33},{2,66}... | collective-permute-start | bytes 12296 | tf_op jit(solution)/shard_map/ppermute | solution.py:474
  50.8 3.7 %collective-permute-start.2 = (f32[2,512]{1,0:T(2,128)S(1)}, f32[2,512]{1,0:T(2,128)S(1)}, u32[]{:S(2)}, u32[]{:S(2)}) collective-permute-start(f32[2,512]{1,0:T(2,128)S(1)} %get-tuple-element.94.refs_2_.refs_5_), channel_id=1, source_target_pairs={{0,32},{32,64},{64,96},{96,0},{1,33},{33,65},{65,97},{97,1},{2,34}... | collective-permute-start | bytes 12296 | tf_op jit(solution)/shard_map/ppermute | solution.py:474
  56.0 3.4 %collective-permute-start.5 = (f32[8,128,128]{2,1,0:T(8,128)S(1)}, f32[8,128,128]{2,1,0:T(8,128)S(1)}, u32[]{:S(2)}, u32[]{:S(2)}) collective-permute-start(f32[8,128,128]{2,1,0:T(8,128)S(1)} %get-tuple-element.101), channel_id=1, source_target_pairs={{0,1},{1,0},{2,3},{3,2},{4,5},{5,4},{6,7},{7,6},{8,9},{9,8},{10,11... | collective-permute-start | bytes 1572872 | tf_op jit(solution)/shard_map/ppermute | solution.py:416
  60.2 13.8 %all-to-all-start.2 = ((f32[16,64,128]{2,1,0:T(8,128)}), f32[16,64,128]{2,1,0:T(8,128)S(1)}, u32[]{:S(2)}, u32[]{:S(2)}) async-start(f32[16,64,128]{2,1,0:T(8,128)} %bitcast.3), calls=%async_computation.2 | async-start | bytes 1048576 | tf_op jit(solution)/shard_map/all_to_all | solution.py:404
  74.8 13.1 %all-to-all-start.3 = ((f32[16,64,128]{2,1,0:T(8,128)}), f32[16,64,128]{2,1,0:T(8,128)S(1)}, u32[]{:S(2)}, u32[]{:S(2)}) async-start(f32[16,64,128]{2,1,0:T(8,128)} %shard_map.138), calls=%async_computation.3 | async-start | bytes 1048576 | tf_op jit(solution)/shard_map/all_to_all | solution.py:404
  87.9 6.5 %collective-permute-start.6 = (f32[8,128,128]{2,1,0:T(8,128)S(1)}, f32[8,128,128]{2,1,0:T(8,128)S(1)}, u32[]{:S(2)}, u32[]{:S(2)}) collective-permute-start(f32[8,128,128]{2,1,0:T(8,128)S(1)} %bitcast.7), channel_id=1, source_target_pairs={{0,1},{1,0},{2,3},{3,2},{4,5},{5,4},{6,7},{7,6},{8,9},{9,8},{10,11... | collective-permute-start | bytes 1572872 | tf_op jit(solution)/shard_map/ppermute | solution.py:421

commit v5 on v4

--- a/solution.py
+++ b/solution.py
@@ -51,7 +51,6 @@
         core = lax.axis_index("seq") % 2
         self.half = 1 - core if other else core
         self.ref, self.buffers, self.semaphores, self.out = ref, buffers, semaphores, out
-        self.started = set()
 
     def copy(self, g):
         if len(self.ref.shape) == 2:
@@ -65,27 +64,11 @@
         source, target = (here, there) if self.out else (there, here)
         return pltpu.make_async_copy(source, target, self.semaphores.at[g])
 
-    def start(self, g):
-        if g not in self.started:
-            self.started.add(g)
-            self.copy(g).start()
-
     def __getitem__(self, index):
         return self.buffers[index]
 
     def __setitem__(self, index, value):
         self.buffers[index] = value
-
-
-class Below:
-    def __init__(self, ref, first):
-        self.ref, self.first = ref, first
-
-    def __getitem__(self, index):
-        return self.ref[(*index, slice(self.first, None))]
-
-    def __setitem__(self, index, value):
-        self.ref[(*index, slice(self.first, None))] = value
 
 
 def buffer_shape(shape, group):
@@ -95,10 +78,10 @@
     return (shape[0] // group, group) + tuple(shape[1:])
 
 
-def streamed(kernel, half, group, groups, whole, ins, outs, late, rest):
+def streamed(kernel, half, group, groups, whole, ins, outs, late, push, rest):
     for copy in whole:
         copy.start()
-    for slabs in (ins, late):
+    for slabs in (ins, push, late):
         for g in range(max([slab.buffers.shape[0] for slab in slabs], default=0)):
             for slab in slabs:
                 if g < slab.buffers.shape[0]:
@@ -112,10 +95,10 @@
             slab.copy(g).wait()
         step(g)
         for slab in outs:
-            slab.start(g)
+            slab.copy(g).start()
     for _ in steps:
         pass
-    for slab in (*outs, *late):
+    for slab in (*outs, *late, *push):
         for g in range(slab.buffers.shape[0]):
             slab.copy(g).wait()
 
@@ -135,8 +118,7 @@
 
 
 def intra_kernel(half, group, ins, outs, rest):
-    tok_rows = ins[0].buffers.shape[1]
-    o_all, kv_all, qt_all = (rest[0], Below(rest[0], tok_rows), *outs) if rest else outs
+    o_all, kv_all, qt_all = outs
     lower = block_mask(False)
 
     def step(g):
@@ -159,13 +141,8 @@
 
 
 def forward_kernel(half, group, ins, outs, rest):
-    (m_all,) = outs
-    if ins:
-        intra, s_ref, gain_ref, *before = rest[:-4]
-        (q, dy), kv = ins, Below(intra, ins[0].buffers.shape[1])
-    else:
-        q, dy, kv, intra, s_ref, gain_ref, *before = rest[:-4]
-    o_ref, stats_ref, square_acc, inner_acc = rest[-4:]
+    *operands, o_ref, m_all, stats_ref, square_acc, inner_acc = rest
+    q, dy, kv, intra, s_ref, gain_ref, *before = (*ins, *operands)
     heads = o_ref.shape[0]
     square_acc[...] = jnp.zeros_like(square_acc)
     inner_acc[...] = jnp.zeros_like(inner_acc)
@@ -195,10 +172,9 @@
 
 
 def state_grad_kernel(first, half, group, ins, outs, rest):
-    (g_all,) = outs
     dy_ref, o_ref, gain_ref, qt_ref, *rest = rest
     if first:
-        length_ref, *stats, ds_ref, inv_ref, coef_ref = rest
+        length_ref, *stats, ds_ref, g_all, inv_ref, coef_ref = rest
         total = sum(ref[...] for ref in stats[1:]) + stats[0][...]
         inv = 1.0 / jnp.sqrt(total[0:1] / WIDTH + EPSILON)
         coef = total[1:2] * (inv * inv * inv) / WIDTH
@@ -209,6 +185,7 @@
                 square = jnp.broadcast_to(value[:, lanes(n)], (HEAD_DIM, HEAD_DIM))
                 ref[n * HEAD_DIM : (n + 1) * HEAD_DIM] = square.T
     else:
+        (g_all,) = outs
         inv_ref, coef_ref, ds_ref = rest
     heads = o_ref.shape[0]
 
@@ -259,37 +236,22 @@
 
 def prefix_grad_kernel(half, group, ins, outs, rest):
     dk, dv = outs
-    k, ds_ref, v = (*rest, *ins)
-
-    def split(head):
-        ds = ds_ref[head]
-        high = ds.astype(BF16)
-        return high, (ds - high.astype(F32)).astype(BF16)
-
-    def value_grad(g):
+    k_ref, v_ref, ds_ref = rest
+
+    def step(g):
         for h in range(group):
-            part = k[g, :, lanes(h)]
-            both = jnp.concatenate(split(g * group + h), 0)
-            dv[g, :, lanes(h)] = dot_nn(jnp.concatenate([part, part], 1), both).astype(BF16)
-
-    def key_grad(g):
-        for h in range(group):
-            part = v[g, :, lanes(h)]
-            both = jnp.concatenate(split(g * group + h), 1)
-            dk[g, :, lanes(h)] = dot_nt(jnp.concatenate([part, part], 1), both).astype(BF16)
-
-    if ins:
-        for g in range(rest[0].shape[0]):
-            value_grad(g)
-            dv.start(g)
-        yield key_grad
-    else:
-
-        def step(g):
-            value_grad(g)
-            key_grad(g)
-
-        yield step
+            ds = ds_ref[g * group + h]
+            high = ds.astype(BF16)
+            low = (ds - high.astype(F32)).astype(BF16)
+            k, v = k_ref[g, :, lanes(h)], v_ref[g, :, lanes(h)]
+            dk[g, :, lanes(h)] = dot_nt(
+                jnp.concatenate([v, v], 1), jnp.concatenate([high, low], 1)
+            ).astype(BF16)
+            dv[g, :, lanes(h)] = dot_nn(
+                jnp.concatenate([k, k], 1), jnp.concatenate([high, low], 0)
+            ).astype(BF16)
+
+    yield step
 
 
 HBM = pl.BlockSpec(memory_space=pltpu.HBM)
@@ -316,7 +278,7 @@
     gains = gain.reshape(2 * half, 1, HEAD_DIM)
     OWN, OTHER = False, True
 
-    def call(kernel, other, streams, held, outs, out_streams, flops, group=LARGE, scratch=(), aliased=(), late=(), keep=(), whole=()):
+    def call(kernel, other, streams, held, outs, out_streams, flops, group=LARGE, scratch=(), aliased=(), late=(), keep=(), whole=(), push=()):
         n_in, n_out, n_late = len(streams), len(out_streams), len(late)
         fetched = [*streams, *(a for a, *_ in late), *whole]
         kept = [pltpu.VMEM(buffer_shape(streams[i].shape, group), streams[i].dtype) for i in keep]
@@ -329,6 +291,8 @@
         buffers += [pltpu.VMEM(a.shape, a.dtype) for a in whole]
         results = [pltpu.VMEM(s, d) for s, d in outs] + kept
         results += [pltpu.HBM(s, d) for s, d in out_streams]
+        results += [pltpu.HBM(s, a.dtype) for a, s in push]
+        n_push = len(push)
         groups = half // group
         size = sum(a.size * a.dtype.itemsize for a in (*fetched, *held))
 
@@ -340,11 +304,11 @@
                 del refs[:count]
                 return taken
 
-            sources, late_sources, whole_sources, held_refs, _ = (
-                take(n) for n in (n_in, n_late, len(whole), len(held), len(aliased))
+            sources, late_sources, whole_sources, held_refs, push_buffers, _ = (
+                take(n) for n in (n_in, n_late, len(whole), len(held), n_push, len(aliased))
             )
-            out_refs, kept_refs, late_buffers, targets = (
-                take(n) for n in (len(outs), len(keep), n_late, n_out)
+            out_refs, kept_refs, late_buffers, targets, push_targets = (
+                take(n) for n in (len(outs), len(keep), n_late, n_out, n_push)
             )
             scratch_refs, loose, out_buffers, whole_refs = (
                 take(n) for n in (len(scratch), len(in_scratch), n_out, len(whole))
@@ -365,23 +329,31 @@
                 for i in range(n_out)
             ]
             core = lax.axis_index("seq") % 2
+            last = n_in + n_late + n_out + len(whole)
+            pushed = [
+                Slabs(a, b, sems.at[last + i], other, True)
+                for i, (a, b) in enumerate(zip(push_targets, push_buffers))
+            ]
             this_half = 1 - core if other else core
             rest = [*held_refs, *whole_refs, *out_refs, *scratch_refs]
-            streamed(kernel, this_half, group, groups, copies, ins, written, brought, rest)
-
-        integer = [jnp.issubdtype(a.dtype, jnp.integer) for a in held]
-        first_aliased = len(fetched) + len(held)
+            streamed(kernel, this_half, group, groups, copies, ins, written, brought, pushed, rest)
+
+        in_place = [*held, *(a for a, _ in push)]
+        integer = [jnp.issubdtype(a.dtype, jnp.integer) for a in in_place]
+        first_aliased = len(fetched) + len(in_place)
         return pl.pallas_call(
             run,
             in_specs=[HBM] * len(fetched)
             + [SMEM if i else VMEM for i in integer]
             + [HBM] * len(aliased),
-            out_specs=[VMEM] * (len(outs) + len(kept)) + [HBM] * n_out,
+            out_specs=[VMEM] * (len(outs) + len(kept)) + [HBM] * (n_out + n_push),
             out_shape=results,
             scratch_shapes=[
                 *scratch,
                 *buffers,
-                pltpu.SemaphoreType.DMA((n_in + n_late + n_out + len(whole), half // SMALL)),
+                pltpu.SemaphoreType.DMA(
+                    (n_in + n_late + n_out + len(whole) + n_push, half // SMALL)
+                ),
             ],
             input_output_aliases={
                 first_aliased + i: len(outs) + len(kept) + i for i in range(len(aliased))
@@ -390,7 +362,7 @@
             compiler_params=pltpu.CompilerParams(vmem_limit_bytes=VMEM_LIMIT),
         )(
             *(in_hbm(a) for a in fetched),
-            *(a if i else in_vmem(a) for a, i in zip(held, integer)),
+            *(a if i else in_vmem(a) for a, i in zip(in_place, integer)),
             *(in_hbm(a) for a in aliased),
         )
 
@@ -431,21 +403,17 @@
     )
     (mine,) = call(prefix_state_kernel, OWN, [prefix_keys, prefix_values], [], [(states, F32)], [], unit)
 
-    kv_qt = [(states, F32), ((half, HEAD_DIM, tok_rows), BF16)]
     token_parts = [queries, keys, values]
 
-    def intra_other():
-        outs = [(tokens, F32), *kv_qt]
-        return call(intra_kernel, OTHER, token_parts, [], [], outs, 9 * unit // 2)
-
-    def intra_own(_):
-        both = (half, tok_rows + HEAD_DIM, HEAD_DIM)
-        outs = [(buffer_shape(both, LARGE), F32)]
-        return call(intra_kernel, OWN, token_parts, [], outs, kv_qt[1:], 9 * unit // 2)
-
-    total_own, total_other, (o_other, kv_other, qt_other), (o_own, qt_own) = sum_over_seq(
-        mine, theirs, intra_other, intra_own
-    )
+    def intra(other):
+        outs = [(tokens, F32), (states, F32), ((half, HEAD_DIM, tok_rows), BF16)]
+        return call(intra_kernel, other, token_parts, [], [], outs, 9 * unit // 2)
+
+    total_own, total_other, (o_own, kv_own, qt_own), (o_other, kv_other, qt_other) = sum_over_seq(
+        mine, theirs, lambda: intra(OWN), lambda _: intra(OTHER)
+    )
+
+    rounded = (half, 2, HEAD_DIM, HEAD_DIM)
 
     def forward(other, streams, held, **options):
         return call(
@@ -453,74 +421,90 @@
             other,
             streams,
             held,
-            [(tokens, F32), ((2, tok_rows), F32)],
-            [((half, 2, HEAD_DIM, HEAD_DIM), BF16)],
+            [(tokens, F32), (buffer_shape(rounded, LARGE), BF16), ((2, tok_rows), F32)],
+            [],
             unit,
             scratch=[pltpu.VMEM(scalar, F32)] * 2,
             **options,
         )
 
-    o_own, stats, dy_own, q_other, dy_other, kv_other, o_other, m_own = forward(
+    o_own, m_own, stats, dy_own, q_other, dy_other, kv_other, o_other = forward(
         OWN,
-        [queries, cotangent],
-        [o_own, total_own, gains],
+        [queries, cotangent, kv_own, o_own],
+        [total_own, gains],
         keep=[1],
         late=[(a, OTHER, LARGE) for a in (queries, cotangent, kv_other, o_other)],
     )
-    o_other, stats, m_other = forward(
+    o_other, m_other, stats = forward(
         OTHER, [], [q_other, dy_other, kv_other, o_other, total_other, gains, stats]
     )
     all_stats = [stats] + [
         lax.ppermute(stats, "head", [(i, (i + k) % head_size) for i in range(head_size)])
         for k in range(1, head_size)
     ]
-    qts = call(bring_kernel, OWN, [], [stats], [], [], 0, late=[(qt_own, OWN, LARGE), (qt_other, OTHER, LARGE)])
-    all_stats, (qt_own, qt_other) = lax.optimization_barrier((all_stats, qts))
-
-    def state_grad(other, dy, o, qt, scalars):
+    qts = call(
+        bring_kernel,
+        OWN,
+        [],
+        [stats],
+        [],
+        [],
+        0,
+        late=[(qt_own, OWN, LARGE), (qt_other, OTHER, LARGE)],
+        push=[(m_own, rounded), (m_other, rounded)],
+    )
+    all_stats, (qt_own, qt_other, m_own, m_other) = lax.optimization_barrier((all_stats, qts))
+
+    def state_grad(other, dy, o, qt, scalars, **options):
         first = len(scalars) > 2
-        outs = [(states, F32)] + [(scalar, F32), (scalar, F32)] * first
+        outs, out_streams = [(states, F32)], [(states, BF16)]
+        if first:
+            outs += [(buffer_shape(states, LARGE), BF16), (scalar, F32), (scalar, F32)]
+            out_streams = []
         kernel = functools.partial(state_grad_kernel, first)
         held = [dy, o, gains, qt, *scalars]
-        return call(kernel, other, [], held, outs, [(states, BF16)], unit)
-
-    theirs, inv, coef, later_other = state_grad(
+        return call(kernel, other, [], held, outs, out_streams, unit, **options)
+
+    theirs, later_other, inv, coef = state_grad(
         OTHER, dy_other, o_other, qt_other, [lengths, *all_stats]
     )
-    mine, later_own = state_grad(OWN, dy_own, o_own, qt_own, [inv, coef])
+    mine, later_own, later_other = state_grad(
+        OWN, dy_own, o_own, qt_own, [inv, coef], push=[(later_other, states)]
+    )
 
     def backward(other, o, m, later, before=(), late=()):
         return call(
             backward_kernel,
             other,
             [queries, keys, values, cotangent, o, m, later],
-            [gains, inv, coef],
+            [gains],
             [],
             [(queries.shape, BF16)] * 4,
             16 * unit,
+            whole=[inv, coef],
             group=SMALL,
             aliased=before,
             late=late,
         )
 
-    total_own, total_other, _, (pre_k, *grads) = sum_over_seq(
+    total_own, total_other, _, (pre_k, pre_v, *grads) = sum_over_seq(
         mine,
         theirs,
         lambda: backward(OWN, o_own, m_own, later_own),
         lambda before: backward(
-            OTHER, o_other, m_other, later_other, before, [(prefix_keys, OWN, LARGE)]
+            OTHER, o_other, m_other, later_other, before, [(prefix_keys, OWN, LARGE), (prefix_values, OWN, LARGE)]
         ),
     )
 
-    def prefix_grad(other, streams, held, **options):
+    def prefix_grad(other, k, v, total, **options):
         outs = [(prefix_keys.shape, BF16)] * 2
-        return call(prefix_grad_kernel, other, streams, held, [], outs, 4 * unit, **options)
+        return call(prefix_grad_kernel, other, [], [k, v, total], [], outs, 4 * unit, **options)
 
     pre_k, pre_v, *prefix_grads = prefix_grad(
-        OWN, [prefix_values], [pre_k, total_own], late=[(a, OTHER, SMALL) for a in (prefix_keys, prefix_values)]
+        OWN, pre_k, pre_v, total_own, late=[(a, OTHER, SMALL) for a in (prefix_keys, prefix_values)]
     )
     prefix_grads = prefix_grad(
-        OTHER, [], [pre_k, total_other, pre_v], group=SMALL, aliased=prefix_grads
+        OTHER, pre_k, pre_v, total_other, group=SMALL, aliased=prefix_grads
     )
     return (*grads, *prefix_grads)
 

time: 97.4 us -> 96.1 us (0.987)
  waiting for transfers between devices: 13.6 us -> 12.1 us
    all_to_all x4, waiting for transfers between devices: 12.8 us -> 11.8 us  [exchange(): lax.all_to_all(value, 'seq', 0, 0, axis_index_groups=chip_groups, tiled=T...]
  transfers between devices with their start and end apart: 11 -> 11, of which waited for: 6 -> 6; matrix products, arithmetic and copies ran while one was open for 0% -> 0% of each run, Pallas kernels for 38% -> 40%
where the time goes in v5:
time: 96.1 us; the launch traced here: 95.4 us
  Pallas kernels  45.5 us (47%)
  starting transfers between devices  34.3 us (36%)
  waiting for transfers between devices  12.1 us (13%)
  other arithmetic  1.74 us (2%)
  between operations  1.69 us (2%)
    pallas_call x13, Pallas kernels, call(): pl.pallas_call(run, in_specs=[HBM] * len(fetched) + [SMEM if i else VMEM...  43.8 us
    all_to_all x4, starting transfers between devices, exchange(): lax.all_to_all(value, 'seq', 0, 0, axis_index_groups=chip_groups, tiled=T...  20.1 us
    all_to_all x4, waiting for transfers between devices, exchange(): lax.all_to_all(value, 'seq', 0, 0, axis_index_groups=chip_groups, tiled=T...  11.8 us
    ppermute x2, starting transfers between devices, sum_over_seq(): return (gathered, lax.ppermute(gathered, 'seq', swap), first, second)  7.19 us
    ppermute x3, starting transfers between devices, body(): lax.ppermute(stats, 'head', [(i, (i + k) % head_size) for i in range(head...  3.68 us
    ppermute x2, starting transfers between devices, sum_over_seq(): paired = mine + lax.ppermute(theirs, 'seq', swap)  3.3 us
  transfers between devices with their start and end apart: 11, of which 6 were waited for; matrix products, arithmetic and copies ran while one was open for 0% of the time, Pallas kernels for 40%

profile of v5, /device:TPU:1, one launch (start us, length us, event | category | flops | bytes accessed | tf_op | source)
XLA Modules:
  0.0 95.4 jit_solution(407079895903921042)
XLA Ops:
  0.6 2.0 %shard_map.128 = f32[8,128,128]{2,1,0:T(8,128)S(1)} custom-call(bf16[512,2048]{1,0:T(8,128)(2,1)} %refs_0_.15, bf16[512,2048]{1,0:T(8,128)(2,1)} %refs_1_.15), custom_call_target="tpu_custom_call" | custom-call | flops 134217728 | bytes 4194304 | tf_op jit(solution)/shard_map/pallas_call | solution.py:344
  2.6 1.5 %collective-permute-start = (f32[8,128,128]{2,1,0:T(8,128)S(1)}, f32[8,128,128]{2,1,0:T(8,128)S(1)}, u32[]{:S(2)}, u32[]{:S(2)}) collective-permute-start(f32[8,128,128]{2,1,0:T(8,128)S(1)} %shard_map.128), channel_id=1, source_target_pairs={{0,1},{1,0},{2,3},{3,2},{4,5},{5,4},{6,7},{7,6},{8,9},{9,8},{10,11... | collective-permute-start | bytes 1572872 | tf_op jit(solution)/shard_map/ppermute | solution.py:388
  4.1 2.0 %shard_map.127 = f32[8,128,128]{2,1,0:T(8,128)S(1)} custom-call(bf16[512,2048]{1,0:T(8,128)(2,1)} %refs_0_.15, bf16[512,2048]{1,0:T(8,128)(2,1)} %refs_1_.15), custom_call_target="tpu_custom_call" | custom-call | flops 134217728 | bytes 4194304 | tf_op jit(solution)/shard_map/pallas_call | solution.py:344
  6.1 0.0 collective-permute-done
  6.1 0.9 add.6
  7.0 7.9 %all-to-all-start = ((f32[16,64,128]{2,1,0:T(8,128)}), f32[16,64,128]{2,1,0:T(8,128)S(1)}, u32[]{:S(2)}, u32[]{:S(2)}) async-start(f32[16,64,128]{2,1,0:T(8,128)} %bitcast), calls=%async_computation | async-start | bytes 1048576 | tf_op jit(solution)/shard_map/all_to_all | solution.py:376
  14.8 5.3 %shard_map.129 = (f32[8,512,128]{2,1,0:T(8,128)}, f32[8,128,128]{2,1,0:T(8,128)}, bf16[8,128,512]{2,1,0:T(8,128)(2,1)}) custom-call(bf16[512,2048]{1,0:T(8,128)(2,1)} %refs_0_.14, bf16[512,2048]{1,0:T(8,128)(2,1)} %refs_1_.14, bf16[512,2048]{1,0:T(8,128)(2,1)} %refs_2_.7), custom_call_target="tpu_custom_call" | custom-call | flops 603979776 | bytes 6291456 | tf_op jit(solution)/shard_map/pallas_call | solution.py:344
  20.2 4.8 %all-to-all-done.pieces_ref = f32[16,64,128]{2,1,0:T(8,128)S(1)} async-done(((f32[16,64,128]{2,1,0:T(8,128)}), f32[16,64,128]{2,1,0:T(8,128)S(1)}, u32[]{:S(2)}, u32[]{:S(2)}) %all-to-all-start) | async-done | bytes 524320 | tf_op jit(solution)/shard_map/all_to_all | solution.py:376
  25.0 0.9 shard_map.130
  25.9 4.3 %all-to-all-start.1 = ((f32[16,64,128]{2,1,0:T(8,128)}), f32[16,64,128]{2,1,0:T(8,128)S(1)}, u32[]{:S(2)}, u32[]{:S(2)}) async-start(f32[16,64,128]{2,1,0:T(8,128)} %shard_map.130), calls=%async_computation.1 | async-start | bytes 1048576 | tf_op jit(solution)/shard_map/all_to_all | solution.py:376
  30.2 0.0 copy-start.4
  30.2 5.3 %shard_map.131 = (f32[8,512,128]{2,1,0:T(8,128)}, f32[8,128,128]{2,1,0:T(8,128)}, bf16[8,128,512]{2,1,0:T(8,128)(2,1)}) custom-call(bf16[512,2048]{1,0:T(8,128)(2,1)} %refs_0_.14, bf16[512,2048]{1,0:T(8,128)(2,1)} %refs_1_.14, bf16[512,2048]{1,0:T(8,128)(2,1)} %refs_2_.7), custom_call_target="tpu_custom_call" | custom-call | flops 603979776 | bytes 6291456 | tf_op jit(solution)/shard_map/pallas_call | solution.py:344
  35.6 3.5 %all-to-all-done.1 = f32[16,64,128]{2,1,0:T(8,128)S(1)} async-done(((f32[16,64,128]{2,1,0:T(8,128)}), f32[16,64,128]{2,1,0:T(8,128)S(1)}, u32[]{:S(2)}, u32[]{:S(2)}) %all-to-all-start.1) | async-done | bytes 524320 | tf_op jit(solution)/shard_map/all_to_all | solution.py:376
  39.1 3.6 %collective-permute-start.1 = (f32[8,128,128]{2,1,0:T(8,128)S(1)}, f32[8,128,128]{2,1,0:T(8,128)S(1)}, u32[]{:S(2)}, u32[]{:S(2)}) collective-permute-start(f32[8,128,128]{2,1,0:T(8,128)S(1)} %bitcast.5), channel_id=1, source_target_pairs={{0,1},{1,0},{2,3},{3,2},{4,5},{5,4},{6,7},{7,6},{8,9},{9,8},{10,11... | collective-permute-start | bytes 1572872 | tf_op jit(solution)/shard_map/ppermute | solution.py:393
  42.7 0.0 copy-done.4
  42.7 4.0 %shard_map.132 = (f32[8,512,128]{2,1,0:T(8,128)S(1)}, bf16[2,4,2,128,128]{4,3,2,1,0:T(8,128)(2,1)S(1)}, f32[2,512]{1,0:T(2,128)S(1)}, bf16[2,512,512]{2,1,0:T(8,...) custom-call(bf16[512,2048]{1,0:T(8,128)(2,1)} %refs_0_.14, ...), custom_call_target="tpu_custom_call" | custom-call | flops 134217728 | bytes 14163968 | tf_op jit(solution)/shard_map/pallas_call | solution.py:344
  46.7 0.0 copy-start
  46.7 0.0 collective-permute-done.1.refs_4_
  46.7 0.9 shard_map.133
  47.6 0.0 copy-start.1
  47.6 2.5 %collective-permute-start.4 = (f32[2,512]{1,0:T(2,128)S(1)}, f32[2,512]{1,0:T(2,128)S(1)}, u32[]{:S(2)}, u32[]{:S(2)}) collective-permute-start(f32[2,512]{1,0:T(2,128)S(1)} %get-tuple-element.109.refs_2_.refs_5_), channel_id=1, source_target_pairs={{0,96},{32,0},{64,32},{96,64},{1,97},{33,1},{65,33},{97,65},{2,98}... | collective-permute-start | bytes 12296 | tf_op jit(solution)/shard_map/ppermute | solution.py:442
  50.1 0.5 collective-permute-start.3
  50.7 0.6 collective-permute-start.2
  51.9 2.0 %shard_map.134 = (bf16[2,4,128,512]{3,2,1,0:T(8,128)(2,1)S(1)}, bf16[2,4,128,512]{3,2,1,0:T(8,128)(2,1)S(1)}, bf16[8,2,128,128]{3,2,1,0:T(8,128)(2,1)}, bf16[8,2,128,128]{3,2,1,0:T(8,128)(2,1)}) custom-call(bf16[8,128,512]{2,1,0:T(8,128)(2,1)} %get-tuple-element.98.refs_0_, bf16[8,128,512]{2,1,0:T(8,128)(2,1)} %get-tuple-element.99.refs_1_, ...), custom_call_target="tpu_custom_call" | custom-call | bytes 2101248 | tf_op jit(solution)/shard_map/pallas_call | solution.py:344
  54.0 0.0 collective-permute-done.4.refs_8_
  54.0 0.1 collective-permute-done.3.refs_7_
  54.1 0.2 collective-permute-done.2.refs_6_
  54.3 0.8 shard_map.135
  55.2 0.0 copy-done.1
  55.2 0.0 copy-start.2
  55.2 0.0 copy-start.3
  55.2 1.8 %collective-permute-start.5 = (f32[8,128,128]{2,1,0:T(8,128)S(1)}, f32[8,128,128]{2,1,0:T(8,128)S(1)}, u32[]{:S(2)}, u32[]{:S(2)}) collective-permute-start(f32[8,128,128]{2,1,0:T(8,128)S(1)} %get-tuple-element.117), channel_id=1, source_target_pairs={{0,1},{1,0},{2,3},{3,2},{4,5},{5,4},{6,7},{7,6},{8,9},{9,8},{10,11... | collective-permute-start | bytes 1572872 | tf_op jit(solution)/shard_map/ppermute | solution.py:388
  57.0 1.5 %shard_map.136 = (f32[8,128,128]{2,1,0:T(8,128)S(1)}, bf16[8,128,128]{2,1,0:T(8,128)(2,1)}, bf16[8,128,128]{2,1,0:T(8,128)(2,1)}) custom-call(bf16[2,512,512]{2,1,0:T(8,128)(2,1)S(1)} %get-tuple-element.90.refs_0_, f32[8,512,128]{2,1,0:T(8,128)S(1)} %get-tuple-element.91.refs_1_.refs_4_, f32[16,1,128]{2,1,0:T(1,128)S(1)} %bitcast.12, ...), custom_call_target="tpu_custom_call" | custom-call | flops 134217728 | bytes 4726784 | tf_op jit(solution)/shard_map/pallas_call | solution.py:344
  58.5 0.0 copy-done.2
  58.5 0.0 copy-done.3
  58.5 0.0 collective-permute-done.5
  58.5 0.9 add.7
  59.4 3.8 %all-to-all-start.2 = ((f32[16,64,128]{2,1,0:T(8,128)}), f32[16,64,128]{2,1,0:T(8,128)S(1)}, u32[]{:S(2)}, u32[]{:S(2)}) async-start(f32[16,64,128]{2,1,0:T(8,128)} %bitcast.3), calls=%async_computation.2 | async-start | bytes 1048576 | tf_op jit(solution)/shard_map/all_to_all | solution.py:376
  63.2 7.7 %shard_map.137 = (bf16[512,2048]{1,0:T(8,128)(2,1)}, bf16[512,2048]{1,0:T(8,128)(2,1)}, bf16[512,2048]{1,0:T(8,128)(2,1)}, bf16[512,2048]{1,0:T(8,128)(2,1)}) custom-call(bf16[512,2048]{1,0:T(8,128)(2,1)} %refs_0_.14, bf16[512,2048]{1,0:T(8,128)(2,1)} %refs_1_.14, bf16[512,2048]{1,0:T(8,128)(2,1)} %refs_2_.7, bf16[512,2048]{1,0:T(8,128)(2,1)} %refs_3_.3, ...), custom_call_target="tpu_custom_call" | custom-call | flops 2147483648 | bytes 11804672 | tf_op jit(solution)/shard_map/pallas_call | solution.py:344
  70.9 2.4 %all-to-all-done.2.pieces_ref = f32[16,64,128]{2,1,0:T(8,128)S(1)} async-done(((f32[16,64,128]{2,1,0:T(8,128)}), f32[16,64,128]{2,1,0:T(8,128)S(1)}, u32[]{:S(2)}, u32[]{:S(2)}) %all-to-all-start.2) | async-done | bytes 524320 | tf_op jit(solution)/shard_map/all_to_all | solution.py:376
  73.2 0.9 shard_map.138
  74.1 4.2 %all-to-all-start.3 = ((f32[16,64,128]{2,1,0:T(8,128)}), f32[16,64,128]{2,1,0:T(8,128)S(1)}, u32[]{:S(2)}, u32[]{:S(2)}) async-start(f32[16,64,128]{2,1,0:T(8,128)} %shard_map.138), calls=%async_computation.3 | async-start | bytes 1048576 | tf_op jit(solution)/shard_map/all_to_all | solution.py:376
  78.3 7.7 %shard_map.139 = (bf16[2,512,512]{2,1,0:T(8,128)(2,1)S(1)}, bf16[2,512,512]{2,1,0:T(8,128)(2,1)S(1)}, bf16[512,2048]{1,0:T(8,128)(2,1)}, bf16[512,2048]{1,0:T(8,...) custom-call(bf16[512,2048]{1,0:T(8,128)(2,1)} %refs_0_.14, ...), custom_call_target="tpu_custom_call", output_to_operand_aliasing={{2}: (12, {}), {3}: (13, {}), {4}: (14, {}), {5}: (15, {})} | custom-call | flops 2147483648 | bytes 15998976 | tf_op jit(solution)/shard_map/pallas_call | solution.py:344
  86.0 1.1 %all-to-all-done.3 = f32[16,64,128]{2,1,0:T(8,128)S(1)} async-done(((f32[16,64,128]{2,1,0:T(8,128)}), f32[16,64,128]{2,1,0:T(8,128)S(1)}, u32[]{:S(2)}, u32[]{:S(2)}) %all-to-all-start.3) | async-done | bytes 524320 | tf_op jit(solution)/shard_map/all_to_all | solution.py:376
  87.1 3.6 %collective-permute-start.6 = (f32[8,128,128]{2,1,0:T(8,128)S(1)}, f32[8,128,128]{2,1,0:T(8,128)S(1)}, u32[]{:S(2)}, u32[]{:S(2)}) collective-permute-start(f32[8,128,128]{2,1,0:T(8,128)S(1)} %bitcast.7), channel_id=1, source_target_pairs={{0,1},{1,0},{2,3},{3,2},{4,5},{5,4},{6,7},{7,6},{8,9},{9,8},{10,11... | collective-permute-start | bytes 1572872 | tf_op jit(solution)/shard_map/ppermute | solution.py:393
  90.7 2.4 %shard_map.140 = (bf16[4,512,256]{2,1,0:T(8,128)(2,1)S(1)}, bf16[4,512,256]{2,1,0:T(8,128)(2,1)S(1)}, bf16[512,2048]{1,0:T(8,128)(2,1)}, bf16[512,2048]{1,0:T(8,128)(2,1)}) custom-call(bf16[512,2048]{1,0:T(8,128)(2,1)} %refs_0_.15, bf16[512,2048]{1,0:T(8,128)(2,1)} %refs_1_.15, bf16[2,512,512]{2,1,0:T(8,128)(2,1)S(1)} %get-tuple-element.141.refs_2_, ...), custom_call_target="tpu_custom_call" | custom-call | flops 536870912 | bytes 6815744 | tf_op jit(solution)/shard_map/pallas_call | solution.py:344
  93.1 0.0 collective-permute-done.6.refs_2_
  93.1 2.1 %shard_map.141 = (bf16[512,2048]{1,0:T(8,128)(2,1)}, bf16[512,2048]{1,0:T(8,128)(2,1)}) custom-call(bf16[4,512,256]{2,1,0:T(8,128)(2,1)S(1)} %get-tuple-element.144.refs_0_, bf16[4,512,256]{2,1,0:T(8,128)(2,1)S(1)} %get-tuple-element.145.refs_1_, f32[8,128,128]{2,1,0:T(8,128)S(1)} %collective-permute-done.6.refs_2_, ...), custom_call_target="tpu_custom_call", output_to_operand_aliasing={{0}: (3, {}), {1}: (4, {})} | custom-call | flops 536870912 | bytes 2621440 | tf_op jit(solution)/shard_map/pallas_call | solution.py:344
  (1 shorter events, 0.0 us)
Async XLA Ops:
  2.6 3.5 %collective-permute-start = (f32[8,128,128]{2,1,0:T(8,128)S(1)}, f32[8,128,128]{2,1,0:T(8,128)S(1)}, u32[]{:S(2)}, u32[]{:S(2)}) collective-permute-start(f32[8,128,128]{2,1,0:T(8,128)S(1)} %shard_map.128), channel_id=1, source_target_pairs={{0,1},{1,0},{2,3},{3,2},{4,5},{5,4},{6,7},{7,6},{8,9},{9,8},{10,11... | collective-permute-start | bytes 1572872 | tf_op jit(solution)/shard_map/ppermute | solution.py:388
  7.0 18.0 %all-to-all-start = ((f32[16,64,128]{2,1,0:T(8,128)}), f32[16,64,128]{2,1,0:T(8,128)S(1)}, u32[]{:S(2)}, u32[]{:S(2)}) async-start(f32[16,64,128]{2,1,0:T(8,128)} %bitcast), calls=%async_computation | async-start | bytes 1048576 | tf_op jit(solution)/shard_map/all_to_all | solution.py:376
  25.9 13.2 %all-to-all-start.1 = ((f32[16,64,128]{2,1,0:T(8,128)}), f32[16,64,128]{2,1,0:T(8,128)S(1)}, u32[]{:S(2)}, u32[]{:S(2)}) async-start(f32[16,64,128]{2,1,0:T(8,128)} %shard_map.130), calls=%async_computation.1 | async-start | bytes 1048576 | tf_op jit(solution)/shard_map/all_to_all | solution.py:376
  30.2 12.4 %copy-start.4 = (f32[2048]{0:T(1024)S(1)}, f32[2048]{0:T(1024)}, u32[]{:S(2)}) copy-start(f32[2048]{0:T(1024)} %param.14) | copy-start | bytes 24580
  39.1 7.6 %collective-permute-start.1 = (f32[8,128,128]{2,1,0:T(8,128)S(1)}, f32[8,128,128]{2,1,0:T(8,128)S(1)}, u32[]{:S(2)}, u32[]{:S(2)}) collective-permute-start(f32[8,128,128]{2,1,0:T(8,128)S(1)} %bitcast.5), channel_id=1, source_target_pairs={{0,1},{1,0},{2,3},{3,2},{4,5},{5,4},{6,7},{7,6},{8,9},{9,8},{10,11... | collective-permute-start | bytes 1572872 | tf_op jit(solution)/shard_map/ppermute | solution.py:393
  46.7 10.3 %copy-start = (f32[8,512,128]{2,1,0:T(8,128)}, f32[8,512,128]{2,1,0:T(8,128)S(1)}, u32[]{:S(2)}) copy-start(f32[8,512,128]{2,1,0:T(8,128)S(1)} %get-tuple-element.91.refs_1_.refs_4_) | copy-start | bytes 6291460
  47.6 7.6 %copy-start.1 = (f32[8,512,128]{2,1,0:T(8,128)}, f32[8,512,128]{2,1,0:T(8,128)S(1)}, u32[]{:S(2)}) copy-start(f32[8,512,128]{2,1,0:T(8,128)S(1)} %get-tuple-element.107.refs_1_.refs_4_) | copy-start | bytes 6291460
  47.6 6.4 %collective-permute-start.4 = (f32[2,512]{1,0:T(2,128)S(1)}, f32[2,512]{1,0:T(2,128)S(1)}, u32[]{:S(2)}, u32[]{:S(2)}) collective-permute-start(f32[2,512]{1,0:T(2,128)S(1)} %get-tuple-element.109.refs_2_.refs_5_), channel_id=1, source_target_pairs={{0,96},{32,0},{64,32},{96,64},{1,97},{33,1},{65,33},{97,65},{2,98}... | collective-permute-start | bytes 12296 | tf_op jit(solution)/shard_map/ppermute | solution.py:442
  50.1 4.0 %collective-permute-start.3 = (f32[2,512]{1,0:T(2,128)S(1)}, f32[2,512]{1,0:T(2,128)S(1)}, u32[]{:S(2)}, u32[]{:S(2)}) collective-permute-start(f32[2,512]{1,0:T(2,128)S(1)} %get-tuple-element.109.refs_2_.refs_5_), channel_id=1, source_target_pairs={{0,64},{32,96},{64,0},{96,32},{1,65},{33,97},{65,1},{97,33},{2,66}... | collective-permute-start | bytes 12296 | tf_op jit(solution)/shard_map/ppermute | solution.py:442
  50.7 3.7 %collective-permute-start.2 = (f32[2,512]{1,0:T(2,128)S(1)}, f32[2,512]{1,0:T(2,128)S(1)}, u32[]{:S(2)}, u32[]{:S(2)}) collective-permute-start(f32[2,512]{1,0:T(2,128)S(1)} %get-tuple-element.109.refs_2_.refs_5_), channel_id=1, source_target_pairs={{0,32},{32,64},{64,96},{96,0},{1,33},{33,65},{65,97},{97,1},{2,34}... | collective-permute-start | bytes 12296 | tf_op jit(solution)/shard_map/ppermute | solution.py:442
  55.2 3.3 %copy-start.2 = (f32[512,128]{1,0:T(8,128)}, f32[512,128]{1,0:T(8,128)S(1)}, u32[]{:S(2)}) copy-start(f32[512,128]{1,0:T(8,128)S(1)} %get-tuple-element.113.refs_4_.refs_7_.refs_9_) | copy-start | bytes 786436
  55.2 3.3 %copy-start.3 = (f32[512,128]{1,0:T(8,128)}, f32[512,128]{1,0:T(8,128)S(1)}, u32[]{:S(2)}) copy-start(f32[512,128]{1,0:T(8,128)S(1)} %get-tuple-element.114.refs_5_.refs_8_.refs_10_) | copy-start | bytes 786436
  55.2 3.3 %collective-permute-start.5 = (f32[8,128,128]{2,1,0:T(8,128)S(1)}, f32[8,128,128]{2,1,0:T(8,128)S(1)}, u32[]{:S(2)}, u32[]{:S(2)}) collective-permute-start(f32[8,128,128]{2,1,0:T(8,128)S(1)} %get-tuple-element.117), channel_id=1, source_target_pairs={{0,1},{1,0},{2,3},{3,2},{4,5},{5,4},{6,7},{7,6},{8,9},{9,8},{10,11... | collective-permute-start | bytes 1572872 | tf_op jit(solution)/shard_map/ppermute | solution.py:388
  59.4 13.8 %all-to-all-start.2 = ((f32[16,64,128]{2,1,0:T(8,128)}), f32[16,64,128]{2,1,0:T(8,128)S(1)}, u32[]{:S(2)}, u32[]{:S(2)}) async-start(f32[16,64,128]{2,1,0:T(8,128)} %bitcast.3), calls=%async_computation.2 | async-start | bytes 1048576 | tf_op jit(solution)/shard_map/all_to_all | solution.py:376
  74.1 13.0 %all-to-all-start.3 = ((f32[16,64,128]{2,1,0:T(8,128)}), f32[16,64,128]{2,1,0:T(8,128)S(1)}, u32[]{:S(2)}, u32[]{:S(2)}) async-start(f32[16,64,128]{2,1,0:T(8,128)} %shard_map.138), calls=%async_computation.3 | async-start | bytes 1048576 | tf_op jit(solution)/shard_map/all_to_all | solution.py:376
  87.1 6.0 %collective-permute-start.6 = (f32[8,128,128]{2,1,0:T(8,128)S(1)}, f32[8,128,128]{2,1,0:T(8,128)S(1)}, u32[]{:S(2)}, u32[]{:S(2)}) collective-permute-start(f32[8,128,128]{2,1,0:T(8,128)S(1)} %bitcast.7), channel_id=1, source_target_pairs={{0,1},{1,0},{2,3},{3,2},{4,5},{5,4},{6,7},{7,6},{8,9},{9,8},{10,11... | collective-permute-start | bytes 1572872 | tf_op jit(solution)/shard_map/ppermute | solution.py:393

commit v6 on v5

--- a/solution.py
+++ b/solution.py
@@ -185,8 +185,7 @@
                 square = jnp.broadcast_to(value[:, lanes(n)], (HEAD_DIM, HEAD_DIM))
                 ref[n * HEAD_DIM : (n + 1) * HEAD_DIM] = square.T
     else:
-        (g_all,) = outs
-        inv_ref, coef_ref, ds_ref = rest
+        inv_ref, coef_ref, ds_ref, g_all = rest
     heads = o_ref.shape[0]
 
     def step(g):
@@ -202,9 +201,9 @@
 
 
 def backward_kernel(half, group, ins, outs, rest):
-    q_all, k_all, v_all, dy, o_all, m_all, g_all = ins
+    q_all, k_all, v_all, dy, o_all, m_all, *g_all = ins
     normed, dq_all, dk_all, dv_all = outs
-    gain_ref, inv_ref, coef_ref = rest
+    gain_ref, *held_g, inv_ref, coef_ref = rest
     heads = gain_ref.shape[0] // 2
     lower, upper = block_mask(False), block_mask(True)
 
@@ -215,7 +214,11 @@
             normed[g, :, lanes(h)] = (gain * o * inv_ref[...]).astype(BF16)
             scaled = gain * dy[g, :, lanes(h)].astype(F32)
             do_all = (scaled * inv_ref[...] - o * coef_ref[...]).astype(BF16)
-            later = g_all[g, h]
+            if held_g:
+                many = held_g[0].shape[1]
+                later = held_g[0][(g * group + h) // many, (g * group + h) % many]
+            else:
+                later = g_all[0][g, h]
             for b in range(2):
                 q, k, v = (slab[g, rows(b), lanes(h)] for slab in (q_all, k_all, v_all))
                 do = do_all[rows(b)]
@@ -457,42 +460,44 @@
 
     def state_grad(other, dy, o, qt, scalars, **options):
         first = len(scalars) > 2
-        outs, out_streams = [(states, F32)], [(states, BF16)]
-        if first:
-            outs += [(buffer_shape(states, LARGE), BF16), (scalar, F32), (scalar, F32)]
-            out_streams = []
+        outs = [(states, F32), (buffer_shape(states, LARGE), BF16)]
+        outs += [(scalar, F32), (scalar, F32)] * first
         kernel = functools.partial(state_grad_kernel, first)
         held = [dy, o, gains, qt, *scalars]
-        return call(kernel, other, [], held, outs, out_streams, unit, **options)
+        return call(kernel, other, [], held, outs, [], unit, **options)
 
     theirs, later_other, inv, coef = state_grad(
         OTHER, dy_other, o_other, qt_other, [lengths, *all_stats]
     )
-    mine, later_own, later_other = state_grad(
-        OWN, dy_own, o_own, qt_own, [inv, coef], push=[(later_other, states)]
-    )
-
-    def backward(other, o, m, later, before=(), late=()):
+    mine, later_own = state_grad(OWN, dy_own, o_own, qt_own, [inv, coef])
+
+    def backward(other, o, m, streams, held, before=(), **options):
         return call(
             backward_kernel,
             other,
-            [queries, keys, values, cotangent, o, m, later],
-            [gains],
+            [queries, keys, values, cotangent, o, m, *streams],
+            [gains, *held],
             [],
             [(queries.shape, BF16)] * 4,
             16 * unit,
             whole=[inv, coef],
             group=SMALL,
             aliased=before,
-            late=late,
+            **options,
         )
 
     total_own, total_other, _, (pre_k, pre_v, *grads) = sum_over_seq(
         mine,
         theirs,
-        lambda: backward(OWN, o_own, m_own, later_own),
+        lambda: backward(OWN, o_own, m_own, [], [later_own], push=[(later_other, states)]),
         lambda before: backward(
-            OTHER, o_other, m_other, later_other, before, [(prefix_keys, OWN, LARGE), (prefix_values, OWN, LARGE)]
+            OTHER,
+            o_other,
+            m_other,
+            [before[-1]],
+            [],
+            before[:-1],
+            late=[(prefix_keys, OWN, LARGE), (prefix_values, OWN, LARGE)],
         ),
     )
 

time: 96.1 us -> 96.1 us (level)
  transfers between devices with their start and end apart: 11 -> 11, of which waited for: 6 -> 7; matrix products, arithmetic and copies ran while one was open for 0% -> 0% of each run, Pallas kernels for 40% -> 39%
where the time goes in v6:
time: 96.1 us; the launch traced here: 95.4 us
  Pallas kernels  44.9 us (47%)
  starting transfers between devices  34.3 us (36%)
  waiting for transfers between devices  12.8 us (13%)
  other arithmetic  1.73 us (2%)
  between operations  1.69 us (2%)
    pallas_call x13, Pallas kernels, call(): pl.pallas_call(run, in_specs=[HBM] * len(fetched) + [SMEM if i else VMEM...  43.1 us
    all_to_all x4, starting transfers between devices, exchange(): lax.all_to_all(value, 'seq', 0, 0, axis_index_groups=chip_groups, tiled=T...  20.1 us
    all_to_all x4, waiting for transfers between devices, exchange(): lax.all_to_all(value, 'seq', 0, 0, axis_index_groups=chip_groups, tiled=T...  11.7 us
    ppermute x2, starting transfers between devices, sum_over_seq(): return (gathered, lax.ppermute(gathered, 'seq', swap), first, second)  7.19 us
    ppermute x3, starting transfers between devices, body(): lax.ppermute(stats, 'head', [(i, (i + k) % head_size) for i in range(head...  3.68 us
    ppermute x2, starting transfers between devices, sum_over_seq(): paired = mine + lax.ppermute(theirs, 'seq', swap)  3.3 us
  transfers between devices with their start and end apart: 11, of which 7 were waited for; matrix products, arithmetic and copies ran while one was open for 0% of the time, Pallas kernels for 39%

profile of v6, /device:TPU:1, one launch (start us, length us, event | category | flops | bytes accessed | tf_op | source)
XLA Modules:
  0.0 95.4 jit_solution(1266820256841854732)
XLA Ops:
  0.6 2.0 %shard_map.128 = f32[8,128,128]{2,1,0:T(8,128)S(1)} custom-call(bf16[512,2048]{1,0:T(8,128)(2,1)} %refs_0_.15, bf16[512,2048]{1,0:T(8,128)(2,1)} %refs_1_.15), custom_call_target="tpu_custom_call" | custom-call | flops 134217728 | bytes 4194304 | tf_op jit(solution)/shard_map/pallas_call | solution.py:347
  2.6 1.5 %collective-permute-start = (f32[8,128,128]{2,1,0:T(8,128)S(1)}, f32[8,128,128]{2,1,0:T(8,128)S(1)}, u32[]{:S(2)}, u32[]{:S(2)}) collective-permute-start(f32[8,128,128]{2,1,0:T(8,128)S(1)} %shard_map.128), channel_id=1, source_target_pairs={{0,1},{1,0},{2,3},{3,2},{4,5},{5,4},{6,7},{7,6},{8,9},{9,8},{10,11... | collective-permute-start | bytes 1572872 | tf_op jit(solution)/shard_map/ppermute | solution.py:391
  4.1 2.0 %shard_map.127 = f32[8,128,128]{2,1,0:T(8,128)S(1)} custom-call(bf16[512,2048]{1,0:T(8,128)(2,1)} %refs_0_.15, bf16[512,2048]{1,0:T(8,128)(2,1)} %refs_1_.15), custom_call_target="tpu_custom_call" | custom-call | flops 134217728 | bytes 4194304 | tf_op jit(solution)/shard_map/pallas_call | solution.py:347
  6.1 0.0 collective-permute-done
  6.1 0.9 add.6
  7.0 7.9 %all-to-all-start = ((f32[16,64,128]{2,1,0:T(8,128)}), f32[16,64,128]{2,1,0:T(8,128)S(1)}, u32[]{:S(2)}, u32[]{:S(2)}) async-start(f32[16,64,128]{2,1,0:T(8,128)} %bitcast), calls=%async_computation | async-start | bytes 1048576 | tf_op jit(solution)/shard_map/all_to_all | solution.py:379
  14.8 5.3 %shard_map.129 = (f32[8,512,128]{2,1,0:T(8,128)}, f32[8,128,128]{2,1,0:T(8,128)}, bf16[8,128,512]{2,1,0:T(8,128)(2,1)}) custom-call(bf16[512,2048]{1,0:T(8,128)(2,1)} %refs_0_.14, bf16[512,2048]{1,0:T(8,128)(2,1)} %refs_1_.14, bf16[512,2048]{1,0:T(8,128)(2,1)} %refs_2_.7), custom_call_target="tpu_custom_call" | custom-call | flops 603979776 | bytes 6291456 | tf_op jit(solution)/shard_map/pallas_call | solution.py:347
  20.2 4.8 %all-to-all-done.pieces_ref = f32[16,64,128]{2,1,0:T(8,128)S(1)} async-done(((f32[16,64,128]{2,1,0:T(8,128)}), f32[16,64,128]{2,1,0:T(8,128)S(1)}, u32[]{:S(2)}, u32[]{:S(2)}) %all-to-all-start) | async-done | bytes 524320 | tf_op jit(solution)/shard_map/all_to_all | solution.py:379
  25.0 0.9 shard_map.130
  25.9 4.3 %all-to-all-start.1 = ((f32[16,64,128]{2,1,0:T(8,128)}), f32[16,64,128]{2,1,0:T(8,128)S(1)}, u32[]{:S(2)}, u32[]{:S(2)}) async-start(f32[16,64,128]{2,1,0:T(8,128)} %shard_map.130), calls=%async_computation.1 | async-start | bytes 1048576 | tf_op jit(solution)/shard_map/all_to_all | solution.py:379
  30.2 0.0 copy-start.4
  30.2 5.3 %shard_map.131 = (f32[8,512,128]{2,1,0:T(8,128)}, f32[8,128,128]{2,1,0:T(8,128)}, bf16[8,128,512]{2,1,0:T(8,128)(2,1)}) custom-call(bf16[512,2048]{1,0:T(8,128)(2,1)} %refs_0_.14, bf16[512,2048]{1,0:T(8,128)(2,1)} %refs_1_.14, bf16[512,2048]{1,0:T(8,128)(2,1)} %refs_2_.7), custom_call_target="tpu_custom_call" | custom-call | flops 603979776 | bytes 6291456 | tf_op jit(solution)/shard_map/pallas_call | solution.py:347
  35.6 3.5 %all-to-all-done.1 = f32[16,64,128]{2,1,0:T(8,128)S(1)} async-done(((f32[16,64,128]{2,1,0:T(8,128)}), f32[16,64,128]{2,1,0:T(8,128)S(1)}, u32[]{:S(2)}, u32[]{:S(2)}) %all-to-all-start.1) | async-done | bytes 524320 | tf_op jit(solution)/shard_map/all_to_all | solution.py:379
  39.1 3.6 %collective-permute-start.1 = (f32[8,128,128]{2,1,0:T(8,128)S(1)}, f32[8,128,128]{2,1,0:T(8,128)S(1)}, u32[]{:S(2)}, u32[]{:S(2)}) collective-permute-start(f32[8,128,128]{2,1,0:T(8,128)S(1)} %bitcast.5), channel_id=1, source_target_pairs={{0,1},{1,0},{2,3},{3,2},{4,5},{5,4},{6,7},{7,6},{8,9},{9,8},{10,11... | collective-permute-start | bytes 1572872 | tf_op jit(solution)/shard_map/ppermute | solution.py:396
  42.7 0.0 copy-done.4
  42.7 4.0 %shard_map.132 = (f32[8,512,128]{2,1,0:T(8,128)S(1)}, bf16[2,4,2,128,128]{4,3,2,1,0:T(8,128)(2,1)S(1)}, f32[2,512]{1,0:T(2,128)S(1)}, bf16[2,512,512]{2,1,0:T(8,...) custom-call(bf16[512,2048]{1,0:T(8,128)(2,1)} %refs_0_.14, ...), custom_call_target="tpu_custom_call" | custom-call | flops 134217728 | bytes 14163968 | tf_op jit(solution)/shard_map/pallas_call | solution.py:347
  46.7 0.0 copy-start
  46.7 0.0 collective-permute-done.1.refs_4_
  46.7 0.9 shard_map.133
  47.6 0.0 copy-start.1
  47.6 2.5 %collective-permute-start.4 = (f32[2,512]{1,0:T(2,128)S(1)}, f32[2,512]{1,0:T(2,128)S(1)}, u32[]{:S(2)}, u32[]{:S(2)}) collective-permute-start(f32[2,512]{1,0:T(2,128)S(1)} %get-tuple-element.110.refs_2_.refs_5_), channel_id=1, source_target_pairs={{0,96},{32,0},{64,32},{96,64},{1,97},{33,1},{65,33},{97,65},{2,98}... | collective-permute-start | bytes 12296 | tf_op jit(solution)/shard_map/ppermute | solution.py:445
  50.1 0.5 collective-permute-start.3
  50.7 0.6 collective-permute-start.2
  51.9 2.0 %shard_map.134 = (bf16[2,4,128,512]{3,2,1,0:T(8,128)(2,1)S(1)}, bf16[2,4,128,512]{3,2,1,0:T(8,128)(2,1)S(1)}, bf16[8,2,128,128]{3,2,1,0:T(8,128)(2,1)}, bf16[8,2,128,128]{3,2,1,0:T(8,128)(2,1)}) custom-call(bf16[8,128,512]{2,1,0:T(8,128)(2,1)} %get-tuple-element.99.refs_0_, bf16[8,128,512]{2,1,0:T(8,128)(2,1)} %get-tuple-element.100.refs_1_, ...), custom_call_target="tpu_custom_call" | custom-call | bytes 2101248 | tf_op jit(solution)/shard_map/pallas_call | solution.py:347
  54.0 0.0 collective-permute-done.4.refs_8_
  54.0 0.1 collective-permute-done.3.refs_7_
  54.1 0.2 collective-permute-done.2.refs_6_
  54.3 0.8 shard_map.135
  55.2 0.0 copy-done.1
  55.2 0.0 copy-start.2
  55.2 0.0 copy-start.3
  55.2 1.8 %collective-permute-start.5 = (f32[8,128,128]{2,1,0:T(8,128)S(1)}, f32[8,128,128]{2,1,0:T(8,128)S(1)}, u32[]{:S(2)}, u32[]{:S(2)}) collective-permute-start(f32[8,128,128]{2,1,0:T(8,128)S(1)} %get-tuple-element.117), channel_id=1, source_target_pairs={{0,1},{1,0},{2,3},{3,2},{4,5},{5,4},{6,7},{7,6},{8,9},{9,8},{10,11... | collective-permute-start | bytes 1572872 | tf_op jit(solution)/shard_map/ppermute | solution.py:391
  57.0 0.0 copy-done
  57.0 0.7 shard_map.136
  57.7 0.0 copy-done.2
  57.7 0.8 collective-permute-done.5
  58.5 0.9 add.7
  59.4 3.8 %all-to-all-start.2 = ((f32[16,64,128]{2,1,0:T(8,128)}), f32[16,64,128]{2,1,0:T(8,128)S(1)}, u32[]{:S(2)}, u32[]{:S(2)}) async-start(f32[16,64,128]{2,1,0:T(8,128)} %bitcast.3), calls=%async_computation.2 | async-start | bytes 1048576 | tf_op jit(solution)/shard_map/all_to_all | solution.py:379
  63.2 7.8 %shard_map.137 = (bf16[512,2048]{1,0:T(8,128)(2,1)}, bf16[512,2048]{1,0:T(8,128)(2,1)}, bf16[512,2048]{1,0:T(8,128)(2,1)}, bf16[512,2048]{1,0:T(8,128)(2,1)}, bf16[8,128,128]{2,1,0:T(8,128)(2,1)}) custom-call(bf16[512,2048]{1,0:T(8,128)(2,1)} %refs_0_.14, bf16[512,2048]{1,0:T(8,128)(2,1)} %refs_1_.14, bf16[512,2048]{1,0:T(8,128)(2,1)} %refs_2_.7, ...), custom_call_target="tpu_custom_call" | custom-call | flops 2147483648 | bytes 11804672 | tf_op jit(solution)/shard_map/pallas_call | solution.py:347
  71.0 2.3 %all-to-all-done.2.pieces_ref = f32[16,64,128]{2,1,0:T(8,128)S(1)} async-done(((f32[16,64,128]{2,1,0:T(8,128)}), f32[16,64,128]{2,1,0:T(8,128)S(1)}, u32[]{:S(2)}, u32[]{:S(2)}) %all-to-all-start.2) | async-done | bytes 524320 | tf_op jit(solution)/shard_map/all_to_all | solution.py:379
  73.2 0.9 shard_map.138
  74.1 4.2 %all-to-all-start.3 = ((f32[16,64,128]{2,1,0:T(8,128)}), f32[16,64,128]{2,1,0:T(8,128)S(1)}, u32[]{:S(2)}, u32[]{:S(2)}) async-start(f32[16,64,128]{2,1,0:T(8,128)} %shard_map.138), calls=%async_computation.3 | async-start | bytes 1048576 | tf_op jit(solution)/shard_map/all_to_all | solution.py:379
  78.3 7.7 %shard_map.139 = (bf16[2,512,512]{2,1,0:T(8,128)(2,1)S(1)}, bf16[2,512,512]{2,1,0:T(8,128)(2,1)S(1)}, bf16[512,2048]{1,0:T(8,128)(2,1)}, bf16[512,2048]{1,0:T(8,...) custom-call(bf16[512,2048]{1,0:T(8,128)(2,1)} %refs_0_.14, ...), custom_call_target="tpu_custom_call", output_to_operand_aliasing={{2}: (12, {}), {3}: (13, {}), {4}: (14, {}), {5}: (15, {})} | custom-call | flops 2147483648 | bytes 15998976 | tf_op jit(solution)/shard_map/pallas_call | solution.py:347
  86.0 1.1 %all-to-all-done.3 = f32[16,64,128]{2,1,0:T(8,128)S(1)} async-done(((f32[16,64,128]{2,1,0:T(8,128)}), f32[16,64,128]{2,1,0:T(8,128)S(1)}, u32[]{:S(2)}, u32[]{:S(2)}) %all-to-all-start.3) | async-done | bytes 524320 | tf_op jit(solution)/shard_map/all_to_all | solution.py:379
  87.1 3.6 %collective-permute-start.6 = (f32[8,128,128]{2,1,0:T(8,128)S(1)}, f32[8,128,128]{2,1,0:T(8,128)S(1)}, u32[]{:S(2)}, u32[]{:S(2)}) collective-permute-start(f32[8,128,128]{2,1,0:T(8,128)S(1)} %bitcast.7), channel_id=1, source_target_pairs={{0,1},{1,0},{2,3},{3,2},{4,5},{5,4},{6,7},{7,6},{8,9},{9,8},{10,11... | collective-permute-start | bytes 1572872 | tf_op jit(solution)/shard_map/ppermute | solution.py:396
  90.7 2.4 %shard_map.140 = (bf16[4,512,256]{2,1,0:T(8,128)(2,1)S(1)}, bf16[4,512,256]{2,1,0:T(8,128)(2,1)S(1)}, bf16[512,2048]{1,0:T(8,128)(2,1)}, bf16[512,2048]{1,0:T(8,128)(2,1)}) custom-call(bf16[512,2048]{1,0:T(8,128)(2,1)} %refs_0_.15, bf16[512,2048]{1,0:T(8,128)(2,1)} %refs_1_.15, bf16[2,512,512]{2,1,0:T(8,128)(2,1)S(1)} %get-tuple-element.143.refs_2_, ...), custom_call_target="tpu_custom_call" | custom-call | flops 536870912 | bytes 6815744 | tf_op jit(solution)/shard_map/pallas_call | solution.py:347
  93.1 0.0 collective-permute-done.6.refs_2_
  93.1 2.1 %shard_map.141 = (bf16[512,2048]{1,0:T(8,128)(2,1)}, bf16[512,2048]{1,0:T(8,128)(2,1)}) custom-call(bf16[4,512,256]{2,1,0:T(8,128)(2,1)S(1)} %get-tuple-element.146.refs_0_, bf16[4,512,256]{2,1,0:T(8,128)(2,1)S(1)} %get-tuple-element.147.refs_1_, f32[8,128,128]{2,1,0:T(8,128)S(1)} %collective-permute-done.6.refs_2_, ...), custom_call_target="tpu_custom_call", output_to_operand_aliasing={{0}: (3, {}), {1}: (4, {})} | custom-call | flops 536870912 | bytes 2621440 | tf_op jit(solution)/shard_map/pallas_call | solution.py:347
  (1 shorter events, 0.0 us)
Async XLA Ops:
  2.6 3.5 %collective-permute-start = (f32[8,128,128]{2,1,0:T(8,128)S(1)}, f32[8,128,128]{2,1,0:T(8,128)S(1)}, u32[]{:S(2)}, u32[]{:S(2)}) collective-permute-start(f32[8,128,128]{2,1,0:T(8,128)S(1)} %shard_map.128), channel_id=1, source_target_pairs={{0,1},{1,0},{2,3},{3,2},{4,5},{5,4},{6,7},{7,6},{8,9},{9,8},{10,11... | collective-permute-start | bytes 1572872 | tf_op jit(solution)/shard_map/ppermute | solution.py:391
  7.0 18.0 %all-to-all-start = ((f32[16,64,128]{2,1,0:T(8,128)}), f32[16,64,128]{2,1,0:T(8,128)S(1)}, u32[]{:S(2)}, u32[]{:S(2)}) async-start(f32[16,64,128]{2,1,0:T(8,128)} %bitcast), calls=%async_computation | async-start | bytes 1048576 | tf_op jit(solution)/shard_map/all_to_all | solution.py:379
  25.9 13.2 %all-to-all-start.1 = ((f32[16,64,128]{2,1,0:T(8,128)}), f32[16,64,128]{2,1,0:T(8,128)S(1)}, u32[]{:S(2)}, u32[]{:S(2)}) async-start(f32[16,64,128]{2,1,0:T(8,128)} %shard_map.130), calls=%async_computation.1 | async-start | bytes 1048576 | tf_op jit(solution)/shard_map/all_to_all | solution.py:379
  30.2 12.4 %copy-start.4 = (f32[2048]{0:T(1024)S(1)}, f32[2048]{0:T(1024)}, u32[]{:S(2)}) copy-start(f32[2048]{0:T(1024)} %param.14) | copy-start | bytes 24580
  39.1 7.6 %collective-permute-start.1 = (f32[8,128,128]{2,1,0:T(8,128)S(1)}, f32[8,128,128]{2,1,0:T(8,128)S(1)}, u32[]{:S(2)}, u32[]{:S(2)}) collective-permute-start(f32[8,128,128]{2,1,0:T(8,128)S(1)} %bitcast.5), channel_id=1, source_target_pairs={{0,1},{1,0},{2,3},{3,2},{4,5},{5,4},{6,7},{7,6},{8,9},{9,8},{10,11... | collective-permute-start | bytes 1572872 | tf_op jit(solution)/shard_map/ppermute | solution.py:396
  46.7 10.3 %copy-start = (f32[8,512,128]{2,1,0:T(8,128)}, f32[8,512,128]{2,1,0:T(8,128)S(1)}, u32[]{:S(2)}) copy-start(f32[8,512,128]{2,1,0:T(8,128)S(1)} %get-tuple-element.92.refs_1_.refs_4_) | copy-start | bytes 6291460
  47.6 7.6 %copy-start.1 = (f32[8,512,128]{2,1,0:T(8,128)}, f32[8,512,128]{2,1,0:T(8,128)S(1)}, u32[]{:S(2)}) copy-start(f32[8,512,128]{2,1,0:T(8,128)S(1)} %get-tuple-element.108.refs_1_.refs_4_) | copy-start | bytes 6291460
  47.6 6.4 %collective-permute-start.4 = (f32[2,512]{1,0:T(2,128)S(1)}, f32[2,512]{1,0:T(2,128)S(1)}, u32[]{:S(2)}, u32[]{:S(2)}) collective-permute-start(f32[2,512]{1,0:T(2,128)S(1)} %get-tuple-element.110.refs_2_.refs_5_), channel_id=1, source_target_pairs={{0,96},{32,0},{64,32},{96,64},{1,97},{33,1},{65,33},{97,65},{2,98}... | collective-permute-start | bytes 12296 | tf_op jit(solution)/shard_map/ppermute | solution.py:445
  50.1 4.0 %collective-permute-start.3 = (f32[2,512]{1,0:T(2,128)S(1)}, f32[2,512]{1,0:T(2,128)S(1)}, u32[]{:S(2)}, u32[]{:S(2)}) collective-permute-start(f32[2,512]{1,0:T(2,128)S(1)} %get-tuple-element.110.refs_2_.refs_5_), channel_id=1, source_target_pairs={{0,64},{32,96},{64,0},{96,32},{1,65},{33,97},{65,1},{97,33},{2,66}... | collective-permute-start | bytes 12296 | tf_op jit(solution)/shard_map/ppermute | solution.py:445
  50.7 3.7 %collective-permute-start.2 = (f32[2,512]{1,0:T(2,128)S(1)}, f32[2,512]{1,0:T(2,128)S(1)}, u32[]{:S(2)}, u32[]{:S(2)}) collective-permute-start(f32[2,512]{1,0:T(2,128)S(1)} %get-tuple-element.110.refs_2_.refs_5_), channel_id=1, source_target_pairs={{0,32},{32,64},{64,96},{96,0},{1,33},{33,65},{65,97},{97,1},{2,34}... | collective-permute-start | bytes 12296 | tf_op jit(solution)/shard_map/ppermute | solution.py:445
  55.2 2.5 %copy-start.2 = (f32[512,128]{1,0:T(8,128)}, f32[512,128]{1,0:T(8,128)S(1)}, u32[]{:S(2)}) copy-start(f32[512,128]{1,0:T(8,128)S(1)} %get-tuple-element.114.refs_4_.refs_6_.refs_9_) | copy-start | bytes 786436
  55.2 2.5 %copy-start.3 = (f32[512,128]{1,0:T(8,128)}, f32[512,128]{1,0:T(8,128)S(1)}, u32[]{:S(2)}) copy-start(f32[512,128]{1,0:T(8,128)S(1)} %get-tuple-element.115.refs_5_.refs_7_.refs_10_) | copy-start | bytes 786436
  55.2 3.3 %collective-permute-start.5 = (f32[8,128,128]{2,1,0:T(8,128)S(1)}, f32[8,128,128]{2,1,0:T(8,128)S(1)}, u32[]{:S(2)}, u32[]{:S(2)}) collective-permute-start(f32[8,128,128]{2,1,0:T(8,128)S(1)} %get-tuple-element.117), channel_id=1, source_target_pairs={{0,1},{1,0},{2,3},{3,2},{4,5},{5,4},{6,7},{7,6},{8,9},{9,8},{10,11... | collective-permute-start | bytes 1572872 | tf_op jit(solution)/shard_map/ppermute | solution.py:391
  59.4 13.8 %all-to-all-start.2 = ((f32[16,64,128]{2,1,0:T(8,128)}), f32[16,64,128]{2,1,0:T(8,128)S(1)}, u32[]{:S(2)}, u32[]{:S(2)}) async-start(f32[16,64,128]{2,1,0:T(8,128)} %bitcast.3), calls=%async_computation.2 | async-start | bytes 1048576 | tf_op jit(solution)/shard_map/all_to_all | solution.py:379
  74.1 13.0 %all-to-all-start.3 = ((f32[16,64,128]{2,1,0:T(8,128)}), f32[16,64,128]{2,1,0:T(8,128)S(1)}, u32[]{:S(2)}, u32[]{:S(2)}) async-start(f32[16,64,128]{2,1,0:T(8,128)} %shard_map.138), calls=%async_computation.3 | async-start | bytes 1048576 | tf_op jit(solution)/shard_map/all_to_all | solution.py:379
  87.1 6.0 %collective-permute-start.6 = (f32[8,128,128]{2,1,0:T(8,128)S(1)}, f32[8,128,128]{2,1,0:T(8,128)S(1)}, u32[]{:S(2)}, u32[]{:S(2)}) collective-permute-start(f32[8,128,128]{2,1,0:T(8,128)S(1)} %bitcast.7), channel_id=1, source_target_pairs={{0,1},{1,0},{2,3},{3,2},{4,5},{5,4},{6,7},{7,6},{8,9},{9,8},{10,11... | collective-permute-start | bytes 1572872 | tf_op jit(solution)/shard_map/ppermute | solution.py:396
